TPU v7x, 256 devices: a whole 4x4x8 slice. The times are simulated.
256 devices in a mesh: st: 64 (over y, z, x_lo), head: 4 (over x_hi, core).
Axes of the slice: x: 4 (x_hi: 2, x_lo: 2; x = x_hi * 2 + x_lo), y: 4, z: 8, core: 2. Of those that a mesh axis runs over, the one named last changes fastest.
Arguments:
- video_tokens: bfloat16 [16384, 1536], P('st'), may hold values from -6 to 6
- cotangent: bfloat16 [16384, 1536], P('st'), may hold values from -6 to 6
- audio_frames: bfloat16 [8192, 1536], P('st'), may hold values from -6 to 6
- input_weights: bfloat16 [3, 1536, 1536], P(None, None, 'head'), may hold values from -0.15625 to 0.15625
- audio_weights: bfloat16 [2, 1536, 1536], P(None, None, 'head'), may hold values from -0.15625 to 0.15625
- output_weight: bfloat16 [1536, 1536], P('head'), may hold values from -0.75 to 0.75
- modulation: float32 [4, 3, 1536], replicated, may hold values from -3 to 3
- tile_clip: int32 [64], replicated, may hold values from 0 to 3, never falling along the last dimension, each value on 1 to 32 neighbouring positions
- dropped: int32 [4], replicated, may hold values 0 or 1
- audio_tile: int32 [8192, 1], P('st'), may hold values from 0 to 63; in each aligned block of 128 rows (0 to 127, 128 to 255, ...) at most 4 rows name the same one
Outputs:
- video_out: bfloat16 [16384, 1536], P('st', 'head')
- video_grad: bfloat16 [16384, 1536], P('st', 'head')
- audio_grad: bfloat16 [8192, 1536], P('st', 'head')
Inputs may be any that keep to these rules, and one draw needn't show every extreme that they name: `tile_clip`: clip numbers never fall along the tiles; each clip spans 1 to 32 consecutive tiles, one exactly 32. `audio_tile`: among the 128 rows of one index of st no tile is named more than 4 times, a bound that some block reaches.
All inputs are finite; a program needn't handle non-finite values.
Results may differ from a plain program's by a relative error of at most 0.039.
Values may be sent and summed in bfloat16 or wider, within the bound.
No kernel may reach another device: no remote copies, remote signals or barrier semaphores. Data moves between devices by JAX's collectives and lax.ppermute only.
A program may use at most 64 MiB of HBM per device.

v0:
```python
import jax
import jax.numpy as jnp
from jax import lax
from jax.sharding import PartitionSpec as P

HD = 64


epsilon = 1e-06


def extended(cells, sides, width):
    for axis, dim in sides:
        count = lax.axis_size(axis)
        ends = count - 1
        head = lax.slice_in_dim(cells, 0, width, axis=dim)
        tail = lax.slice_in_dim(cells, cells.shape[dim] - width, cells.shape[dim], axis=dim)
        cells = jnp.concatenate(
            [
                lax.ppermute(tail, axis, [(i, (i + 1) % count) for i in range(ends)]),
                cells,
                lax.ppermute(head, axis, [((i + 1) % count, i) for i in range(ends)]),
            ],
            axis=dim,
        )
    return cells


def row_scale(matrix):
    return lax.rsqrt(jnp.mean(matrix * matrix, axis=-1, keepdims=True) + epsilon)


def raw_scores(queries, key_rows):
    factor = float(HD) ** (-0.5)
    return (
        jnp.einsum("nhe,mhe->hnm", queries, key_rows[:, 0], preferred_element_type=jnp.float32)
        * factor
    )


def score_grads(probabilities, key_rows, output_grad, row_dots):
    weight_grad = jnp.einsum(
        "nhe,mhe->hnm", output_grad, key_rows[:, 1], preferred_element_type=jnp.float32
    )
    return (probabilities * (weight_grad - row_dots[:, :, None])).astype(jnp.bfloat16)


def key_grads(score_grad, rounded, queries, output_grad):
    factor = float(HD) ** (-0.5)
    key_grad = (
        jnp.einsum("hnm,nhe->mhe", score_grad, queries, preferred_element_type=jnp.float32) * factor
    )
    value_grad = jnp.einsum(
        "hnm,nhe->mhe", rounded, output_grad, preferred_element_type=jnp.float32
    )
    return jnp.stack((key_grad, value_grad), axis=1)


def per_device(
    video_tokens,
    cotangent,
    audio_frames,
    input_weights,
    audio_weights,
    output_weight,
    modulation,
    tile_clip,
    dropped,
    audio_tile,
):
    tok_rows, model_width = video_tokens.shape
    group_width = input_weights.shape[2]
    head_count = group_width // HD
    audio_rows = audio_frames.shape[0]
    tile_count = lax.axis_size("st")
    slot_depth = 2 * audio_rows // tile_count
    slot_total = tile_count * slot_depth
    factor = float(HD) ** (-0.5)
    position = lax.axis_index("st")
    head_group = lax.axis_index("head")
    columns = head_group * group_width
    tile_ids = jnp.arange(tile_count, dtype=jnp.int32)
    my_clip = jnp.sum(jnp.where(tile_ids == position, tile_clip, 0))
    same_clip = (tile_clip == my_clip).astype(jnp.float32)
    left_ok = jnp.sum(jnp.where(tile_ids == position - 1, same_clip, 0.0))
    right_ok = jnp.sum(jnp.where(tile_ids == position + 1, same_clip, 0.0))
    clip_ids = jnp.arange(dropped.shape[0], dtype=jnp.int32)
    clip_pick = (clip_ids == my_clip).astype(jnp.float32)
    mod_rows = jnp.sum(clip_pick[:, None, None] * modulation, axis=0)
    shifts, scales, gating = (mod_rows[0], mod_rows[1], mod_rows[2])
    inputs = video_tokens.astype(jnp.float32)
    input_scale = row_scale(inputs)
    normed = inputs * input_scale
    modulated = (normed * (1.0 + scales) + shifts).astype(jnp.bfloat16)
    queries = jnp.dot(modulated, input_weights[0], preferred_element_type=jnp.float32).astype(
        jnp.bfloat16
    )
    own_keys_flat = jnp.dot(modulated, input_weights[1], preferred_element_type=jnp.float32).astype(
        jnp.bfloat16
    )
    own_values_flat = jnp.dot(
        modulated, input_weights[2], preferred_element_type=jnp.float32
    ).astype(jnp.bfloat16)
    own_pairs = jnp.stack((own_keys_flat, own_values_flat), axis=1)
    face_rows = extended(own_pairs, (("st", 0),), tok_rows)
    sounds = audio_frames.astype(jnp.float32)
    sound_scale = row_scale(sounds)
    sound_normed = sounds * sound_scale
    sound_in = sound_normed.astype(jnp.bfloat16)
    sound_keys = jnp.dot(sound_in, audio_weights[0], preferred_element_type=jnp.float32).astype(
        jnp.bfloat16
    )
    sound_values = jnp.dot(sound_in, audio_weights[1], preferred_element_type=jnp.float32).astype(
        jnp.bfloat16
    )
    sound_pairs = jnp.stack((sound_keys, sound_values), axis=1)
    targets = audio_tile[:, 0]
    target_hot = (targets[:, None] == tile_ids[None, :]).astype(jnp.int32)
    target_clip = jnp.sum(target_hot * tile_clip[None, :], axis=1)
    clip_hot = (target_clip[:, None] == clip_ids[None, :]).astype(jnp.int32)
    alive_rows = 1 - jnp.sum(clip_hot * dropped[None, :], axis=1)
    slot_rank = jnp.sum((jnp.cumsum(target_hot, axis=0) - 1) * target_hot, axis=1)
    slot_of = targets * slot_depth + slot_rank
    slot_ids = jnp.arange(slot_total, dtype=jnp.int32)
    dispatch = ((slot_ids[:, None] == slot_of[None, :]) & (alive_rows[None, :] > 0)).astype(
        jnp.bfloat16
    )
    outgoing = jnp.einsum(
        "sa,aec->sec", dispatch, sound_pairs, preferred_element_type=jnp.float32
    ).astype(jnp.bfloat16)
    slot_flags = jnp.sum(dispatch.astype(jnp.float32), axis=1).astype(jnp.bfloat16)
    arrived, arrived_flags = (
        lax.all_to_all(outgoing, "st", split_axis=0, concat_axis=0, tiled=True),
        lax.all_to_all(slot_flags, "st", split_axis=0, concat_axis=0, tiled=True),
    )
    key_rows = jnp.concatenate((face_rows, arrived), axis=0).reshape(-1, 2, head_count, HD)
    edge_ones = jnp.ones((tok_rows,), jnp.float32)
    key_mask = jnp.concatenate(
        (edge_ones * left_ok, edge_ones, edge_ones * right_ok, arrived_flags.astype(jnp.float32))
    )
    query_heads = queries.reshape(tok_rows, head_count, HD)
    weights = jnp.exp(raw_scores(query_heads, key_rows)) * key_mask[None, None, :]
    totals = jnp.sum(weights, axis=-1)
    probabilities = weights / totals[:, :, None]
    rounded = probabilities.astype(jnp.bfloat16)
    attended = (
        jnp.einsum("hnm,mhe->nhe", rounded, key_rows[:, 1], preferred_element_type=jnp.float32)
        .astype(jnp.bfloat16)
        .reshape(tok_rows, group_width)
    )
    out_part = jnp.dot(attended, output_weight, preferred_element_type=jnp.float32)
    out_share = lax.psum_scatter(
        out_part.astype(jnp.bfloat16), "head", scatter_dimension=1, tiled=True
    ).astype(jnp.float32)
    gate_share = lax.dynamic_slice_in_dim(gating, columns, group_width)
    input_share = lax.dynamic_slice_in_dim(inputs, columns, group_width, 1)
    video_out = (input_share + gate_share * out_share).astype(jnp.bfloat16)
    contract = (((1,), (1,)), ((), ()))
    out_grad = (cotangent.astype(jnp.float32) * gating).astype(jnp.bfloat16)
    attended_grad = lax.dot_general(
        out_grad, output_weight, contract, preferred_element_type=jnp.float32
    ).astype(jnp.bfloat16)
    grad_heads = attended_grad.reshape(tok_rows, head_count, HD)
    row_dots = jnp.einsum(
        "nhe,nhe->hn",
        grad_heads,
        attended.reshape(tok_rows, head_count, HD),
        preferred_element_type=jnp.float32,
    )
    score_grad = score_grads(probabilities, key_rows, grad_heads, row_dots)
    query_grad = (
        jnp.einsum("hnm,mhe->nhe", score_grad, key_rows[:, 0], preferred_element_type=jnp.float32)
        * factor
    )
    all_grad = key_grads(score_grad, rounded, query_heads, grad_heads)
    side_grads = jnp.concatenate(
        (all_grad[:tok_rows], all_grad[2 * tok_rows : 3 * tok_rows]), axis=0
    )
    returned = extended(side_grads.astype(jnp.bfloat16), (("st", 0),), tok_rows).astype(
        side_grads.dtype
    )
    pair_grad = all_grad[tok_rows : 2 * tok_rows] + returned[:tok_rows] + returned[3 * tok_rows :]
    slot_grad = all_grad[3 * tok_rows :]
    pair_total = pair_grad.astype(jnp.bfloat16).reshape(tok_rows, 2, group_width)
    query_total = query_grad.astype(jnp.bfloat16).reshape(tok_rows, group_width)
    slot_back = slot_grad.astype(jnp.bfloat16).reshape(slot_total, 2, group_width)
    sound_back = lax.all_to_all(slot_back, "st", split_axis=0, concat_axis=0, tiled=True)
    sound_pair_grad = jnp.einsum(
        "sa,sec->aec", dispatch, sound_back, preferred_element_type=jnp.float32
    ).astype(jnp.bfloat16)
    video_part = lax.dot_general(
        query_total, input_weights[0], contract, preferred_element_type=jnp.float32
    )
    video_part = video_part + lax.dot_general(
        pair_total[:, 0], input_weights[1], contract, preferred_element_type=jnp.float32
    )
    video_part = video_part + lax.dot_general(
        pair_total[:, 1], input_weights[2], contract, preferred_element_type=jnp.float32
    )
    sound_part = lax.dot_general(
        sound_pair_grad[:, 0], audio_weights[0], contract, preferred_element_type=jnp.float32
    )
    sound_part = sound_part + lax.dot_general(
        sound_pair_grad[:, 1], audio_weights[1], contract, preferred_element_type=jnp.float32
    )
    video_sum, sound_sum = (
        lax.psum(video_part.astype(jnp.bfloat16), "head").astype(jnp.float32),
        lax.psum(sound_part.astype(jnp.bfloat16), "head").astype(jnp.float32),
    )
    hat_grad = video_sum * (1.0 + scales)
    video_full = cotangent.astype(jnp.float32) + input_scale * (
        hat_grad - normed * jnp.mean(hat_grad * normed, axis=-1, keepdims=True)
    )
    sound_full = sound_scale * (
        sound_sum - sound_normed * jnp.mean(sound_sum * sound_normed, axis=-1, keepdims=True)
    )
    video_grad = lax.dynamic_slice_in_dim(video_full, columns, group_width, 1).astype(jnp.bfloat16)
    audio_grad = lax.dynamic_slice_in_dim(sound_full, columns, group_width, 1).astype(jnp.bfloat16)
    return (video_out, video_grad, audio_grad)


def solution(mesh):
    return jax.shard_map(
        per_device,
        mesh=mesh,
        in_specs=(
            P("st", None),
            P("st", None),
            P("st", None),
            P(None, None, "head"),
            P(None, None, "head"),
            P("head", None),
            P(),
            P(),
            P(),
            P("st", None),
        ),
        out_specs=(P("st", "head"), P("st", "head"), P("st", "head")),
        check_vma=False,
    )
```

profile of v0, /device:TPU:1, one launch (start us, length us, event | category | flops | bytes accessed | tf_op | source)
XLA Modules:
  0.0 209.2 jit_solution(14099302549811253475)
XLA Ops:
  7.2 1.4 fusion.102
  12.9 2.2 %fusion.42 = bf16[256,1,384]{2,0,1:T(8,128)(2,1)S(1)} fusion(bf16[3,1536,384]{2,1,0:T(8,128)(2,1)} %param.13, f32[1536]{0:T(1024)S(1)} %get-tuple-element.4, f32[1536]{0:T(1024)S(1)} %get-tuple-element.5, f32[256]{0:T(256)S(1)} %add_rsqrt_fusion, bf16[256,1536]{1,0:T(8,128)(2,1)} %param.10), kind=kOutput, calls=%fused_computation.52 | convolution fusion | flops 304054272 | bytes 2176000 | tf_op jit(solution)/shard_map/dot_general | solution.py:101
  15.1 2.0 fusion.45
  17.8 3.9 %collective-permute-start = (bf16[256,2,384]{2,0,1:T(8,128)(2,1)S(1)}, bf16[256,2,384]{2,0,1:T(8,128)(2,1)S(1)}, u32[]{:S(2)}, u32[]{:S(2)}) collective-permute-start(bf16[256,2,384]{2,0,1:T(8,128)(2,1)S(1)} %pad_maximum_fusion.5), channel_id=1, source_target_pairs={{0,4},{4,8},{8,12},{12,16},{16,20},{20,24},{24,28},{28,32},{32,36}... | collective-permute-start | bytes 1179656 | tf_op jit(solution)/shard_map/ppermute | solution.py:20
  24.5 14.8 %all-to-all-start.1 = ((bf16[64,4,1]{1,2,0:T(2,128)(2,1)}), bf16[64,4,1]{1,2,0:T(2,128)(2,1)S(1)}, u32[]{:S(2)}, u32[]{:S(2)}) async-start(bf16[64,4,1]{1,2,0:T(2,128)(2,1)} %all_to_all.16), calls=%async_computation.1 | async-start | bytes 65536 | tf_op jit(solution)/shard_map/all_to_all | solution.py:134
  39.5 1.8 fusion.54
  43.3 5.1 %all-to-all-done.1 = bf16[64,4,1]{1,2,0:T(2,128)(2,1)S(1)} async-done(((bf16[64,4,1]{1,2,0:T(2,128)(2,1)}), bf16[64,4,1]{1,2,0:T(2,128)(2,1)S(1)}, u32[]{:S(2)}, u32[]{:S(2)}) %all-to-all-start.1) | async-done | bytes 544 | tf_op jit(solution)/shard_map/all_to_all | solution.py:134
  49.1 6.4 %all-to-all-start = ((bf16[256,2,384]{2,1,0:T(2,128)(2,1)}), bf16[256,2,384]{2,1,0:T(2,128)(2,1)S(1)}, u32[]{:S(2)}, u32[]{:S(2)}) async-start(bf16[256,2,384]{2,1,0:T(2,128)(2,1)} %copy.36), calls=%async_computation | async-start | bytes 786432 | tf_op jit(solution)/shard_map/all_to_all | solution.py:133
  55.5 2.0 fusion.35
  63.2 4.7 %all-to-all-done = bf16[256,2,384]{2,1,0:T(2,128)(2,1)S(1)} async-done(((bf16[256,2,384]{2,1,0:T(2,128)(2,1)}), bf16[256,2,384]{2,1,0:T(2,128)(2,1)S(1)}, u32[]{:S(2)}, u32[]{:S(2)}) %all-to-all-start) | async-done | bytes 393248 | tf_op jit(solution)/shard_map/all_to_all | solution.py:133
  68.7 1.4 pad_maximum_fusion.1
  70.1 1.6 copy.38
  71.8 2.8 %fusion.1 = (f32[6,256]{1,0:T(8,128)S(1)}, f32[6,256,1024]{2,1,0:T(8,128)S(1)}) fusion(f32[1024]{0:T(1024)S(1)} %pad_maximum_fusion.6, bf16[256,6,64]{0,2,1:T(8,128)(2,1)} %bitcast.125, bf16[1024,2,6,64]{0,3,2,1:T(8,128)(2,1)} %bitcast.120), kind=kOutput, calls=%fused_computation.3 | convolution fusion | flops 206043648 | bytes 7284736 | tf_op jit(solution)/shard_map/nhe,mhe->hnm/dot_general | solution.py:36
  74.6 1.4 fusion.9
  76.1 2.3 %fusion.79 = (f32[6,256]{1,0:T(8,128)S(1)}, bf16[6,64,256]{2,1,0:T(8,128)(2,1)}) fusion(bf16[6,256,64]{1,2,0:T(8,128)(2,1)S(1)} %bitcast.134, f32[6,256]{1,0:T(8,128)S(1)} %get-tuple-element.21, f32[1024]{0:T(1024)S(1)} %pad_maximum_fusion.6, f32[6,256,1024]{2,1,0:T(8,128)S(1)} %get-tuple-element.22, bf16[1024,2,6,64]{0,3,2,1:T(8,128)(2,1)S(1)} %bitcast.121), kind=kOutput, calls=%fused_computation.91 | convolution fusion | flops 208108032 | bytes 7489536 | tf_op jit(solution)/shard_map/hnm,mhe->nhe/dot_general | solution.py:147
  78.4 2.2 %multiply_convert_fusion = bf16[6,256,1024]{2,1,0:T(8,128)(2,1)S(1)} fusion(f32[6,256]{1,0:T(8,128)S(1)} %get-tuple-element.23, bf16[256,6,64]{0,2,1:T(8,128)(2,1)S(1)} %bitcast.135, bf16[1024,2,6,64]{0,3,2,1:T(8,128)(2,1)S(1)} %bitcast.122, f32[6,256]{1,0:T(8,128)S(1)} %get-tuple-element.21, f32[1024]{0:T(1024)S(1)} %pad_maximum_fusion.6, ...), kind=kOutput, calls=%fused_computation | convolution fusion | flops 210763776 | bytes 10440704 | tf_op jit(solution)/shard_map/nhe,mhe->hnm/dot_general | solution.py:42
  81.3 1.8 fusion.38
  84.4 1.9 copy.42
  86.3 7.6 %all-to-all-start.2 = ((bf16[256,2,384]{2,1,0:T(2,128)(2,1)}), bf16[256,2,384]{2,1,0:T(2,128)(2,1)}, u32[]{:S(2)}, u32[]{:S(2)}) async-start(bf16[256,2,384]{2,1,0:T(2,128)(2,1)} %copy.42), calls=%async_computation.2 | async-start | bytes 786432 | tf_op jit(solution)/shard_map/all_to_all | solution.py:187
  94.0 3.6 %collective-permute-start.2 = (bf16[256,2,6,64]{0,3,2,1:T(8,128)(2,1)}, bf16[256,2,6,64]{0,3,2,1:T(8,128)(2,1)}, u32[]{:S(2)}, u32[]{:S(2)}) collective-permute-start(bf16[256,2,6,64]{0,3,2,1:T(8,128)(2,1)} %get-tuple-element.14), channel_id=1, source_target_pairs={{0,4},{4,8},{8,12},{12,16},{16,20},{20,24},{24,28},{28,32},{32,36}... | collective-permute-start | bytes 1179656 | tf_op jit(solution)/shard_map/ppermute | solution.py:20
  98.9 2.4 %convolution_convert_fusion = bf16[256,1536]{1,0:T(8,128)(2,1)} fusion(bf16[256,384]{0,1:T(8,128)(2,1)} %bitcast.131, bf16[384,1536]{1,0:T(8,128)(2,1)S(1)} %copy-done), kind=kOutput, calls=%fused_computation.11 | convolution fusion | flops 302383104 | bytes 2162688 | tf_op jit(solution)/shard_map/dot_general | solution.py:151
  101.3 2.3 %copy.54 = bf16[256,1536]{0,1:T(8,128)(2,1)} copy(bf16[256,1536]{1,0:T(8,128)(2,1)} %convolution_convert_fusion) | data formatting | bytes 1572864
  104.0 2.1 %fusion.12 = f32[256,1536]{1,0:T(8,128)S(1)} fusion(bf16[256,384]{0,1:T(8,128)(2,1)} %bitcast.130, bf16[3,1536,384]{2,1,0:T(8,128)(2,1)} %param.13), kind=kOutput, calls=%fused_computation.28 | convolution fusion | flops 301989888 | bytes 2949120 | tf_op jit(solution)/shard_map/dot_general | solution.py:191
  106.1 9.9 %collective-permute-done.2 = bf16[256,2,6,64]{0,3,2,1:T(8,128)(2,1)} collective-permute-done((bf16[256,2,6,64]{0,3,2,1:T(8,128)(2,1)}, bf16[256,2,6,64]{0,3,2,1:T(8,128)(2,1)}, u32[]{:S(2)}, u32[]{:S(2)}) %collective-permute-start.2) | collective-permute-done | bytes 393248 | tf_op jit(solution)/shard_map/ppermute | solution.py:20
  116.1 3.9 %collective-permute-done.3 = bf16[256,2,6,64]{0,3,2,1:T(8,128)(2,1)} collective-permute-done((bf16[256,2,6,64]{0,3,2,1:T(8,128)(2,1)}, bf16[256,2,6,64]{0,3,2,1:T(8,128)(2,1)}, u32[]{:S(2)}, u32[]{:S(2)}) %collective-permute-start.3) | collective-permute-done | bytes 393248 | tf_op jit(solution)/shard_map/ppermute | solution.py:22
  121.9 1.5 fusion.3
  124.8 1.8 fusion.19
  131.2 13.2 %reduce-scatter.4.cloned.1.call-done = bf16[384,256]{1,0:T(8,128)(2,1)} async-done(((bf16[1536,256]{1,0:T(8,128)(2,1)}), bf16[384,256]{1,0:T(8,128)(2,1)}) %reduce-scatter.4.cloned.1.call-update) | async-done | bytes 196624
  144.4 1.7 copy.55
  146.2 1.8 add_convert_fusion.1
  148.0 50.5 %all-reduce.3.cloned.1.call-done = (bf16[256,1536]{1,0:T(8,128)(2,1)}, bf16[128,1536]{1,0:T(8,128)(2,1)}) async-done(((bf16[256,1536]{1,0:T(8,128)(2,1)}, bf16[128,1536]{1,0:T(8,128)(2,1)}), (bf16[256,1536]{1,0:T(8,128)(2,1)}, bf16[128,1536]{1,0:T(8,128)(2,1)})) %all-reduce.3.cloned.1.call-update) | async-done | bytes 1179664 | tf_op jit(solution)/shard_map/psum | solution.py:207
  198.5 1.5 multiply_reduce_fusion.2
  (117 shorter events, 30.7 us)
Async XLA Ops:
  7.2 50.3 %copy-start = (bf16[384,1536]{1,0:T(8,128)(2,1)S(1)}, bf16[384,1536]{1,0:T(8,128)(2,1)}, u32[]{:S(2)}) copy-start(bf16[384,1536]{1,0:T(8,128)(2,1)} %param.15) | copy-start | bytes 3538948
  12.9 2.2 %copy-start.1 = (bf16[256,1536]{1,0:T(8,128)(2,1)S(1)}, bf16[256,1536]{1,0:T(8,128)(2,1)}, u32[]{:S(2)}) copy-start(bf16[256,1536]{1,0:T(8,128)(2,1)} %param.10) | copy-start | bytes 2359300
  15.1 2.0 copy-start.13
  15.1 8.0 %copy-start.21 = (s32[128,1]{0,1:T(1,128)S(1)}, s32[128,1]{0,1:T(1,128)}, u32[]{:S(2)}) copy-start(s32[128,1]{0,1:T(1,128)} %param.19) | copy-start | bytes 1540
  15.1 8.2 %copy-start.24 = (s32[64]{0:T(128)S(1)}, s32[64]{0:T(128)}, u32[]{:S(2)}) copy-start(s32[64]{0:T(128)} %param.17) | copy-start | bytes 772
  15.1 8.4 %copy-start.30 = (s32[4]{0:T(128)S(1)}, s32[4]{0:T(128)}, u32[]{:S(2)}) copy-start(s32[4]{0:T(128)} %param.18) | copy-start | bytes 52
  15.1 24.2 %copy-start.11 = (bf16[128,1536]{1,0:T(8,128)(2,1)S(1)}, bf16[128,1536]{1,0:T(8,128)(2,1)}, u32[]{:S(2)}) copy-start(bf16[128,1536]{1,0:T(8,128)(2,1)} %param.12) | copy-start | bytes 1179652
  17.8 50.1 %collective-permute-start = (bf16[256,2,384]{2,0,1:T(8,128)(2,1)S(1)}, bf16[256,2,384]{2,0,1:T(8,128)(2,1)S(1)}, u32[]{:S(2)}, u32[]{:S(2)}) collective-permute-start(bf16[256,2,384]{2,0,1:T(8,128)(2,1)S(1)} %pad_maximum_fusion.5), channel_id=1, source_target_pairs={{0,4},{4,8},{8,12},{12,16},{16,20},{20,24},{24,28},{28,32},{32,36}... | collective-permute-start | bytes 1179656 | tf_op jit(solution)/shard_map/ppermute | solution.py:20
  21.8 46.9 %collective-permute-start.1 = (bf16[256,2,384]{2,0,1:T(8,128)(2,1)S(1)}, bf16[256,2,384]{2,0,1:T(8,128)(2,1)}, u32[]{:S(2)}, u32[]{:S(2)}) collective-permute-start(bf16[256,2,384]{2,0,1:T(8,128)(2,1)S(1)} %pad_maximum_fusion.5), channel_id=1, source_target_pairs={{4,0},{8,4},{12,8},{16,12},{20,16},{24,20},{28,24},{32,28},{36,32}... | collective-permute-start | bytes 1179656 | tf_op jit(solution)/shard_map/ppermute | solution.py:22
  23.6 18.2 %copy-start.26 = (pred[128]{0:T(512)(128)(4,1)}, pred[128]{0:T(512)(128)(4,1)S(1)}, u32[]{:S(2)}) copy-start(pred[128]{0:T(512)(128)(4,1)S(1)} %subtract_compare_fusion) | copy-start | bytes 388
  23.6 18.2 %copy-start.28 = (s32[128]{0:T(128)}, s32[128]{0:T(128)S(1)}, u32[]{:S(2)}) copy-start(s32[128]{0:T(128)S(1)} %multiply_add_fusion) | copy-start | bytes 1540
  24.5 23.9 %all-to-all-start.1 = ((bf16[64,4,1]{1,2,0:T(2,128)(2,1)}), bf16[64,4,1]{1,2,0:T(2,128)(2,1)S(1)}, u32[]{:S(2)}, u32[]{:S(2)}) async-start(bf16[64,4,1]{1,2,0:T(2,128)(2,1)} %all_to_all.16), calls=%async_computation.1 | async-start | bytes 65536 | tf_op jit(solution)/shard_map/all_to_all | solution.py:134
  39.3 2.0 copy-start.6
  39.5 2.3 %copy-start.22 = (f32[128]{0:T(128)}, f32[128]{0:T(128)S(1)}, u32[]{:S(2)}) copy-start(f32[128]{0:T(128)S(1)} %add_rsqrt_fusion.1) | copy-start | bytes 1540
  49.1 18.8 %all-to-all-start = ((bf16[256,2,384]{2,1,0:T(2,128)(2,1)}), bf16[256,2,384]{2,1,0:T(2,128)(2,1)S(1)}, u32[]{:S(2)}, u32[]{:S(2)}) async-start(bf16[256,2,384]{2,1,0:T(2,128)(2,1)} %copy.36), calls=%async_computation | async-start | bytes 786432 | tf_op jit(solution)/shard_map/all_to_all | solution.py:133
  55.4 2.0 copy-start.15
  55.5 2.0 copy-start.20
  57.5 2.3 %copy-start.25 = (s32[64]{0:T(128)S(1)}, s32[64]{0:T(128)}, u32[]{:S(2)}) copy-start(s32[64]{0:T(128)} %param.17) | copy-start | bytes 772
  71.8 2.8 %copy-start.18 = (bf16[256,384]{0,1:T(8,128)(2,1)S(1)}, bf16[256,384]{0,1:T(8,128)(2,1)}, u32[]{:S(2)}) copy-start(bf16[256,384]{0,1:T(8,128)(2,1)} %copy.41) | copy-start | bytes 589828
  76.0 7.0 %copy-start.2 = (f32[1024,1,6,64]{0,3,2,1:T(8,128)}, f32[1024,1,6,64]{0,3,2,1:T(8,128)S(1)}, u32[]{:S(2)}) copy-start(f32[1024,1,6,64]{0,3,2,1:T(8,128)S(1)} %fusion.9) | copy-start | bytes 4718596
  78.4 2.2 %copy-start.8 = (bf16[256,384]{0,1:T(8,128)(2,1)S(1)}, bf16[256,384]{0,1:T(8,128)(2,1)}, u32[]{:S(2)}) copy-start(bf16[256,384]{0,1:T(8,128)(2,1)} %copy.39) | copy-start | bytes 589828
  86.3 37.1 %all-to-all-start.2 = ((bf16[256,2,384]{2,1,0:T(2,128)(2,1)}), bf16[256,2,384]{2,1,0:T(2,128)(2,1)}, u32[]{:S(2)}, u32[]{:S(2)}) async-start(bf16[256,2,384]{2,1,0:T(2,128)(2,1)} %copy.42), calls=%async_computation.2 | async-start | bytes 786432 | tf_op jit(solution)/shard_map/all_to_all | solution.py:187
  94.0 50.5 %reduce-scatter.4.cloned.1.call-start = ((), (), s32[]{:S(2)}) async-start(), calls=%async_computation.4 | async-start | bytes 983040
  94.0 22.0 %collective-permute-start.2 = (bf16[256,2,6,64]{0,3,2,1:T(8,128)(2,1)}, bf16[256,2,6,64]{0,3,2,1:T(8,128)(2,1)}, u32[]{:S(2)}, u32[]{:S(2)}) collective-permute-start(bf16[256,2,6,64]{0,3,2,1:T(8,128)(2,1)} %get-tuple-element.14), channel_id=1, source_target_pairs={{0,4},{4,8},{8,12},{12,16},{16,20},{20,24},{24,28},{28,32},{32,36}... | collective-permute-start | bytes 1179656 | tf_op jit(solution)/shard_map/ppermute | solution.py:20
  97.6 22.3 %collective-permute-start.3 = (bf16[256,2,6,64]{0,3,2,1:T(8,128)(2,1)}, bf16[256,2,6,64]{0,3,2,1:T(8,128)(2,1)}, u32[]{:S(2)}, u32[]{:S(2)}) collective-permute-start(bf16[256,2,6,64]{0,3,2,1:T(8,128)(2,1)} %get-tuple-element.13), channel_id=1, source_target_pairs={{4,0},{8,4},{12,8},{16,12},{20,16},{24,20},{28,24},{32,28},{36,32}... | collective-permute-start | bytes 1179656 | tf_op jit(solution)/shard_map/ppermute | solution.py:22
  103.7 94.9 %all-reduce.3.cloned.1.call-start = ((), (), s32[]{:S(2)}) async-start(), calls=%async_computation.5 | async-start | bytes 2359296 | tf_op jit(solution)/shard_map/psum | solution.py:207
  103.9 16.0 %copy-start.3 = (f32[1024,1,6,64]{0,3,2,1:T(8,128)S(1)}, f32[1024,1,6,64]{0,3,2,1:T(8,128)}, u32[]{:S(2)}) copy-start(f32[1024,1,6,64]{0,3,2,1:T(8,128)} %copy-done.2) | copy-start | bytes 4718596
  103.9 16.0 %copy-start.9 = (bf16[256,2,6,64]{0,3,2,1:T(8,128)(2,1)S(1)}, bf16[256,2,6,64]{0,3,2,1:T(8,128)(2,1)}, u32[]{:S(2)}) copy-start(bf16[256,2,6,64]{0,3,2,1:T(8,128)(2,1)} %get-tuple-element.13) | copy-start | bytes 1179652
  104.0 16.0 %copy-start.10 = (bf16[256,2,6,64]{0,3,2,1:T(8,128)(2,1)S(1)}, bf16[256,2,6,64]{0,3,2,1:T(8,128)(2,1)}, u32[]{:S(2)}) copy-start(bf16[256,2,6,64]{0,3,2,1:T(8,128)(2,1)} %get-tuple-element.14) | copy-start | bytes 1179652
  106.1 15.1 %copy-start.5 = (bf16[3,1536,384]{2,1,0:T(8,128)(2,1)S(1)}, bf16[3,1536,384]{2,1,0:T(8,128)(2,1)}, u32[]{:S(2)}) copy-start(bf16[3,1536,384]{2,1,0:T(8,128)(2,1)} %param.13) | copy-start | bytes 10616836
  123.4 3.2 %copy-start.7 = (bf16[2,1536,384]{2,1,0:T(8,128)(2,1)S(1)}, bf16[2,1536,384]{2,1,0:T(8,128)(2,1)}, u32[]{:S(2)}) copy-start(bf16[2,1536,384]{2,1,0:T(8,128)(2,1)} %param.14) | copy-start | bytes 7077892
  198.5 1.6 copy-start.16
  (8 other events, 8.7 us)
Sparse Core Ops, SparseCore 0:
  103.8 40.5 reduce-scatter.3
  147.4 51.0 all-reduce.2
where the time goes:
time: 210 us; the launch traced here: 209 us
  waiting for transfers between devices  87.4 us (42%)
  starting transfers between devices  39.2 us (19%)
  matrix products  31.6 us (15%)
  other arithmetic  19.7 us (9%)
  local copies, waits for them, and re-layouts  16.6 us (8%)
  between operations  14.7 us (7%)
    psum x1, waiting for transfers between devices, per_device(): lax.psum(video_part.astype(jnp.bfloat16), 'head').astype(jnp.float32)  50.5 us
    all_to_all x1, starting transfers between devices, per_device(): lax.all_to_all(slot_flags, 'st', split_axis=0, concat_axis=0, tiled=True)  14.8 us
    unnamed x3, waiting for transfers between devices  13.3 us
    ppermute x2, waiting for transfers between devices, extended(): lax.ppermute(tail, axis, [(i, (i + 1) % count) for i in range(ends)])  9.94 us
    all_to_all x1, starting transfers between devices, per_device(): lax.all_to_all(slot_back, 'st', split_axis=0, concat_axis=0, tiled=True)  7.64 us
    ppermute x2, starting transfers between devices, extended(): lax.ppermute(tail, axis, [(i, (i + 1) % count) for i in range(ends)])  7.56 us
    unnamed x64, local copies, waits for them, and re-layouts  6.37 us
    all_to_all x1, starting transfers between devices, per_device(): lax.all_to_all(outgoing, 'st', split_axis=0, concat_axis=0, tiled=True)  6.37 us
  transfers between devices with their start and end apart: 9, of which 6 were waited for; matrix products, arithmetic and copies ran while one was open for 16% of the time, Pallas kernels for 0%

commit v1 on v0

v1 whole, which is shorter than its diff:
```python
import jax
import jax.numpy as jnp
from jax import lax
from jax.experimental import pallas as pl
from jax.experimental.pallas import tpu as pltpu
from jax.sharding import PartitionSpec as P

HD = 64
EPS = 1e-06
DEAD = -1e30
EMPTY = 32768.0
LOG4 = 1.3862943611198906
F32 = jnp.float32
BF16 = jnp.bfloat16
VMEM_LIMIT = 56 * 1024 * 1024

NN = (((1,), (0,)), ((), ()))
NT = (((1,), (1,)), ((), ()))
TN = (((0,), (0,)), ((), ()))


def mm(a, b, dims=NN):
    return lax.dot_general(a, b, dims, preferred_element_type=F32)


def iota(shape, dim):
    return lax.broadcasted_iota(jnp.int32, shape, dim)


def row_scale(matrix):
    return lax.rsqrt(jnp.mean(matrix * matrix, axis=-1, keepdims=True) + EPS)


def to_row(col):
    n = col.shape[0]
    eye = iota((n, n), 0) == iota((n, n), 1)
    return jnp.sum(jnp.where(eye, col, jnp.zeros_like(col)), axis=0, keepdims=True)


def to_col(row):
    n = row.shape[1]
    eye = iota((n, n), 0) == iota((n, n), 1)
    return jnp.sum(jnp.where(eye, row, jnp.zeros_like(row)), axis=1, keepdims=True)


def fetch(pairs, sems):
    copies = [pltpu.make_async_copy(src, dst, sems.at[i]) for i, (src, dst) in enumerate(pairs)]
    for copy in copies:
        copy.start()
    return copies


def audio_front(audio_ref, target_ref, weights_hbm, out_ref, weights, sems):
    rows = audio_ref.shape[0]
    copies = fetch([(weights_hbm.at[i], weights.at[i]) for i in range(2)], sems)
    sounds = audio_ref[...].astype(F32)
    sound_in = (sounds * row_scale(sounds)).astype(BF16)
    tcol = target_ref[...]
    trow = to_row(tcol)
    earlier = (tcol == trow) & (iota((rows, rows), 0) < iota((rows, rows), 1))
    rank = jnp.sum(earlier.astype(jnp.int32), axis=0, keepdims=True)
    slot = trow * 8 + rank
    slots = out_ref.shape[0]
    place = iota((slots, rows), 0)
    to_key = (place == slot).astype(BF16)
    to_value = (place == slot + 4).astype(BF16)
    dispatch = jnp.concatenate((to_key, to_value), axis=1)
    filled = jnp.sum(dispatch.astype(F32), axis=1, keepdims=True)
    pairs = []
    for i in range(2):
        copies[i].wait()
        pairs.append(mm(sound_in, weights[i]).astype(BF16))
    sent = mm(dispatch, jnp.concatenate(pairs, axis=0))
    shape = sent.shape
    mark = ((iota(shape, 0) & 7) < 4) & (iota(shape, 1) == 0) & (filled < 0.5)
    out_ref[...] = jnp.where(mark, EMPTY, sent).astype(BF16)


def video_front(tokens_ref, mod_ref, clip_ref, weights_hbm, kv_ref, modulated_ref, weights, sems):
    rows = tokens_ref.shape[0]
    copies = fetch([(weights_hbm.at[i + 1], weights.at[i]) for i in range(2)], sems)
    mod = mod_ref[clip_ref[lax.axis_index("st")]]
    inputs = tokens_ref[...].astype(F32)
    modulated = (inputs * row_scale(inputs) * (1.0 + mod[1:2]) + mod[0:1]).astype(BF16)
    modulated_ref[...] = modulated
    for i in range(2):
        copies[i].wait()
        kv_ref[pl.ds(i * rows, rows), :] = mm(modulated, weights[i]).astype(BF16)


def query_front(
    modulated_ref, cotangent_ref, mod_ref, clip_ref, wq_hbm, wo_hbm, q_ref, g_ref, gt_ref, wq, wo, sems
):
    copies = fetch([(wq_hbm.at[0], wq), (wo_hbm, wo)], sems)
    gating = mod_ref[clip_ref[lax.axis_index("st")]][2:3]
    out_grad = (cotangent_ref[...].astype(F32) * gating).astype(BF16)
    copies[0].wait()
    queries = mm(modulated_ref[...], wq[...]).astype(BF16)
    q_ref[...] = (queries.astype(F32) * (float(HD) ** -0.5)).astype(BF16)
    copies[1].wait()
    grads = mm(out_grad, wo[...], NT)
    g_ref[...] = grads.astype(BF16)
    gt_ref[...] = grads.T.astype(BF16)


def attention(
    clip_ref,
    dropped_ref,
    q_ref,
    g_ref,
    gt_ref,
    own_ref,
    left_ref,
    right_ref,
    slots_ref,
    at_ref,
    dq_ref,
    dl_ref,
    do_ref,
    dr_ref,
    ds_ref,
    aud_ref,
    daud_ref,
    bias_ref,
):
    rows, width = q_ref.shape
    slots = slots_ref.shape[0]
    half = slots // 2
    position = lax.axis_index("st")
    count = clip_ref.shape[0]
    clip = clip_ref[position]
    before = clip_ref[jnp.maximum(position - 1, 0)]
    after = clip_ref[jnp.minimum(position + 1, count - 1)]
    left_bias = jnp.where((before == clip) & (position > 0), -LOG4, DEAD)
    right_bias = jnp.where((after == clip) & (position < count - 1), -LOG4, DEAD)
    alive = dropped_ref[clip] == 0
    pick_row = iota((half, slots), 0)
    pick_at = (pick_row >> 2) * 8 + (pick_row & 3)
    arrived = slots_ref[...]
    for i in range(2):
        pick = (iota((half, slots), 1) == pick_at + 4 * i).astype(BF16)
        aud_ref[pl.ds(i * half, half), :] = mm(pick, arrived).astype(BF16)
    head = aud_ref[pl.ds(0, half), pl.ds(0, 128)].astype(F32)
    live = (head[:, 0:1] < EMPTY * 0.5) & alive
    bias_ref[...] = jnp.broadcast_to(jnp.where(live, -LOG4, DEAD), bias_ref.shape)
    lane = iota((rows, 128), 1)

    def pair_step(pair, carried):
        cols = pl.ds(pl.multiple_of(pair * 128, 128), 128)
        q_pair = q_ref[:, cols]
        g_pair = g_ref[:, cols]
        sources = (left_ref, own_ref, right_ref, aud_ref)
        keys = [ref[pl.ds(0, rows), cols] for ref in sources]
        values = [ref[pl.ds(rows, rows), cols] for ref in sources]
        keys_t = [k.T for k in keys]
        values_t = [v.T for v in values]
        d_keys = [jnp.zeros((rows, 128), F32) for _ in sources]
        d_values = [jnp.zeros((rows, 128), F32) for _ in sources]
        for side in range(2):
            mine = (lane // HD) == side
            q = jnp.where(mine, q_pair, jnp.zeros_like(q_pair))
            g = jnp.where(mine, g_pair, jnp.zeros_like(g_pair))
            head_rows = pl.ds(pl.multiple_of(pair * 128 + side * HD, HD), HD)
            biases = (left_bias, -LOG4, right_bias, jnp.concatenate([bias_ref[...]] * 2, axis=1))
            weights = [jnp.exp(mm(k, q, NT) + b) for k, b in zip(keys, biases)]
            totals = sum(jnp.sum(w, axis=0, keepdims=True) for w in weights)
            inverse = 1.0 / totals
            probs = [w * inverse for w in weights]
            rounded = [p.astype(BF16) for p in probs]
            att = sum(mm(v, p) for v, p in zip(values_t, rounded))
            att = att[side * HD : (side + 1) * HD].astype(BF16)
            at_ref[head_rows, :] = att
            dots = jnp.sum(att.astype(F32) * gt_ref[head_rows, :].astype(F32), axis=0, keepdims=True)
            score_grads = [
                (p * (mm(v, g, NT) - dots)).astype(BF16) for p, v in zip(probs, values)
            ]
            dq = sum(mm(k, s) for k, s in zip(keys_t, score_grads))
            dq = dq[side * HD : (side + 1) * HD] * (float(HD) ** -0.5)
            dq_ref[head_rows, :] = dq.astype(BF16)
            for b in range(4):
                d_keys[b] = d_keys[b] + mm(score_grads[b], q)
                d_values[b] = d_values[b] + mm(rounded[b], g)
        for b, ref in enumerate((dl_ref, do_ref, dr_ref, daud_ref)):
            ref[pl.ds(0, rows), cols] = d_keys[b].astype(ref.dtype)
            ref[pl.ds(rows, rows), cols] = d_values[b].astype(ref.dtype)
        return carried

    lax.fori_loop(0, width // 128, pair_step, 0)
    back_row = iota((slots, half), 0)
    back_at = (back_row >> 3) * 4 + (back_row & 3)
    total = jnp.zeros((slots, width), F32)
    for i in range(2):
        inside = (back_row & 4) == 4 * i
        put = ((iota((slots, half), 1) == back_at) & inside).astype(BF16)
        total = total + mm(put, daud_ref[pl.ds(i * half, half), :])
    ds_ref[...] = total.astype(BF16)


def out_project(at_ref, wo_ref, *out_refs):
    rows = at_ref.shape[0]
    attended = at_ref[...].astype(F32).T.astype(BF16)
    me = lax.axis_index("head")
    for k, ref in enumerate(out_refs):
        cols = pl.ds(pl.multiple_of((me ^ k) * rows, 128), rows)
        ref[...] = mm(attended, wo_ref[:, cols]).astype(BF16)


def input_project(
    dq_ref,
    do_ref,
    fl_ref,
    fr_ref,
    back_ref,
    tokens_ref,
    audio_ref,
    target_ref,
    mod_ref,
    clip_ref,
    weights_hbm,
    audio_weights_hbm,
    out0,
    out1,
    out2,
    out3,
    weights,
    audio_weights,
    sems,
):
    rows = tokens_ref.shape[0]
    sound_rows = audio_ref.shape[0]
    width = do_ref.shape[1]
    copies = fetch([(weights_hbm, weights), (audio_weights_hbm, audio_weights)], sems)
    me = lax.axis_index("head")
    mod = mod_ref[clip_ref[lax.axis_index("st")]]
    inputs = tokens_ref[...].astype(F32)
    normed = inputs * row_scale(inputs)
    sounds = audio_ref[...].astype(F32)
    sound_normed = sounds * row_scale(sounds)
    queries = dq_ref[...].astype(F32).T.astype(BF16)
    pair = do_ref[...] + fl_ref[...].astype(F32) + fr_ref[...].astype(F32)
    pair = pair.astype(BF16)
    tcol = target_ref[...]
    trow = to_row(tcol)
    earlier = (tcol == trow) & (iota((sound_rows, sound_rows), 1) < iota((sound_rows, sound_rows), 0))
    slot = tcol * 8 + jnp.sum(earlier.astype(jnp.int32), axis=1, keepdims=True)
    slots = back_ref.shape[0]
    back = back_ref[...]
    sound_grads = []
    for i in range(2):
        pick = (iota((sound_rows, slots), 1) == slot + 4 * i).astype(BF16)
        sound_grads.append(mm(pick, back).astype(BF16))
    for copy in copies:
        copy.wait()
    outs = (out0, out1, out2, out3)
    dots = jnp.zeros((rows, 1), F32)
    sound_dots = jnp.zeros((sound_rows, 1), F32)
    hat = normed * (1.0 + mod[1:2])
    for k in range(4):
        start = pl.multiple_of((me ^ k) * width, 128)
        feats = pl.ds(start, width)
        part = mm(queries, weights[0, feats, :], NT)
        part = part + mm(pair[:rows], weights[1, feats, :], NT)
        part = part + mm(pair[rows:], weights[2, feats, :], NT)
        sound_part = mm(sound_grads[0], audio_weights[0, feats, :], NT)
        sound_part = sound_part + mm(sound_grads[1], audio_weights[1, feats, :], NT)
        outs[k][pl.ds(0, rows), :] = part.astype(BF16)
        outs[k][pl.ds(rows, sound_rows), :] = sound_part.astype(BF16)
    for k in range(4):
        block = slice(k * width, (k + 1) * width)
        chunk = jnp.zeros((rows + sound_rows, width), F32)
        for j in range(4):
            chosen = (me ^ j) == k
            chunk = chunk + jnp.where(chosen, outs[j][pl.ds(0, rows + sound_rows), :].astype(F32), 0.0)
        dots = dots + jnp.sum(chunk[:rows] * hat[:, block], axis=1, keepdims=True)
        sound_dots = sound_dots + jnp.sum(
            chunk[rows:] * sound_normed[:, block], axis=1, keepdims=True
        )
    row = jnp.concatenate((to_row(dots), to_row(sound_dots)), axis=1)
    high = row.astype(BF16).astype(F32)
    low = row - high
    where_row = iota((16, rows + sound_rows), 0)
    extra = jnp.where(where_row == 0, high, jnp.where(where_row == 1, low, 0.0)).astype(BF16)
    for k in range(4):
        outs[k][pl.ds(rows + sound_rows, 16), :] = extra


def finish(
    tokens_ref,
    cotangent_ref,
    audio_ref,
    mod_ref,
    clip_ref,
    o0,
    o1,
    o2,
    o3,
    g0,
    g1,
    g2,
    g3,
    video_out_ref,
    video_grad_ref,
    audio_grad_ref,
):
    rows, width = video_out_ref.shape
    sound_rows = audio_grad_ref.shape[0]
    model = tokens_ref.shape[1]
    me = lax.axis_index("head")
    cols = pl.ds(pl.multiple_of(me * width, 128), width)
    clip = clip_ref[lax.axis_index("st")]
    mod = mod_ref[clip, :, cols]
    inputs = tokens_ref[...].astype(F32)
    scale = row_scale(inputs)
    mine = tokens_ref[:, cols].astype(F32)
    out_sum = sum(ref[...].astype(F32) for ref in (o0, o1, o2, o3))
    video_out_ref[...] = (mine + mod[2:3] * out_sum).astype(BF16)
    parts = (g0, g1, g2, g3)
    total = sum(ref[pl.ds(0, rows + sound_rows), :].astype(F32) for ref in parts)
    extra = sum(ref[pl.ds(rows + sound_rows, 16), :].astype(F32) for ref in parts)
    row = (extra[0:1] + extra[1:2]) * (1.0 / model)
    mean = to_col(row[:, :rows])
    sound_mean = to_col(row[:, rows:])
    hat = total[:rows] * (1.0 + mod[1:2])
    video_grad_ref[...] = (
        cotangent_ref[:, cols].astype(F32) + scale * (hat - mine * scale * mean)
    ).astype(BF16)
    sounds = audio_ref[...].astype(F32)
    sound_scale = row_scale(sounds)
    sound_mine = audio_ref[:, cols].astype(F32) * sound_scale
    audio_grad_ref[...] = (sound_scale * (total[rows:] - sound_mine * sound_mean)).astype(BF16)


VM = pl.BlockSpec(memory_space=pltpu.VMEM)
SM = pl.BlockSpec(memory_space=pltpu.SMEM)
HBM = pl.BlockSpec(memory_space=pl.ANY)


def call(body, ins, outs, flops, name, scratch=()):
    return pl.pallas_call(
        body,
        in_specs=list(ins),
        out_specs=[VM] * len(outs),
        out_shape=[jax.ShapeDtypeStruct(shape, dtype) for shape, dtype in outs],
        scratch_shapes=list(scratch),
        compiler_params=pltpu.CompilerParams(vmem_limit_bytes=VMEM_LIMIT),
        cost_estimate=pl.CostEstimate(flops=flops, bytes_accessed=4 << 20, transcendentals=0),
        name=name,
    )


def per_device(
    video_tokens,
    cotangent,
    audio_frames,
    input_weights,
    audio_weights,
    output_weight,
    modulation,
    tile_clip,
    dropped,
    audio_tile,
):
    rows, model = video_tokens.shape
    width = input_weights.shape[2]
    sound_rows = audio_frames.shape[0]
    count = lax.axis_size("st")
    slots = 8 * count
    dma = pltpu.SemaphoreType.DMA((2,))
    wide = pltpu.VMEM((2, model, width), BF16)
    (sent,) = call(
        audio_front,
        (VM, VM, HBM),
        [((slots, width), BF16)],
        2 * sound_rows * model * 2 * width,
        "audio_front",
        (wide, dma),
    )(audio_frames, audio_tile, audio_weights)
    arrived = lax.all_to_all(sent, "st", split_axis=0, concat_axis=0, tiled=True)
    kv, modulated = call(
        video_front,
        (VM, VM, SM, HBM),
        [((2 * rows, width), BF16), ((rows, model), BF16)],
        2 * rows * model * 2 * width,
        "video_front",
        (wide, dma),
    )(video_tokens, modulation, tile_clip, input_weights)
    up = [(i, i + 1) for i in range(count - 1)]
    down = [(i + 1, i) for i in range(count - 1)]
    from_left = lax.ppermute(kv, "st", up)
    from_right = lax.ppermute(kv, "st", down)
    queries, grads, grads_t = call(
        query_front,
        (VM, VM, VM, SM, HBM, HBM),
        [((rows, width), BF16), ((rows, width), BF16), ((width, rows), BF16)],
        2 * rows * model * 2 * width,
        "query_front",
        (pltpu.VMEM((model, width), BF16), pltpu.VMEM((width, model), BF16), dma),
    )(modulated, cotangent, modulation, tile_clip, input_weights, output_weight)
    half = slots // 2
    attended_t, dq_t, d_left, d_own, d_right, d_slots = call(
        attention,
        (SM, SM) + (VM,) * 7,
        [
            ((width, rows), BF16),
            ((width, rows), BF16),
            ((2 * rows, width), BF16),
            ((2 * rows, width), F32),
            ((2 * rows, width), BF16),
            ((slots, width), BF16),
        ],
        2 * 6 * rows * (3 * rows + half) * width,
        "attention",
        (
            pltpu.VMEM((slots, width), BF16),
            pltpu.VMEM((slots, width), BF16),
            pltpu.VMEM((half, 128), F32),
        ),
    )(tile_clip, dropped, queries, grads, grads_t, kv, from_left, from_right, arrived)
    back = lax.all_to_all(d_slots, "st", split_axis=0, concat_axis=0, tiled=True)
    grad_from_right = lax.ppermute(d_left, "st", down)
    grad_from_left = lax.ppermute(d_right, "st", up)
    out_parts = call(
        out_project,
        (VM, VM),
        [((rows, width), BF16)] * 4,
        2 * rows * width * model,
        "out_project",
    )(attended_t, output_weight)
    groups = lax.axis_size("head")
    swaps = [[(i, i ^ k) for i in range(groups)] for k in range(groups)]
    outs = [out_parts[0]] + [lax.ppermute(out_parts[k], "head", swaps[k]) for k in (1, 2, 3)]
    parts = call(
        input_project,
        (VM,) * 9 + (SM, HBM, HBM),
        [((rows + sound_rows + 16, width), BF16)] * 4,
        2 * (3 * rows + 2 * sound_rows) * width * model,
        "input_project",
        (pltpu.VMEM((3, model, width), BF16), wide, dma),
    )(
        dq_t,
        d_own,
        grad_from_left,
        grad_from_right,
        back,
        video_tokens,
        audio_frames,
        audio_tile,
        modulation,
        tile_clip,
        input_weights,
        audio_weights,
    )
    sums = [parts[0]] + [lax.ppermute(parts[k], "head", swaps[k]) for k in (1, 2, 3)]
    return tuple(
        call(
            finish,
            (VM,) * 4 + (SM,) + (VM,) * 8,
            [((rows, width), BF16), ((rows, width), BF16), ((sound_rows, width), BF16)],
            4 * rows * model,
            "finish",
        )(video_tokens, cotangent, audio_frames, modulation, tile_clip, *outs, *sums)
    )


def solution(mesh):
    return jax.shard_map(
        per_device,
        mesh=mesh,
        in_specs=(
            P("st", None),
            P("st", None),
            P("st", None),
            P(None, None, "head"),
            P(None, None, "head"),
            P("head", None),
            P(),
            P(),
            P(),
            P("st", None),
        ),
        out_specs=(P("st", "head"), P("st", "head"), P("st", "head")),
        check_vma=False,
    )
```

time: 210 us -> 137 us (0.65)
  waiting for transfers between devices: 87.4 us -> 48.7 us
  Pallas kernels: 0 us -> 38.2 us
  matrix products: 31.6 us -> 0 us
  other arithmetic: 19.7 us -> 0 us
  between operations: 14.7 us -> 0.81 us
  local copies, waits for them, and re-layouts: 16.6 us -> 5.03 us
  starting transfers between devices: 39.2 us -> 43.4 us
    psum x1 -> x0, waiting for transfers between devices: 50.5 us -> none  [per_device(): lax.psum(video_part.astype(jnp.bfloat16), 'head').astype(jnp.float32)]
    pallas_call x0 -> x7, Pallas kernels: none -> 38.2 us  [the longest x1 10.4 us: per_device(): call(attention, (SM, SM) + (VM,) * 7, [((width, rows), BF16), ((width, ro...]
    ppermute x4 -> x10, waiting for transfers between devices: 13.8 us -> 48.7 us  [the longest x3 19.1 us: per_device(): lax.ppermute(out_parts[k], 'head', swaps[k])]
    dot_general x20 -> x0, matrix products: 31.6 us -> none  [the longest x1 2.82 us: raw_scores(): jnp.einsum('nhe,mhe->hnm', queries, key_rows[:, 0], preferred_element_typ...]
    unnamed x3 -> x0, waiting for transfers between devices: 13.3 us -> none
    all_to_all x3 -> x2, waiting for transfers between devices: 9.79 us -> 0.01 us  [the longest x1 0.01 us: per_device(): lax.all_to_all(sent, 'st', split_axis=0, concat_axis=0, tiled=True)]
    convert_element_type x10 -> x0, other arithmetic: 8.98 us -> none  [the longest x1 1.83 us: per_device(): video_out = (input_share + gate_share * out_share).astype(jnp.bfloat16)]
    ppermute x4 -> x10, starting transfers between devices: 10.1 us -> 18.8 us  [the longest x3 4.69 us: per_device(): lax.ppermute(out_parts[k], 'head', swaps[k])]
  transfers between devices with their start and end apart: 9 -> 12, of which waited for: 6 -> 5; matrix products, arithmetic and copies ran while one was open for 16% -> 0% of each run, Pallas kernels for 0% -> 15%
where the time goes in v1:
time: 137 us; the launch traced here: 136 us
  waiting for transfers between devices  48.7 us (36%)
  starting transfers between devices  43.4 us (32%)
  Pallas kernels  38.2 us (28%)
  local copies, waits for them, and re-layouts  5.03 us (4%)
    ppermute x3, waiting for transfers between devices, per_device(): lax.ppermute(out_parts[k], 'head', swaps[k])  19.1 us
    ppermute x1, waiting for transfers between devices, per_device(): grad_from_left = lax.ppermute(d_right, 'st', up)  14.4 us
    all_to_all x1, starting transfers between devices, per_device(): lax.all_to_all(sent, 'st', split_axis=0, concat_axis=0, tiled=True)  13.6 us
    ppermute x1, waiting for transfers between devices, per_device(): from_right = lax.ppermute(kv, 'st', down)  12.1 us
    all_to_all x1, starting transfers between devices, per_device(): lax.all_to_all(d_slots, 'st', split_axis=0, concat_axis=0, tiled=True)  11.1 us
    pallas_call x1, Pallas kernels, per_device(): call(attention, (SM, SM) + (VM,) * 7, [((width, rows), BF16), ((width, ro...  10.4 us
    pallas_call x1, Pallas kernels, per_device(): call(input_project, (VM,) * 9 + (SM, HBM, HBM), [((rows + sound_rows + 16...  8.64 us
    unnamed x32, local copies, waits for them, and re-layouts  5.03 us
  transfers between devices with their start and end apart: 12, of which 5 were waited for; matrix products, arithmetic and copies ran while one was open for 0% of the time, Pallas kernels for 15%

profile of v1, /device:TPU:1, one launch (start us, length us, event | category | flops | bytes accessed | tf_op | source)
XLA Modules:
  0.0 136.2 jit_solution(18065386829228706181)
XLA Ops:
  0.6 1.4 %copy.15.target_ref = s32[128,1]{1,0:T(8,128)} copy(s32[128,1]{0,1:T(1,128)} %param.19) | data formatting | bytes 1024 | tf_op args[9]
  2.1 4.0 %audio_front.1 = bf16[512,384]{1,0:T(8,128)(2,1)} custom-call(bf16[128,1536]{1,0:T(8,128)(2,1)} %audio_ref.5, s32[128,1]{1,0:T(8,128)} %copy.15.target_ref, bf16[2,1536,384]{2,1,0:T(8,128)(2,1)} %audio_weights_hbm.1), custom_call_target="tpu_custom_call" | custom-call | flops 301989888 | bytes 4194304 | tf_op jit(solution)/shard_map/audio_front/pallas_call | solution.py:370
  6.1 13.6 %all-to-all-start = ((bf16[64,8,384]{2,1,0:T(8,128)(2,1)}), bf16[64,8,384]{2,1,0:T(8,128)(2,1)S(1)}, u32[]{:S(2)}, u32[]{:S(2)}) async-start(bf16[64,8,384]{2,1,0:T(8,128)(2,1)} %bitcast.5), calls=%async_computation | async-start | bytes 786432 | tf_op jit(solution)/shard_map/all_to_all | solution.py:378
  19.7 0.7 copy.18.mod_ref
  20.4 4.3 %video_front.1 = (bf16[512,384]{1,0:T(8,128)(2,1)}, bf16[256,1536]{1,0:T(8,128)(2,1)}) custom-call(bf16[256,1536]{1,0:T(8,128)(2,1)} %tokens_ref.5, f32[4,3,1536]{2,1,0:T(4,128)} %copy.18.mod_ref, s32[64]{0:T(128)} %clip_ref.9, bf16[3,1536,384]{2,1,0:T(8,128)(2,1)} %weights_hbm.5), custom_call_target="tpu_custom_call" | custom-call | flops 603979776 | bytes 4194304 | tf_op jit(solution)/shard_map/video_front/pallas_call | solution.py:379
  24.8 1.3 collective-permute-start.1
  26.1 4.0 %collective-permute-start = (bf16[512,384]{1,0:T(8,128)(2,1)}, bf16[512,384]{1,0:T(8,128)(2,1)S(1)}, u32[]{:S(2)}, u32[]{:S(2)}) collective-permute-start(bf16[512,384]{1,0:T(8,128)(2,1)} %get-tuple-element.26.own_ref), channel_id=1, source_target_pairs={{0,4},{4,8},{8,12},{12,16},{16,20},{20,24},{24,28},{28,32},{32,36}... | collective-permute-start | bytes 1179656 | tf_op jit(solution)/shard_map/ppermute | solution.py:389
  30.1 4.6 %query_front.1 = (bf16[256,384]{1,0:T(8,128)(2,1)}, bf16[256,384]{1,0:T(8,128)(2,1)}, bf16[384,256]{1,0:T(8,128)(2,1)}) custom-call(bf16[256,1536]{1,0:T(8,128)(2,1)} %get-tuple-element.22.modulated_ref, bf16[256,1536]{1,0:T(8,128)(2,1)} %cotangent_ref.3, f32[4,3,1536]{2,1,0:T(4,128)} %copy.18.mod_ref, s32[64]{0:T(128)} %clip_ref.9, ...), custom_call_target="tpu_custom_call" | custom-call | flops 603979776 | bytes 4194304 | tf_op jit(solution)/shard_map/query_front/pallas_call | solution.py:391
  34.7 12.1 %collective-permute-done.1.right_ref = bf16[512,384]{1,0:T(8,128)(2,1)S(1)} collective-permute-done((bf16[512,384]{1,0:T(8,128)(2,1)}, bf16[512,384]{1,0:T(8,128)(2,1)S(1)}, u32[]{:S(2)}, u32[]{:S(2)}) %collective-permute-start.1) | collective-permute-done | bytes 393248 | tf_op jit(solution)/shard_map/ppermute | solution.py:390
  46.8 0.7 copy-done.11
  47.5 0.2 copy-done.12
  47.8 10.4 %attention.1 = (bf16[384,256]{1,0:T(8,128)(2,1)}, bf16[384,256]{1,0:T(8,128)(2,1)}, bf16[512,384]{1,0:T(8,128)(2,1)}, f32[512,384]{1,0:T(8,128)}, bf16[512,384]{1,0:T(8,128)(2,1)}, /*index=5*/bf16[512,384]{1,0:T(8,128)(2,1)}) custom-call(s32[64]{0:T(128)} %clip_ref.9, s32[4]{0:T(128)} %dropped_ref.1, bf16[256,384]{1,0:T(8,128)(2,1)} %get-tuple-element.23.q_ref, ...), custom_call_target="tpu_custom_call" | custom-call | flops 1207959552 | bytes 4194304 | tf_op jit(solution)/shard_map/attention/pallas_call | solution.py:400
  58.1 11.1 %all-to-all-start.1 = ((bf16[64,8,384]{2,1,0:T(8,128)(2,1)}), bf16[64,8,384]{2,1,0:T(8,128)(2,1)S(1)}, u32[]{:S(2)}, u32[]{:S(2)}) async-start(bf16[64,8,384]{2,1,0:T(8,128)(2,1)} %bitcast.7), calls=%async_computation.1 | async-start | bytes 786432 | tf_op jit(solution)/shard_map/all_to_all | solution.py:419
  69.2 2.9 %collective-permute-start.5 = (bf16[512,384]{1,0:T(8,128)(2,1)}, bf16[512,384]{1,0:T(8,128)(2,1)S(1)}, u32[]{:S(2)}, u32[]{:S(2)}) collective-permute-start(bf16[512,384]{1,0:T(8,128)(2,1)} %get-tuple-element.34), channel_id=1, source_target_pairs={{0,4},{4,8},{8,12},{12,16},{16,20},{20,24},{24,28},{28,32},{32,36}... | collective-permute-start | bytes 1179656 | tf_op jit(solution)/shard_map/ppermute | solution.py:421
  72.1 1.3 collective-permute-start.6
  73.4 2.8 %out_project.1 = (bf16[256,384]{1,0:T(8,128)(2,1)}, bf16[256,384]{1,0:T(8,128)(2,1)}, bf16[256,384]{1,0:T(8,128)(2,1)}, bf16[256,384]{1,0:T(8,128)(2,1)}) custom-call(bf16[384,256]{1,0:T(8,128)(2,1)} %get-tuple-element.27.at_ref, bf16[384,1536]{1,0:T(8,128)(2,1)} %wo_ref.1), custom_call_target="tpu_custom_call" | custom-call | flops 301989888 | bytes 4194304 | tf_op jit(solution)/shard_map/out_project/pallas_call | solution.py:422
  76.2 1.3 collective-permute-start.2
  77.5 14.4 %collective-permute-done.5.fl_ref = bf16[512,384]{1,0:T(8,128)(2,1)S(1)} collective-permute-done((bf16[512,384]{1,0:T(8,128)(2,1)}, bf16[512,384]{1,0:T(8,128)(2,1)S(1)}, u32[]{:S(2)}, u32[]{:S(2)}) %collective-permute-start.5) | collective-permute-done | bytes 393248 | tf_op jit(solution)/shard_map/ppermute | solution.py:421
  91.9 3.1 %collective-permute-done.6.fr_ref = bf16[512,384]{1,0:T(8,128)(2,1)S(1)} collective-permute-done((bf16[512,384]{1,0:T(8,128)(2,1)}, bf16[512,384]{1,0:T(8,128)(2,1)S(1)}, u32[]{:S(2)}, u32[]{:S(2)}) %collective-permute-start.6) | collective-permute-done | bytes 393248 | tf_op jit(solution)/shard_map/ppermute | solution.py:420
  95.1 0.7 copy-done.2
  95.8 0.2 copy-done
  96.0 8.6 %input_project.1 = (bf16[400,384]{1,0:T(8,128)(2,1)}, bf16[400,384]{1,0:T(8,128)(2,1)}, bf16[400,384]{1,0:T(8,128)(2,1)}, bf16[400,384]{1,0:T(8,128)(2,1)}) custom-call(bf16[384,256]{1,0:T(8,128)(2,1)} %get-tuple-element.32.dq_ref, f32[512,384]{1,0:T(8,128)} %get-tuple-element.33.do_ref, bf16[512,384]{1,0:T(8,128)(2,1)} %copy-done.1, ...), custom_call_target="tpu_custom_call" | custom-call | flops 1207959552 | bytes 4194304 | tf_op jit(solution)/shard_map/input_project/pallas_call | solution.py:432
  104.7 1.3 collective-permute-start.7
  106.0 2.4 %collective-permute-start.8 = (bf16[400,384]{1,0:T(8,128)(2,1)}, bf16[400,384]{1,0:T(8,128)(2,1)S(1)}, u32[]{:S(2)}, u32[]{:S(2)}) collective-permute-start(bf16[400,384]{1,0:T(8,128)(2,1)} %get-tuple-element.39), channel_id=1, source_target_pairs={{0,2},{1,3},{2,0},{3,1},{4,6},{5,7},{6,4},{7,5},{8,10},{9,11},{10,... | collective-permute-start | bytes 921608 | tf_op jit(solution)/shard_map/ppermute | solution.py:453
  108.4 0.8 collective-permute-start.9
  109.2 2.4 %collective-permute-start.3 = (bf16[256,384]{1,0:T(8,128)(2,1)S(1)}, bf16[256,384]{1,0:T(8,128)(2,1)S(1)}, u32[]{:S(2)}, u32[]{:S(2)}) collective-permute-start(bf16[256,384]{1,0:T(8,128)(2,1)S(1)} %copy-done.14), channel_id=1, source_target_pairs={{0,2},{1,3},{2,0},{3,1},{4,6},{5,7},{6,4},{7,5},{8,10},{9,11},{10,... | collective-permute-start | bytes 589832 | tf_op jit(solution)/shard_map/ppermute | solution.py:431
  111.7 1.0 collective-permute-start.4
  112.6 14.7 %collective-permute-done.3.o2 = bf16[256,384]{1,0:T(8,128)(2,1)S(1)} collective-permute-done((bf16[256,384]{1,0:T(8,128)(2,1)S(1)}, bf16[256,384]{1,0:T(8,128)(2,1)S(1)}, u32[]{:S(2)}, u32[]{:S(2)}) %collective-permute-start.3) | collective-permute-done | bytes 196640 | tf_op jit(solution)/shard_map/ppermute | solution.py:431
  127.3 4.4 %collective-permute-done.4.o3 = bf16[256,384]{1,0:T(8,128)(2,1)S(1)} collective-permute-done((bf16[256,384]{1,0:T(8,128)(2,1)S(1)}, bf16[256,384]{1,0:T(8,128)(2,1)S(1)}, u32[]{:S(2)}, u32[]{:S(2)}) %collective-permute-start.4) | collective-permute-done | bytes 196640 | tf_op jit(solution)/shard_map/ppermute | solution.py:431
  131.8 0.6 copy-done.9
  132.6 0.1 copy-done.6
  132.8 3.5 %finish.1 = (bf16[256,384]{1,0:T(8,128)(2,1)}, bf16[256,384]{1,0:T(8,128)(2,1)}, bf16[128,384]{1,0:T(8,128)(2,1)}) custom-call(bf16[256,1536]{1,0:T(8,128)(2,1)} %tokens_ref.5, bf16[256,1536]{1,0:T(8,128)(2,1)} %cotangent_ref.3, bf16[128,1536]{1,0:T(8,128)(2,1)} %audio_ref.5, f32[4,3,1536]{2,1,0:T(4,128)} %copy.18.mod_ref, s32[64]{0:T(128)} %clip_ref.9, ...), custom_call_target="tpu_custom_call" | custom-call | flops 1572864 | bytes 4194304 | tf_op jit(solution)/shard_map/finish/pallas_call | solution.py:455
  (31 shorter events, 0.4 us)
Async XLA Ops:
  0.6 19.1 %copy-start.10 = (f32[4,3,1536]{2,0,1:T(4,128)S(1)}, f32[4,3,1536]{2,0,1:T(4,128)}, u32[]{:S(2)}) copy-start(f32[4,3,1536]{2,0,1:T(4,128)} %param.16) | copy-start | bytes 221188
  6.1 40.6 %all-to-all-start = ((bf16[64,8,384]{2,1,0:T(8,128)(2,1)}), bf16[64,8,384]{2,1,0:T(8,128)(2,1)S(1)}, u32[]{:S(2)}, u32[]{:S(2)}) async-start(bf16[64,8,384]{2,1,0:T(8,128)(2,1)} %bitcast.5), calls=%async_computation | async-start | bytes 786432 | tf_op jit(solution)/shard_map/all_to_all | solution.py:378
  24.8 22.0 %collective-permute-start.1 = (bf16[512,384]{1,0:T(8,128)(2,1)}, bf16[512,384]{1,0:T(8,128)(2,1)S(1)}, u32[]{:S(2)}, u32[]{:S(2)}) collective-permute-start(bf16[512,384]{1,0:T(8,128)(2,1)} %get-tuple-element.26.own_ref), channel_id=1, source_target_pairs={{4,0},{8,4},{12,8},{16,12},{20,16},{24,20},{28,24},{32,28},{36,32}... | collective-permute-start | bytes 1179656 | tf_op jit(solution)/shard_map/ppermute | solution.py:390
  26.1 20.7 %collective-permute-start = (bf16[512,384]{1,0:T(8,128)(2,1)}, bf16[512,384]{1,0:T(8,128)(2,1)S(1)}, u32[]{:S(2)}, u32[]{:S(2)}) collective-permute-start(bf16[512,384]{1,0:T(8,128)(2,1)} %get-tuple-element.26.own_ref), channel_id=1, source_target_pairs={{0,4},{4,8},{8,12},{12,16},{16,20},{20,24},{24,28},{28,32},{32,36}... | collective-permute-start | bytes 1179656 | tf_op jit(solution)/shard_map/ppermute | solution.py:389
  46.7 0.7 copy-start.11
  46.7 0.9 copy-start.12
  46.8 1.0 copy-start.3
  58.1 36.9 %all-to-all-start.1 = ((bf16[64,8,384]{2,1,0:T(8,128)(2,1)}), bf16[64,8,384]{2,1,0:T(8,128)(2,1)S(1)}, u32[]{:S(2)}, u32[]{:S(2)}) async-start(bf16[64,8,384]{2,1,0:T(8,128)(2,1)} %bitcast.7), calls=%async_computation.1 | async-start | bytes 786432 | tf_op jit(solution)/shard_map/all_to_all | solution.py:419
  69.2 22.7 %collective-permute-start.5 = (bf16[512,384]{1,0:T(8,128)(2,1)}, bf16[512,384]{1,0:T(8,128)(2,1)S(1)}, u32[]{:S(2)}, u32[]{:S(2)}) collective-permute-start(bf16[512,384]{1,0:T(8,128)(2,1)} %get-tuple-element.34), channel_id=1, source_target_pairs={{0,4},{4,8},{8,12},{12,16},{16,20},{20,24},{24,28},{28,32},{32,36}... | collective-permute-start | bytes 1179656 | tf_op jit(solution)/shard_map/ppermute | solution.py:421
  72.1 22.9 %collective-permute-start.6 = (bf16[512,384]{1,0:T(8,128)(2,1)}, bf16[512,384]{1,0:T(8,128)(2,1)S(1)}, u32[]{:S(2)}, u32[]{:S(2)}) collective-permute-start(bf16[512,384]{1,0:T(8,128)(2,1)} %get-tuple-element.35), channel_id=1, source_target_pairs={{4,0},{8,4},{12,8},{16,12},{20,16},{24,20},{28,24},{32,28},{36,32}... | collective-permute-start | bytes 1179656 | tf_op jit(solution)/shard_map/ppermute | solution.py:420
  76.2 35.5 %collective-permute-start.2 = (bf16[256,384]{1,0:T(8,128)(2,1)}, bf16[256,384]{1,0:T(8,128)(2,1)S(1)}, u32[]{:S(2)}, u32[]{:S(2)}) collective-permute-start(bf16[256,384]{1,0:T(8,128)(2,1)} %get-tuple-element.29), channel_id=1, source_target_pairs={{0,1},{1,0},{2,3},{3,2},{4,5},{5,4},{6,7},{7,6},{8,9},{9,8},{10,11... | collective-permute-start | bytes 589832 | tf_op jit(solution)/shard_map/ppermute | solution.py:431
  91.9 3.2 %copy-start.1 = (bf16[512,384]{1,0:T(8,128)(2,1)}, bf16[512,384]{1,0:T(8,128)(2,1)S(1)}, u32[]{:S(2)}) copy-start(bf16[512,384]{1,0:T(8,128)(2,1)S(1)} %collective-permute-done.5.fl_ref) | copy-start | bytes 1179652
  95.1 0.7 copy-start.2
  95.1 0.9 copy-start
  96.0 13.2 %copy-start.14 = (bf16[256,384]{1,0:T(8,128)(2,1)S(1)}, bf16[256,384]{1,0:T(8,128)(2,1)}, u32[]{:S(2)}) copy-start(bf16[256,384]{1,0:T(8,128)(2,1)} %get-tuple-element.30) | copy-start | bytes 589828
  96.0 15.7 %copy-start.13 = (bf16[256,384]{1,0:T(8,128)(2,1)S(1)}, bf16[256,384]{1,0:T(8,128)(2,1)}, u32[]{:S(2)}) copy-start(bf16[256,384]{1,0:T(8,128)(2,1)} %get-tuple-element.31) | copy-start | bytes 589828
  104.7 27.1 %collective-permute-start.7 = (bf16[400,384]{1,0:T(8,128)(2,1)}, bf16[400,384]{1,0:T(8,128)(2,1)S(1)}, u32[]{:S(2)}, u32[]{:S(2)}) collective-permute-start(bf16[400,384]{1,0:T(8,128)(2,1)} %get-tuple-element.38), channel_id=1, source_target_pairs={{0,1},{1,0},{2,3},{3,2},{4,5},{5,4},{6,7},{7,6},{8,9},{9,8},{10,11... | collective-permute-start | bytes 921608 | tf_op jit(solution)/shard_map/ppermute | solution.py:453
  106.0 25.8 %collective-permute-start.8 = (bf16[400,384]{1,0:T(8,128)(2,1)}, bf16[400,384]{1,0:T(8,128)(2,1)S(1)}, u32[]{:S(2)}, u32[]{:S(2)}) collective-permute-start(bf16[400,384]{1,0:T(8,128)(2,1)} %get-tuple-element.39), channel_id=1, source_target_pairs={{0,2},{1,3},{2,0},{3,1},{4,6},{5,7},{6,4},{7,5},{8,10},{9,11},{10,... | collective-permute-start | bytes 921608 | tf_op jit(solution)/shard_map/ppermute | solution.py:453
  108.4 23.3 %collective-permute-start.9 = (bf16[400,384]{1,0:T(8,128)(2,1)}, bf16[400,384]{1,0:T(8,128)(2,1)S(1)}, u32[]{:S(2)}, u32[]{:S(2)}) collective-permute-start(bf16[400,384]{1,0:T(8,128)(2,1)} %get-tuple-element.40), channel_id=1, source_target_pairs={{0,3},{1,2},{2,1},{3,0},{4,7},{5,6},{6,5},{7,4},{8,11},{9,10},{10,... | collective-permute-start | bytes 921608 | tf_op jit(solution)/shard_map/ppermute | solution.py:453
  109.2 18.1 %collective-permute-start.3 = (bf16[256,384]{1,0:T(8,128)(2,1)S(1)}, bf16[256,384]{1,0:T(8,128)(2,1)S(1)}, u32[]{:S(2)}, u32[]{:S(2)}) collective-permute-start(bf16[256,384]{1,0:T(8,128)(2,1)S(1)} %copy-done.14), channel_id=1, source_target_pairs={{0,2},{1,3},{2,0},{3,1},{4,6},{5,7},{6,4},{7,5},{8,10},{9,11},{10,... | collective-permute-start | bytes 589832 | tf_op jit(solution)/shard_map/ppermute | solution.py:431
  111.7 20.1 %copy-start.7 = (bf16[256,384]{1,0:T(8,128)(2,1)}, bf16[256,384]{1,0:T(8,128)(2,1)S(1)}, u32[]{:S(2)}) copy-start(bf16[256,384]{1,0:T(8,128)(2,1)S(1)} %collective-permute-done.2.o1) | copy-start | bytes 589828
  111.7 20.1 %collective-permute-start.4 = (bf16[256,384]{1,0:T(8,128)(2,1)S(1)}, bf16[256,384]{1,0:T(8,128)(2,1)S(1)}, u32[]{:S(2)}, u32[]{:S(2)}) collective-permute-start(bf16[256,384]{1,0:T(8,128)(2,1)S(1)} %copy-done.13), channel_id=1, source_target_pairs={{0,3},{1,2},{2,1},{3,0},{4,7},{5,6},{6,5},{7,4},{8,11},{9,10},{10,... | collective-permute-start | bytes 589832 | tf_op jit(solution)/shard_map/ppermute | solution.py:431
  127.3 4.5 %copy-start.8 = (bf16[256,384]{1,0:T(8,128)(2,1)}, bf16[256,384]{1,0:T(8,128)(2,1)S(1)}, u32[]{:S(2)}) copy-start(bf16[256,384]{1,0:T(8,128)(2,1)S(1)} %collective-permute-done.3.o2) | copy-start | bytes 589828
  131.7 0.7 copy-start.9
  131.7 0.8 copy-start.4
  131.7 0.9 copy-start.5
  131.8 1.0 copy-start.6

commit v2 on v0

v2 whole, which is shorter than its diff:
```python
import jax
import jax.numpy as jnp
from jax import lax
from jax.experimental import pallas as pl
from jax.experimental.pallas import tpu as pltpu
from jax.sharding import PartitionSpec as P

HD = 64
EPS = 1e-06
DEAD = -1e30
EMPTY = 32768.0
LOG4 = 1.3862943611198906
F32 = jnp.float32
BF16 = jnp.bfloat16
VMEM_LIMIT = 60 * 1024 * 1024
HEAVY = 10**13

NN = (((1,), (0,)), ((), ()))
NT = (((1,), (1,)), ((), ()))
TN = (((0,), (0,)), ((), ()))


def mm(a, b, dims=NN):
    return lax.dot_general(a, b, dims, preferred_element_type=F32)


def iota(shape, dim):
    return lax.broadcasted_iota(jnp.int32, shape, dim)


def row_scale(matrix):
    return lax.rsqrt(jnp.mean(matrix * matrix, axis=-1, keepdims=True) + EPS)


def to_row(col):
    n = col.shape[0]
    eye = iota((n, n), 0) == iota((n, n), 1)
    return jnp.sum(jnp.where(eye, col, jnp.zeros_like(col)), axis=0, keepdims=True)


def to_col(row):
    n = row.shape[1]
    eye = iota((n, n), 0) == iota((n, n), 1)
    return jnp.sum(jnp.where(eye, row, jnp.zeros_like(row)), axis=1, keepdims=True)


class Source:
    def __init__(self, ref, buf, sems, first, pieces):
        self.buf = buf
        self.copies = []
        self.done = []
        for i, piece in enumerate(pieces):
            src, dst = (ref, buf) if piece is None else (ref.at[piece[0]], buf.at[piece[1]])
            self.copies.append(pltpu.make_async_copy(src, dst, sems.at[first + i]))
            self.done.append(False)

    def start(self):
        for copy in self.copies:
            copy.start()

    def wait(self, i=0):
        if not self.done[i]:
            self.done[i] = True
            self.copies[i].wait()
        return self.buf

    def __getitem__(self, at):
        return self.wait()[at]


class Sink:
    def __init__(self, ref, buf, sem):
        self.buf = buf
        self.shape = buf.shape
        self.dtype = buf.dtype
        self.copy = pltpu.make_async_copy(buf, ref, sem)
        self.started = False

    def __setitem__(self, at, value):
        self.buf[at] = value

    def __getitem__(self, at):
        return self.buf[at]

    def send(self):
        if not self.started:
            self.started = True
            self.copy.start()


class Taken:
    def __init__(self, shape, dtype, pieces=(None,)):
        self.shape, self.dtype, self.pieces = shape, dtype, pieces


SMALL = "small"
RAW = "raw"


def call(body, ins, args, outs, flops, name, scratch=()):
    specs = []
    for spec, arg in zip(ins, args):
        if spec is None:
            spec = Taken(arg.shape, arg.dtype)
        specs.append(spec)
    taken = [spec for spec in specs if isinstance(spec, Taken)]
    n_copies = sum(1 if callable(spec.pieces) else len(spec.pieces) for spec in taken)

    def kernel(*refs):
        refs = list(refs)
        in_refs = refs[: len(specs)]
        out_refs = refs[len(specs) : len(specs) + len(outs)]
        rest = refs[len(specs) + len(outs) :]
        in_bufs = rest[: len(taken)]
        out_bufs = rest[len(taken) : len(taken) + len(outs)]
        in_sems, out_sems = rest[len(taken) + len(outs) : len(taken) + len(outs) + 2]
        extra = rest[len(taken) + len(outs) + 2 :]
        operands, used, first = [], 0, 0
        for spec, ref in zip(specs, in_refs):
            if not isinstance(spec, Taken):
                operands.append(ref)
                continue
            pieces = spec.pieces() if callable(spec.pieces) else spec.pieces
            source = Source(ref, in_bufs[used], in_sems, first, pieces)
            source.start()
            operands.append(source)
            used += 1
            first += len(pieces)
        sinks = [Sink(r, b, out_sems.at[i]) for i, (r, b) in enumerate(zip(out_refs, out_bufs))]
        body(*operands, *sinks, *extra)
        for sink in sinks:
            sink.send()
        for source in operands:
            if isinstance(source, Source):
                for i in range(len(source.copies)):
                    source.wait(i)
        for sink in sinks:
            sink.copy.wait()

    return pl.pallas_call(
        kernel,
        in_specs=[SM if spec == SMALL else HBM for spec in specs],
        out_specs=[HBM] * len(outs),
        out_shape=[jax.ShapeDtypeStruct(shape, dtype) for shape, dtype in outs],
        scratch_shapes=[pltpu.VMEM(spec.shape, spec.dtype) for spec in taken]
        + [pltpu.VMEM(shape, dtype) for shape, dtype in outs]
        + [pltpu.SemaphoreType.DMA((n_copies,)), pltpu.SemaphoreType.DMA((len(outs),))]
        + list(scratch),
        compiler_params=pltpu.CompilerParams(vmem_limit_bytes=VMEM_LIMIT),
        cost_estimate=pl.CostEstimate(flops=flops, bytes_accessed=4 << 20, transcendentals=0),
        name=name,
    )(*args)


SM = pl.BlockSpec(memory_space=pltpu.SMEM)
HBM = pl.BlockSpec(memory_space=pl.ANY)


def my_columns(width):
    return pl.ds(pl.multiple_of(lax.axis_index("head") * width, 128), width)


def modulation_rows(mod, clip_ref):
    clip = clip_ref[lax.axis_index("st")]
    return [mod[i, pl.ds(clip, 1), :] for i in range(3)]


def video_front(tokens, mod, weights, clip_ref, kv, modulated):
    rows = kv.shape[0] // 2
    shifts, scales, _ = modulation_rows(mod, clip_ref)
    inputs = tokens[...].astype(F32)
    hidden = (inputs * row_scale(inputs) * (1.0 + scales) + shifts).astype(BF16)
    modulated[...] = hidden
    modulated.send()
    for i in range(2):
        kv[pl.ds(i * rows, rows), :] = mm(hidden, weights.wait(i)[i]).astype(BF16)


def slot_of(trow, tcol, axis):
    n = trow.shape[1]
    earlier = (tcol == trow) & (iota((n, n), axis) < iota((n, n), 1 - axis))
    rank = jnp.sum(earlier.astype(jnp.int32), axis=axis, keepdims=True)
    return (trow if axis == 0 else tcol) * 8 + rank


def audio_front(audio, targets, weights, after, out):
    sounds = audio[...].astype(F32)
    sound_in = (sounds * row_scale(sounds)).astype(BF16)
    rows = sound_in.shape[0]
    trow = targets[...]
    slot = slot_of(trow, to_col(trow), 0)
    slots = out.shape[0]
    place = iota((slots, rows), 0)
    to_key = (place == slot).astype(BF16)
    to_value = (place == slot + 4).astype(BF16)
    dispatch = jnp.concatenate((to_key, to_value), axis=1)
    filled = jnp.sum(dispatch.astype(F32), axis=1, keepdims=True)
    pairs = [mm(sound_in, weights.wait(i)[i]).astype(BF16) for i in range(2)]
    sent = mm(dispatch, jnp.concatenate(pairs, axis=0))
    shape = sent.shape
    mark = ((iota(shape, 0) & 7) < 4) & (iota(shape, 1) == 0) & (filled < 0.5)
    out[...] = jnp.where(mark, EMPTY, sent).astype(BF16)


def query_front(modulated, cotangent, mod, wq, wo, clip_ref, q, g, gt):
    gating = modulation_rows(mod, clip_ref)[2]
    queries = mm(modulated[...], wq[0]).astype(BF16)
    q[...] = (queries.astype(F32) * (float(HD) ** -0.5)).astype(BF16)
    q.send()
    out_grad = (cotangent[...].astype(F32) * gating).astype(BF16)
    grads = mm(out_grad, wo[...], NT)
    g[...] = grads.astype(BF16)
    g.send()
    gt[...] = grads.T.astype(BF16)


def neighbours(position):
    odd = position & 1
    return position + 1 - 2 * odd, position - 1 + 2 * odd


def attention(q_in, g_in, gt_in, own, near, far, slots_in, clip_ref, dropped_ref,
              at, dq, d_own, d_near, d_far, d_audio, k_all, v_all, bias_ref, sems):
    rows, width = q_in.buf.shape
    slots = slots_in.buf.shape[0]
    half = slots // 2
    loads = []
    for i, ref in enumerate((near, own, far)):
        for j, dst in enumerate((k_all, v_all)):
            src = ref.at[pl.ds(j * rows, rows)]
            loads.append(pltpu.make_async_copy(src, dst.at[pl.ds(i * rows, rows)], sems.at[2 * i + j]))
    for load in loads:
        load.start()
    position = lax.axis_index("st")
    count = clip_ref.shape[0]
    clip = clip_ref[position]

    def side_bias(tile):
        inside = (tile >= 0) & (tile < count)
        other = clip_ref[jnp.clip(tile, 0, count - 1)]
        return jnp.where(inside & (other == clip), -LOG4, DEAD)

    near_bias, far_bias = [side_bias(tile) for tile in neighbours(position)]
    alive = dropped_ref[clip] == 0
    for i, bias in enumerate((near_bias, -LOG4, far_bias)):
        bias_ref[pl.ds(i * rows, rows), :] = jnp.full((rows, 128), bias, F32)
    pick_at = (iota((half, slots), 0) >> 2) * 8 + (iota((half, slots), 0) & 3)
    arrived = slots_in[...]
    for i, dst in enumerate((k_all, v_all)):
        pick = (iota((half, slots), 1) == pick_at + 4 * i).astype(BF16)
        dst[pl.ds(3 * rows, half), :] = mm(pick, arrived).astype(BF16)
    head = k_all[pl.ds(3 * rows, half), pl.ds(0, 128)].astype(F32)
    live = (head[:, 0:1] < EMPTY * 0.5) & alive
    bias_ref[pl.ds(3 * rows, half), :] = jnp.broadcast_to(jnp.where(live, -LOG4, DEAD), (half, 128))
    lane = iota((rows, 128), 1)
    q_ref, g_ref, gt_ref = q_in.wait(), g_in.wait(), gt_in.wait()
    for load in loads:
        load.wait()
    sinks = (d_near, d_own, d_far)
    audio_grads = []
    for pair in range(width // 128):
        cols = slice(pair * 128, (pair + 1) * 128)
        q_pair = q_ref[:, cols]
        g_pair = g_ref[:, cols]
        keys = k_all[:, cols]
        values = v_all[:, cols]
        keys_t = keys.T
        values_t = values.T
        qs, gs, ps, ss = [], [], [], []
        for side in range(2):
            mine = (lane // HD) == side
            half_rows = slice(side * HD, (side + 1) * HD)
            head_rows = slice(pair * 128 + side * HD, pair * 128 + (side + 1) * HD)
            q = jnp.where(mine, q_pair, jnp.zeros_like(q_pair))
            g = jnp.where(mine, g_pair, jnp.zeros_like(g_pair))
            bias = jnp.concatenate([bias_ref[...]] * 2, axis=1)
            weights = jnp.exp(mm(keys, q, NT) + bias)
            inverse = 1.0 / jnp.sum(weights, axis=0, keepdims=True)
            probs = weights * inverse
            rounded = probs.astype(BF16)
            att = mm(values_t[half_rows], rounded).astype(BF16)
            at[head_rows, :] = att
            dots = jnp.sum(att.astype(F32) * gt_ref[head_rows, :].astype(F32), axis=0, keepdims=True)
            score_grad = (probs * (mm(values, g, NT) - dots)).astype(BF16)
            dq[head_rows, :] = (mm(keys_t[half_rows], score_grad) * (float(HD) ** -0.5)).astype(BF16)
            qs.append(q)
            gs.append(g)
            ps.append(rounded)
            ss.append(score_grad)
        d_keys = mm(jnp.concatenate(ss, axis=1), jnp.concatenate(qs, axis=0))
        d_values = mm(jnp.concatenate(ps, axis=1), jnp.concatenate(gs, axis=0))
        for b, sink in enumerate(sinks):
            block = slice(b * rows, (b + 1) * rows)
            sink[pl.ds(0, rows), cols] = d_keys[block].astype(sink.dtype)
            sink[pl.ds(rows, rows), cols] = d_values[block].astype(sink.dtype)
        audio_grads.append((d_keys[3 * rows :].astype(BF16), d_values[3 * rows :].astype(BF16)))
    for i in range(2):
        d_audio[pl.ds(i * half, half), :] = jnp.concatenate([grad[i] for grad in audio_grads], axis=1)


def out_project(d_audio, at, wo, d_slots, to_core, mine, cross):
    rows, width = mine.shape
    slots = d_slots.shape[0]
    half = slots // 2
    back_row = iota((slots, half), 0)
    back_at = (back_row >> 3) * 4 + (back_row & 3)
    total = jnp.zeros((slots, width), F32)
    for i in range(2):
        put = ((iota((slots, half), 1) == back_at) & ((back_row & 4) == 4 * i)).astype(BF16)
        total = total + mm(put, d_audio[pl.ds(i * half, half), :])
    d_slots[...] = total.astype(BF16)
    d_slots.send()
    attended = at[...].astype(F32).T.astype(BF16)
    weights = wo.wait()
    me = lax.axis_index("head")

    def chunk(k):
        cols = pl.ds(pl.multiple_of((me ^ k) * width, 128), width)
        return mm(attended, weights[:, cols]).astype(BF16)

    to_core[pl.ds(0, rows), :] = chunk(1)
    to_core[pl.ds(rows, rows), :] = chunk(3)
    to_core.send()
    mine[...] = chunk(0)
    cross[...] = chunk(2)


def pair_sum_out(mine, cross, arrived, mine_out, cross_out):
    rows = mine_out.shape[0]
    got = arrived.wait()
    cross_out[...] = (cross[...].astype(F32) + got[pl.ds(rows, rows), :].astype(F32)).astype(BF16)
    cross_out.send()
    mine_out[...] = mine[...].astype(F32) + got[pl.ds(0, rows), :].astype(F32)


def finish_out(tokens, mod, mine, cross, clip_ref, out):
    cols = my_columns(out.shape[1])
    gating = mod.wait()[2, pl.ds(clip_ref[lax.axis_index("st")], 1), cols]
    total = mine[...] + cross[...].astype(F32)
    out[...] = (tokens[...].astype(F32) + gating * total).astype(BF16)


def two_terms(row):
    high = row.astype(BF16).astype(F32)
    where_row = iota((16, row.shape[1]), 0)
    return jnp.where(where_row == 0, high, jnp.where(where_row == 1, row - high, 0.0)).astype(BF16)


def input_project(targets, mod, dq, d_own, near, far, back, tokens, audio, weights, audio_weights, clip_ref, after,
                  to_core, mine, cross, scale_out, part_ref):
    rows = tokens.buf.shape[0]
    sound_rows = audio.buf.shape[0]
    both = rows + sound_rows
    width = mine.shape[1]
    me = lax.axis_index("head")
    scales = modulation_rows(mod, clip_ref)[1]
    queries = dq[...].astype(F32).T.astype(BF16)
    pair = (d_own[...] + near[...].astype(F32) + far[...].astype(F32)).astype(BF16)
    trow = targets[...]
    slot = slot_of(trow, to_col(trow), 1)
    arrived = back[...]
    slots = arrived.shape[0]
    sound_grads = []
    for i in range(2):
        pick = (iota((sound_rows, slots), 1) == slot + 4 * i).astype(BF16)
        sound_grads.append(mm(pick, arrived).astype(BF16))
    inputs = tokens[...].astype(F32)
    scale = row_scale(inputs)
    hat = inputs * scale * (1.0 + scales)
    sounds = audio[...].astype(F32)
    sound_scale = row_scale(sounds)
    sound_normed = sounds * sound_scale
    scale_out[pl.ds(0, rows), :] = jnp.broadcast_to(scale, (rows, 128))
    scale_out[pl.ds(rows, sound_rows), :] = jnp.broadcast_to(sound_scale, (sound_rows, 128))
    scale_out.send()
    grads = (queries, pair[:rows], pair[rows:])
    part = sum(mm(grad, weights.wait(i)[i], NT) for i, grad in enumerate(grads)).astype(BF16)
    part_ref[pl.ds(0, rows), :] = part
    dots = jnp.sum(part.astype(F32) * hat, axis=1, keepdims=True)
    part = sum(mm(grad, audio_weights.wait(i)[i], NT) for i, grad in enumerate(sound_grads)).astype(BF16)
    part_ref[pl.ds(rows, sound_rows), :] = part
    sound_dots = jnp.sum(part.astype(F32) * sound_normed, axis=1, keepdims=True)
    extra = two_terms(jnp.concatenate((to_row(dots), to_row(sound_dots)), axis=1))
    for k, sink, first in ((1, to_core, 0), (3, to_core, both + 16), (0, mine, 0), (2, cross, 0)):
        cols = pl.ds(pl.multiple_of((me ^ k) * width, 128), width)
        sink[pl.ds(first, both), :] = part_ref[:, cols]
        sink[pl.ds(first + both, 16), :] = extra
        if k == 3:
            to_core.send()


def pair_sum(mine, cross, arrived, mine_out, cross_out):
    height = mine_out.shape[0]
    both = height - 16
    got = arrived.wait()
    total = cross[...].astype(F32) + got[pl.ds(height, height), :].astype(F32)
    extra = total[both : both + 1] + total[both + 1 : both + 2]
    cross_out[pl.ds(0, both), :] = total[:both].astype(BF16)
    cross_out[pl.ds(both, 16), :] = two_terms(extra)
    cross_out.send()
    mine_out[...] = mine[...].astype(F32) + got[pl.ds(0, height), :].astype(F32)


def finish(tokens, cotangent, audio, scale_in, mod, mine, cross, clip_ref, video_grad, audio_grad):
    rows, width = video_grad.shape
    sound_rows = audio_grad.shape[0]
    both = rows + sound_rows
    model = 4 * width
    cols = my_columns(width)
    scales = mod.wait()[1, pl.ds(clip_ref[lax.axis_index("st")], 1), cols]
    scale = scale_in[...][:, 0:1]
    normed = tokens[...].astype(F32) * scale[:rows]
    sound_normed = audio[...].astype(F32) * scale[rows:]
    total = mine[...] + cross[...].astype(F32)
    row = (total[both : both + 1] + total[both + 1 : both + 2]) * (1.0 / model)
    hat = total[:rows] * (1.0 + scales) - normed * to_col(row[:, :rows])
    video_grad[...] = (cotangent[...].astype(F32) + scale[:rows] * hat).astype(BF16)
    video_grad.send()
    sound_hat = total[rows:both] - sound_normed * to_col(row[:, rows:])
    audio_grad[...] = (scale[rows:] * sound_hat).astype(BF16)


def per_device(
    video_tokens,
    cotangent,
    audio_frames,
    input_weights,
    audio_weights,
    output_weight,
    modulation,
    tile_clip,
    dropped,
    audio_tile,
):
    rows, model = video_tokens.shape
    width = input_weights.shape[2]
    sound_rows = audio_frames.shape[0]
    count = lax.axis_size("st")
    slots = 8 * count
    targets = audio_tile.T
    modulation = jnp.transpose(modulation, (1, 0, 2))

    def layers(first, last):
        pieces = [(pl.ds(i, 1), pl.ds(i - first, 1)) for i in range(first, last)]
        return Taken((last - first, model, width), BF16, pieces)

    def own_block(n):
        return Taken((n, width), BF16, lambda: [((slice(None), my_columns(width)), slice(None))])

    kv, modulated = call(
        video_front,
        (None, None, layers(1, 3), SMALL),
        (video_tokens, modulation, input_weights, tile_clip),
        [((2 * rows, width), BF16), ((rows, model), BF16)],
        2 * rows * model * 2 * width,
        "video_front",
    )
    near_swap = [(i, i ^ 1) for i in range(count)]
    far_swap = [p for i in range(1, count - 2, 2) for p in ((i, i + 1), (i + 1, i))]
    near = lax.ppermute(kv, "st", near_swap)
    far = lax.ppermute(kv, "st", far_swap)
    (sent,) = call(
        audio_front,
        (None, None, layers(0, 2), RAW),
        (audio_frames, targets, audio_weights, kv),
        [((slots, width), BF16)],
        2 * sound_rows * model * 2 * width,
        "audio_front",
    )
    arrived = lax.all_to_all(sent, "st", split_axis=0, concat_axis=0, tiled=True)
    queries, grads, grads_t = call(
        query_front,
        (None, None, None, layers(0, 1), None, SMALL),
        (modulated, cotangent, modulation, input_weights, output_weight, tile_clip),
        [((rows, width), BF16), ((rows, width), BF16), ((width, rows), BF16)],
        HEAVY,
        "query_front",
    )
    half = slots // 2
    attended_t, dq_t, d_own, d_near, d_far, d_audio = call(
        attention,
        (None, None, None, RAW, RAW, RAW, None, SMALL, SMALL),
        (queries, grads, grads_t, kv, near, far, arrived, tile_clip, dropped),
        [
            ((width, rows), BF16),
            ((width, rows), BF16),
            ((2 * rows, width), F32),
            ((2 * rows, width), BF16),
            ((2 * rows, width), BF16),
            ((slots, width), BF16),
        ],
        2 * 6 * rows * (3 * rows + half) * width,
        "attention",
        (
            pltpu.VMEM((3 * rows + half, width), BF16),
            pltpu.VMEM((3 * rows + half, width), BF16),
            pltpu.VMEM((3 * rows + half, 128), F32),
            pltpu.SemaphoreType.DMA((6,)),
        ),
    )
    back_near = lax.ppermute(d_near, "st", near_swap)
    back_far = lax.ppermute(d_far, "st", far_swap)
    groups = lax.axis_size("head")
    core_swap = [(i, i ^ 1) for i in range(groups)]
    cross_swap = [(i, i ^ 2) for i in range(groups)]
    block = ((rows, width), BF16)
    d_slots, to_core, mine, cross = call(
        out_project,
        (None, None, None),
        (d_audio, attended_t, output_weight),
        [((slots, width), BF16), ((2 * rows, width), BF16), block, block],
        HEAVY,
        "out_project",
    )
    back = lax.all_to_all(d_slots, "st", split_axis=0, concat_axis=0, tiled=True)
    out_mine, out_cross = call(
        pair_sum_out,
        (None,) * 3,
        (mine, cross, lax.ppermute(to_core, "head", core_swap)),
        [((rows, width), F32), block],
        HEAVY,
        "pair_sum_out",
    )
    (video_out,) = call(
        finish_out,
        (own_block(rows),) + (None,) * 3 + (SMALL,),
        (video_tokens, modulation, out_mine, lax.ppermute(out_cross, "head", cross_swap), tile_clip),
        [block],
        HEAVY,
        "finish_out",
    )
    height = rows + sound_rows + 16
    block = ((height, width), BF16)
    to_core, mine, cross, scale = call(
        input_project,
        (None,) * 9 + (layers(0, 3), layers(0, 2), SMALL, RAW),
        (
            targets,
            modulation,
            dq_t,
            d_own,
            back_near,
            back_far,
            back,
            video_tokens,
            audio_frames,
            input_weights,
            audio_weights,
            tile_clip,
            out_cross,
        ),
        [((2 * height, width), BF16), block, block, ((rows + sound_rows, 128), F32)],
        2 * (3 * rows + 2 * sound_rows) * width * model,
        "input_project",
        (pltpu.VMEM((rows + sound_rows, model), BF16),),
    )
    mine, cross = call(
        pair_sum,
        (None,) * 3,
        (mine, cross, lax.ppermute(to_core, "head", core_swap)),
        [((height, width), F32), block],
        height * width,
        "pair_sum",
    )
    video_grad, audio_grad = call(
        finish,
        (own_block(rows), own_block(rows), own_block(sound_rows)) + (None,) * 4 + (SMALL,),
        (
            video_tokens,
            cotangent,
            audio_frames,
            scale,
            modulation,
            mine,
            lax.ppermute(cross, "head", cross_swap),
            tile_clip,
        ),
        [((rows, width), BF16), ((sound_rows, width), BF16)],
        4 * rows * model,
        "finish",
    )
    return video_out, video_grad, audio_grad


def solution(mesh):
    return jax.shard_map(
        per_device,
        mesh=mesh,
        in_specs=(
            P("st", None),
            P("st", None),
            P("st", None),
            P(None, None, "head"),
            P(None, None, "head"),
            P("head", None),
            P(),
            P(),
            P(),
            P("st", None),
        ),
        out_specs=(P("st", "head"), P("st", "head"), P("st", "head")),
        check_vma=False,
    )
```

time: 210 us -> 111 us (0.53)
  waiting for transfers between devices: 87.4 us -> 23.1 us
  Pallas kernels: 0 us -> 44.8 us
  matrix products: 31.6 us -> 0 us
  other arithmetic: 19.7 us -> 0 us
  local copies, waits for them, and re-layouts: 16.6 us -> 2.28 us
  between operations: 14.7 us -> 0.95 us
    psum x1 -> x0, waiting for transfers between devices: 50.5 us -> none  [per_device(): lax.psum(video_part.astype(jnp.bfloat16), 'head').astype(jnp.float32)]
    pallas_call x0 -> x10, Pallas kernels: none -> 44.8 us  [call(): pl.pallas_call(kernel, in_specs=[SM if spec == SMALL else HBM for spec in...]
    dot_general x20 -> x0, matrix products: 31.6 us -> none  [the longest x1 2.82 us: raw_scores(): jnp.einsum('nhe,mhe->hnm', queries, key_rows[:, 0], preferred_element_typ...]
    unnamed x3 -> x0, waiting for transfers between devices: 13.3 us -> none
    convert_element_type x10 -> x0, other arithmetic: 8.98 us -> none  [the longest x1 1.83 us: per_device(): video_out = (input_share + gate_share * out_share).astype(jnp.bfloat16)]
    reduce_sum x10 -> x0, other arithmetic: 7.53 us -> none  [the longest x2 1.53 us: row_scale(): jnp.mean(matrix * matrix, axis=-1, keepdims=True) + epsilon]
    ppermute x4 -> x8, starting transfers between devices: 10.1 us -> 17.5 us  [the longest x2 5.88 us: per_device(): lax.ppermute(to_core, 'head', core_swap)]
    all_to_all x3 -> x2, starting transfers between devices: 28.8 us -> 21.8 us  [the longest x1 11.8 us: per_device(): lax.all_to_all(sent, 'st', split_axis=0, concat_axis=0, tiled=True)]
  transfers between devices with their start and end apart: 9 -> 10, of which waited for: 6 -> 5; matrix products, arithmetic and copies ran while one was open for 16% -> 0% of each run, Pallas kernels for 0% -> 14%
where the time goes in v2:
time: 111 us; the launch traced here: 110 us
  Pallas kernels  44.8 us (40%)
  starting transfers between devices  39.3 us (35%)
  waiting for transfers between devices  23.1 us (21%)
  local copies, waits for them, and re-layouts  2.28 us (2%)
    pallas_call x10, Pallas kernels, call(): pl.pallas_call(kernel, in_specs=[SM if spec == SMALL else HBM for spec in...  44.8 us
    all_to_all x1, starting transfers between devices, per_device(): lax.all_to_all(sent, 'st', split_axis=0, concat_axis=0, tiled=True)  11.8 us
    all_to_all x1, starting transfers between devices, per_device(): lax.all_to_all(d_slots, 'st', split_axis=0, concat_axis=0, tiled=True)  10 us
    all_to_all x1, waiting for transfers between devices, per_device(): lax.all_to_all(sent, 'st', split_axis=0, concat_axis=0, tiled=True)  8.12 us
    ppermute x1, waiting for transfers between devices, per_device(): back_near = lax.ppermute(d_near, 'st', near_swap)  8.06 us
    ppermute x2, starting transfers between devices, per_device(): lax.ppermute(to_core, 'head', core_swap)  5.88 us
    ppermute x1, waiting for transfers between devices, per_device(): lax.ppermute(cross, 'head', cross_swap)  4.76 us
    ppermute x1, starting transfers between devices, per_device(): near = lax.ppermute(kv, 'st', near_swap)  4.22 us
  transfers between devices with their start and end apart: 10, of which 5 were waited for; matrix products, arithmetic and copies ran while one was open for 0% of the time, Pallas kernels for 14%

profile of v2, /device:TPU:1, one launch (start us, length us, event | category | flops | bytes accessed | tf_op | source)
XLA Modules:
  0.0 110.5 jit_solution(15568421277520716317)
XLA Ops:
  0.6 4.2 %video_front.1 = (bf16[512,384]{1,0:T(8,128)(2,1)}, bf16[256,1536]{1,0:T(8,128)(2,1)}) custom-call(bf16[256,1536]{1,0:T(8,128)(2,1)} %refs_0_.7, f32[3,4,1536]{2,1,0:T(4,128)} %bitcast.7, bf16[3,1536,384]{2,1,0:T(8,128)(2,1)} %refs_9_.1, s32[64]{0:T(128)} %refs_7_.5), custom_call_target="tpu_custom_call" | custom-call | flops 603979776 | bytes 4194304 | tf_op jit(solution)/shard_map/video_front/pallas_call | solution.py:140
  4.8 1.4 %collective-permute-start.1 = (bf16[512,384]{1,0:T(8,128)(2,1)}, bf16[512,384]{1,0:T(8,128)(2,1)}, u32[]{:S(2)}, u32[]{:S(2)}) collective-permute-start(bf16[512,384]{1,0:T(8,128)(2,1)} %get-tuple-element.32.refs_3_), channel_id=1, source_target_pairs={{4,8},{8,4},{12,16},{16,12},{20,24},{24,20},{28,32},{32,28},{36,40... | collective-permute-start | bytes 1179656 | tf_op jit(solution)/shard_map/ppermute | solution.py:461
  6.2 4.2 %collective-permute-start = (bf16[512,384]{1,0:T(8,128)(2,1)}, bf16[512,384]{1,0:T(8,128)(2,1)}, u32[]{:S(2)}, u32[]{:S(2)}) collective-permute-start(bf16[512,384]{1,0:T(8,128)(2,1)} %get-tuple-element.32.refs_3_), channel_id=1, source_target_pairs={{0,4},{4,0},{8,12},{12,8},{16,20},{20,16},{24,28},{28,24},{32,36},... | collective-permute-start | bytes 1179656 | tf_op jit(solution)/shard_map/ppermute | solution.py:460
  10.5 3.3 %audio_front.1 = bf16[512,384]{1,0:T(8,128)(2,1)} custom-call(bf16[128,1536]{1,0:T(8,128)(2,1)} %refs_2_.7, s32[1,128]{1,0:T(1,128)} %bitcast.13, bf16[2,1536,384]{2,1,0:T(8,128)(2,1)} %refs_10_.1, bf16[512,384]{1,0:T(8,128)(2,1)} %get-tuple-element.32.refs_3_), custom_call_target="tpu_custom_call" | custom-call | flops 301989888 | bytes 4194304 | tf_op jit(solution)/shard_map/audio_front/pallas_call | solution.py:140
  13.7 11.8 %all-to-all-start = ((bf16[64,8,384]{2,1,0:T(8,128)(2,1)}), bf16[64,8,384]{2,1,0:T(8,128)(2,1)}, u32[]{:S(2)}, u32[]{:S(2)}) async-start(bf16[64,8,384]{2,1,0:T(8,128)(2,1)} %bitcast.6), calls=%async_computation | async-start | bytes 786432 | tf_op jit(solution)/shard_map/all_to_all | solution.py:470
  25.6 4.7 %query_front.1 = (bf16[256,384]{1,0:T(8,128)(2,1)}, bf16[256,384]{1,0:T(8,128)(2,1)}, bf16[384,256]{1,0:T(8,128)(2,1)}) custom-call(bf16[256,1536]{1,0:T(8,128)(2,1)} %get-tuple-element.28.refs_0_, bf16[256,1536]{1,0:T(8,128)(2,1)} %refs_1_.3, f32[3,4,1536]{2,1,0:T(4,128)} %bitcast.8, bf16[3,1536,384]{2,1,0:T(8,128)(2,1)} %refs_9_.1, ...), custom_call_target="tpu_custom_call" | custom-call | flops 9999999827968 | bytes 4194304 | tf_op jit(solution)/shard_map/query_front/pallas_call | solution.py:140
  30.3 0.0 collective-permute-done.1.refs_5_
  30.3 0.0 collective-permute-done.refs_4_
  30.3 8.1 %all-to-all-done = bf16[64,8,384]{2,1,0:T(8,128)(2,1)} async-done(((bf16[64,8,384]{2,1,0:T(8,128)(2,1)}), bf16[64,8,384]{2,1,0:T(8,128)(2,1)}, u32[]{:S(2)}, u32[]{:S(2)}) %all-to-all-start) | async-done | bytes 393248 | tf_op jit(solution)/shard_map/all_to_all | solution.py:470
  38.4 12.0 %attention.1 = (bf16[384,256]{1,0:T(8,128)(2,1)}, bf16[384,256]{1,0:T(8,128)(2,1)}, f32[512,384]{1,0:T(8,128)}, bf16[512,384]{1,0:T(8,128)(2,1)}, bf16[512,384]{1,0:T(8,128)(2,1)}, /*index=5*/bf16[512,384]{1,0:T(8,128)(2,1)}) custom-call(bf16[256,384]{1,0:T(8,128)(2,1)} %get-tuple-element.29.refs_0_, bf16[256,384]{1,0:T(8,128)(2,1)} %get-tuple-element.30.refs_1_, ...), custom_call_target="tpu_custom_call" | custom-call | flops 1207959552 | bytes 4194304 | tf_op jit(solution)/shard_map/attention/pallas_call | solution.py:140
  50.4 3.0 %out_project.1 = (bf16[512,384]{1,0:T(8,128)(2,1)}, bf16[512,384]{1,0:T(8,128)(2,1)}, bf16[256,384]{1,0:T(8,128)(2,1)}, bf16[256,384]{1,0:T(8,128)(2,1)}) custom-call(bf16[512,384]{1,0:T(8,128)(2,1)} %get-tuple-element.33.refs_0_, bf16[384,256]{1,0:T(8,128)(2,1)} %get-tuple-element.34.refs_1_, bf16[384,1536]{1,0:T(8,128)(2,1)} %refs_2_.6), custom_call_target="tpu_custom_call" | custom-call | flops 9999999827968 | bytes 4194304 | tf_op jit(solution)/shard_map/out_project/pallas_call | solution.py:140
  53.4 2.9 %collective-permute-start.2 = (bf16[512,384]{1,0:T(8,128)(2,1)}, bf16[512,384]{1,0:T(8,128)(2,1)S(1)}, u32[]{:S(2)}, u32[]{:S(2)}) collective-permute-start(bf16[512,384]{1,0:T(8,128)(2,1)} %get-tuple-element.37), channel_id=1, source_target_pairs={{0,1},{1,0},{2,3},{3,2},{4,5},{5,4},{6,7},{7,6},{8,9},{9,8},{10,11... | collective-permute-start | bytes 1179656 | tf_op jit(solution)/shard_map/ppermute | solution.py:519
  56.3 0.1 collective-permute-start.4
  56.4 1.4 %collective-permute-start.5 = (bf16[512,384]{1,0:T(8,128)(2,1)}, bf16[512,384]{1,0:T(8,128)(2,1)}, u32[]{:S(2)}, u32[]{:S(2)}) collective-permute-start(bf16[512,384]{1,0:T(8,128)(2,1)} %get-tuple-element.43), channel_id=1, source_target_pairs={{4,8},{8,4},{12,16},{16,12},{20,24},{24,20},{28,32},{32,28},{36,40... | collective-permute-start | bytes 1179656 | tf_op jit(solution)/shard_map/ppermute | solution.py:502
  57.8 10.0 %all-to-all-start.1 = ((bf16[64,8,384]{2,1,0:T(8,128)(2,1)}), bf16[64,8,384]{2,1,0:T(8,128)(2,1)}, u32[]{:S(2)}, u32[]{:S(2)}) async-start(bf16[64,8,384]{2,1,0:T(8,128)(2,1)} %bitcast.12), calls=%async_computation.1 | async-start | bytes 786432 | tf_op jit(solution)/shard_map/all_to_all | solution.py:515
  67.8 0.0 collective-permute-done.2.refs_2_
  67.8 0.7 copy-done.2
  68.6 2.1 %pair_sum_out.1 = (f32[256,384]{1,0:T(8,128)}, bf16[256,384]{1,0:T(8,128)(2,1)}) custom-call(bf16[256,384]{1,0:T(8,128)(2,1)} %get-tuple-element.35.refs_0_, bf16[256,384]{1,0:T(8,128)(2,1)} %get-tuple-element.36.refs_1_, bf16[512,384]{1,0:T(8,128)(2,1)} %copy-done.2), custom_call_target="tpu_custom_call" | custom-call | flops 9999999827968 | bytes 4194304 | tf_op jit(solution)/shard_map/pair_sum_out/pallas_call | solution.py:140
  70.7 8.1 %collective-permute-done.4.refs_4_ = bf16[512,384]{1,0:T(8,128)(2,1)} collective-permute-done((bf16[512,384]{1,0:T(8,128)(2,1)}, bf16[512,384]{1,0:T(8,128)(2,1)}, u32[]{:S(2)}, u32[]{:S(2)}) %collective-permute-start.4) | collective-permute-done | bytes 393248 | tf_op jit(solution)/shard_map/ppermute | solution.py:501
  78.8 0.0 collective-permute-done.5.refs_5_
  78.8 1.8 %all-to-all-done.1 = bf16[64,8,384]{2,1,0:T(8,128)(2,1)} async-done(((bf16[64,8,384]{2,1,0:T(8,128)(2,1)}), bf16[64,8,384]{2,1,0:T(8,128)(2,1)}, u32[]{:S(2)}, u32[]{:S(2)}) %all-to-all-start.1) | async-done | bytes 393248 | tf_op jit(solution)/shard_map/all_to_all | solution.py:515
  80.6 7.3 %input_project.1 = (bf16[800,384]{1,0:T(8,128)(2,1)}, bf16[400,384]{1,0:T(8,128)(2,1)}, bf16[400,384]{1,0:T(8,128)(2,1)}, f32[384,128]{1,0:T(8,128)}) custom-call(s32[1,128]{1,0:T(1,128)} %bitcast.14, f32[3,4,1536]{2,1,0:T(4,128)} %bitcast.9, bf16[384,256]{1,0:T(8,128)(2,1)} %get-tuple-element.40.refs_2_, f32[512,384]{1,0:T(8,128)} %get-tuple-element.41.refs_3_, ...), custom_call_target="tpu_custom_call" | custom-call | flops 1207959552 | bytes 4194304 | tf_op jit(solution)/shard_map/input_project/pallas_call | solution.py:140
  88.0 3.0 %collective-permute-start.6 = (bf16[800,384]{1,0:T(8,128)(2,1)}, bf16[800,384]{1,0:T(8,128)(2,1)S(1)}, u32[]{:S(2)}, u32[]{:S(2)}) collective-permute-start(bf16[800,384]{1,0:T(8,128)(2,1)} %get-tuple-element.48), channel_id=1, source_target_pairs={{0,1},{1,0},{2,3},{3,2},{4,5},{5,4},{6,7},{7,6},{8,9},{9,8},{10,11... | collective-permute-start | bytes 1843208 | tf_op jit(solution)/shard_map/ppermute | solution.py:560
  91.0 2.5 %collective-permute-start.3 = (bf16[256,384]{1,0:T(8,128)(2,1)S(1)}, bf16[256,384]{1,0:T(8,128)(2,1)S(1)}, u32[]{:S(2)}, u32[]{:S(2)}) collective-permute-start(bf16[256,384]{1,0:T(8,128)(2,1)S(1)} %copy-done.1), channel_id=1, source_target_pairs={{0,2},{1,3},{2,0},{3,1},{4,6},{5,7},{6,4},{7,5},{8,10},{9,11},{10,... | collective-permute-start | bytes 589832 | tf_op jit(solution)/shard_map/ppermute | solution.py:527
  93.5 0.9 copy-done
  94.3 2.3 %pair_sum.1 = (f32[400,384]{1,0:T(8,128)}, bf16[400,384]{1,0:T(8,128)(2,1)}) custom-call(bf16[400,384]{1,0:T(8,128)(2,1)} %get-tuple-element.46.refs_0_, bf16[400,384]{1,0:T(8,128)(2,1)} %get-tuple-element.47.refs_1_, bf16[800,384]{1,0:T(8,128)(2,1)} %copy-done), custom_call_target="tpu_custom_call" | custom-call | flops 153600 | bytes 4194304 | tf_op jit(solution)/shard_map/pair_sum/pallas_call | solution.py:140
  96.7 1.9 %collective-permute-start.7 = (bf16[400,384]{1,0:T(8,128)(2,1)}, bf16[400,384]{1,0:T(8,128)(2,1)}, u32[]{:S(2)}, u32[]{:S(2)}) collective-permute-start(bf16[400,384]{1,0:T(8,128)(2,1)} %get-tuple-element.50), channel_id=1, source_target_pairs={{0,2},{1,3},{2,0},{3,1},{4,6},{5,7},{6,4},{7,5},{8,10},{9,11},{10,... | collective-permute-start | bytes 921608 | tf_op jit(solution)/shard_map/ppermute | solution.py:575
  98.6 0.4 collective-permute-done.3.refs_3_
  99.0 0.7 copy-done.3
  99.6 2.7 %finish_out.1 = bf16[256,384]{1,0:T(8,128)(2,1)} custom-call(bf16[256,1536]{1,0:T(8,128)(2,1)} %refs_0_.7, f32[3,4,1536]{2,1,0:T(4,128)} %bitcast.10, f32[256,384]{1,0:T(8,128)} %get-tuple-element.38.refs_2_, bf16[256,384]{1,0:T(8,128)(2,1)} %copy-done.3, s32[64]{0:T(128)} %refs_7_.5), custom_call_target="tpu_custom_call" | custom-call | flops 9999999827968 | bytes 4194304 | tf_op jit(solution)/shard_map/finish_out/pallas_call | solution.py:140
  102.3 4.8 %collective-permute-done.7.refs_6_ = bf16[400,384]{1,0:T(8,128)(2,1)} collective-permute-done((bf16[400,384]{1,0:T(8,128)(2,1)}, bf16[400,384]{1,0:T(8,128)(2,1)}, u32[]{:S(2)}, u32[]{:S(2)}) %collective-permute-start.7) | collective-permute-done | bytes 307232 | tf_op jit(solution)/shard_map/ppermute | solution.py:575
  107.1 3.2 %finish.1 = (bf16[256,384]{1,0:T(8,128)(2,1)}, bf16[128,384]{1,0:T(8,128)(2,1)}) custom-call(bf16[256,1536]{1,0:T(8,128)(2,1)} %refs_0_.7, bf16[256,1536]{1,0:T(8,128)(2,1)} %refs_1_.3, bf16[128,1536]{1,0:T(8,128)(2,1)} %refs_2_.7, f32[384,128]{1,0:T(8,128)} %get-tuple-element.45.refs_3_, f32[3,4,1536]{2,1,0:T(4,128)} %bitcast.11, ...), custom_call_target="tpu_custom_call" | custom-call | flops 1572864 | bytes 4194304 | tf_op jit(solution)/shard_map/finish/pallas_call | solution.py:140
  (6 shorter events, 0.0 us)
Async XLA Ops:
  4.8 25.5 %collective-permute-start.1 = (bf16[512,384]{1,0:T(8,128)(2,1)}, bf16[512,384]{1,0:T(8,128)(2,1)}, u32[]{:S(2)}, u32[]{:S(2)}) collective-permute-start(bf16[512,384]{1,0:T(8,128)(2,1)} %get-tuple-element.32.refs_3_), channel_id=1, source_target_pairs={{4,8},{8,4},{12,16},{16,12},{20,24},{24,20},{28,32},{32,28},{36,40... | collective-permute-start | bytes 1179656 | tf_op jit(solution)/shard_map/ppermute | solution.py:461
  6.2 24.1 %collective-permute-start = (bf16[512,384]{1,0:T(8,128)(2,1)}, bf16[512,384]{1,0:T(8,128)(2,1)}, u32[]{:S(2)}, u32[]{:S(2)}) collective-permute-start(bf16[512,384]{1,0:T(8,128)(2,1)} %get-tuple-element.32.refs_3_), channel_id=1, source_target_pairs={{0,4},{4,0},{8,12},{12,8},{16,20},{20,16},{24,28},{28,24},{32,36},... | collective-permute-start | bytes 1179656 | tf_op jit(solution)/shard_map/ppermute | solution.py:460
  13.7 24.7 %all-to-all-start = ((bf16[64,8,384]{2,1,0:T(8,128)(2,1)}), bf16[64,8,384]{2,1,0:T(8,128)(2,1)}, u32[]{:S(2)}, u32[]{:S(2)}) async-start(bf16[64,8,384]{2,1,0:T(8,128)(2,1)} %bitcast.6), calls=%async_computation | async-start | bytes 786432 | tf_op jit(solution)/shard_map/all_to_all | solution.py:470
  53.4 14.4 %collective-permute-start.2 = (bf16[512,384]{1,0:T(8,128)(2,1)}, bf16[512,384]{1,0:T(8,128)(2,1)S(1)}, u32[]{:S(2)}, u32[]{:S(2)}) collective-permute-start(bf16[512,384]{1,0:T(8,128)(2,1)} %get-tuple-element.37), channel_id=1, source_target_pairs={{0,1},{1,0},{2,3},{3,2},{4,5},{5,4},{6,7},{7,6},{8,9},{9,8},{10,11... | collective-permute-start | bytes 1179656 | tf_op jit(solution)/shard_map/ppermute | solution.py:519
  56.3 22.5 %collective-permute-start.4 = (bf16[512,384]{1,0:T(8,128)(2,1)}, bf16[512,384]{1,0:T(8,128)(2,1)}, u32[]{:S(2)}, u32[]{:S(2)}) collective-permute-start(bf16[512,384]{1,0:T(8,128)(2,1)} %get-tuple-element.42), channel_id=1, source_target_pairs={{0,4},{4,0},{8,12},{12,8},{16,20},{20,16},{24,28},{28,24},{32,36},... | collective-permute-start | bytes 1179656 | tf_op jit(solution)/shard_map/ppermute | solution.py:501
  56.4 22.4 %collective-permute-start.5 = (bf16[512,384]{1,0:T(8,128)(2,1)}, bf16[512,384]{1,0:T(8,128)(2,1)}, u32[]{:S(2)}, u32[]{:S(2)}) collective-permute-start(bf16[512,384]{1,0:T(8,128)(2,1)} %get-tuple-element.43), channel_id=1, source_target_pairs={{4,8},{8,4},{12,16},{16,12},{20,24},{24,20},{28,32},{32,28},{36,40... | collective-permute-start | bytes 1179656 | tf_op jit(solution)/shard_map/ppermute | solution.py:502
  57.8 22.8 %all-to-all-start.1 = ((bf16[64,8,384]{2,1,0:T(8,128)(2,1)}), bf16[64,8,384]{2,1,0:T(8,128)(2,1)}, u32[]{:S(2)}, u32[]{:S(2)}) async-start(bf16[64,8,384]{2,1,0:T(8,128)(2,1)} %bitcast.12), calls=%async_computation.1 | async-start | bytes 786432 | tf_op jit(solution)/shard_map/all_to_all | solution.py:515
  67.8 0.8 copy-start.2
  70.7 20.3 %copy-start.1 = (bf16[256,384]{1,0:T(8,128)(2,1)S(1)}, bf16[256,384]{1,0:T(8,128)(2,1)}, u32[]{:S(2)}) copy-start(bf16[256,384]{1,0:T(8,128)(2,1)} %get-tuple-element.39.refs_12_) | copy-start | bytes 589828
  88.0 5.5 %collective-permute-start.6 = (bf16[800,384]{1,0:T(8,128)(2,1)}, bf16[800,384]{1,0:T(8,128)(2,1)S(1)}, u32[]{:S(2)}, u32[]{:S(2)}) collective-permute-start(bf16[800,384]{1,0:T(8,128)(2,1)} %get-tuple-element.48), channel_id=1, source_target_pairs={{0,1},{1,0},{2,3},{3,2},{4,5},{5,4},{6,7},{7,6},{8,9},{9,8},{10,11... | collective-permute-start | bytes 1843208 | tf_op jit(solution)/shard_map/ppermute | solution.py:560
  91.0 8.0 %collective-permute-start.3 = (bf16[256,384]{1,0:T(8,128)(2,1)S(1)}, bf16[256,384]{1,0:T(8,128)(2,1)S(1)}, u32[]{:S(2)}, u32[]{:S(2)}) collective-permute-start(bf16[256,384]{1,0:T(8,128)(2,1)S(1)} %copy-done.1), channel_id=1, source_target_pairs={{0,2},{1,3},{2,0},{3,1},{4,6},{5,7},{6,4},{7,5},{8,10},{9,11},{10,... | collective-permute-start | bytes 589832 | tf_op jit(solution)/shard_map/ppermute | solution.py:527
  93.5 0.9 copy-start
  96.7 10.4 %collective-permute-start.7 = (bf16[400,384]{1,0:T(8,128)(2,1)}, bf16[400,384]{1,0:T(8,128)(2,1)}, u32[]{:S(2)}, u32[]{:S(2)}) collective-permute-start(bf16[400,384]{1,0:T(8,128)(2,1)} %get-tuple-element.50), channel_id=1, source_target_pairs={{0,2},{1,3},{2,0},{3,1},{4,6},{5,7},{6,4},{7,5},{8,10},{9,11},{10,... | collective-permute-start | bytes 921608 | tf_op jit(solution)/shard_map/ppermute | solution.py:575
  99.0 0.7 copy-start.3

commit v3 on v2

v3 whole, which is shorter than its diff:
```python
import jax
import jax.numpy as jnp
from jax import lax
from jax.experimental import pallas as pl
from jax.experimental.pallas import tpu as pltpu
from jax.sharding import PartitionSpec as P

HD = 64
EPS = 1e-06
DEAD = -1e30
EMPTY = 32768.0
LOG4 = 1.3862943611198906
F32 = jnp.float32
BF16 = jnp.bfloat16
VMEM_LIMIT = 60 * 1024 * 1024
HEAVY = 10**13

NN = (((1,), (0,)), ((), ()))
NT = (((1,), (1,)), ((), ()))
TN = (((0,), (0,)), ((), ()))


def mm(a, b, dims=NN):
    return lax.dot_general(a, b, dims, preferred_element_type=F32)


def iota(shape, dim):
    return lax.broadcasted_iota(jnp.int32, shape, dim)


def row_scale(matrix):
    return lax.rsqrt(jnp.mean(matrix * matrix, axis=-1, keepdims=True) + EPS)


def to_row(col):
    n = col.shape[0]
    eye = iota((n, n), 0) == iota((n, n), 1)
    return jnp.sum(jnp.where(eye, col, jnp.zeros_like(col)), axis=0, keepdims=True)


def to_col(row):
    n = row.shape[1]
    eye = iota((n, n), 0) == iota((n, n), 1)
    return jnp.sum(jnp.where(eye, row, jnp.zeros_like(row)), axis=1, keepdims=True)


class Source:
    def __init__(self, ref, buf, sems, first, pieces):
        self.buf = buf
        self.copies = []
        self.done = []
        for i, piece in enumerate(pieces):
            src, dst = (ref, buf) if piece is None else (ref.at[piece[0]], buf.at[piece[1]])
            self.copies.append(pltpu.make_async_copy(src, dst, sems.at[first + i]))
            self.done.append(False)

    def start(self, i):
        self.copies[i].start()

    def wait(self, i=0):
        if not self.done[i]:
            self.done[i] = True
            self.copies[i].wait()
        return self.buf

    def __getitem__(self, at):
        return self.wait()[at]


class Sink:
    def __init__(self, ref, buf, sems, first, pieces):
        self.buf = buf
        self.shape = buf.shape
        self.dtype = buf.dtype
        self.copies = []
        self.started = []
        for i, piece in enumerate(pieces):
            src, dst = (buf, ref) if piece is None else (buf.at[piece], ref.at[piece])
            self.copies.append(pltpu.make_async_copy(src, dst, sems.at[first + i]))
            self.started.append(False)

    def __setitem__(self, at, value):
        self.buf[at] = value

    def send(self, i=0):
        if not self.started[i]:
            self.started[i] = True
            self.copies[i].start()


class Taken:
    def __init__(self, shape, dtype, pieces=(None,), space=pltpu.VMEM):
        self.shape, self.dtype, self.pieces, self.space = shape, dtype, pieces, space
        self.count = 1 if callable(pieces) else len(pieces)


RAW = "raw"
HBM = pl.BlockSpec(memory_space=pl.ANY)


def call(body, ins, args, outs, flops, name, scratch=()):
    specs = [Taken(arg.shape, arg.dtype) if spec is None else spec for spec, arg in zip(ins, args)]
    taken = [spec for spec in specs if isinstance(spec, Taken)]
    outs = [out if len(out) == 3 else out + ((None,),) for out in outs]
    n_in = sum(spec.count for spec in taken)
    n_out = sum(len(pieces) for _, _, pieces in outs)

    def kernel(*refs):
        in_refs = refs[: len(specs)]
        out_refs = refs[len(specs) : len(specs) + len(outs)]
        rest = refs[len(specs) + len(outs) :]
        in_bufs = rest[: len(taken)]
        out_bufs = rest[len(taken) : len(taken) + len(outs)]
        in_sems, out_sems = rest[len(taken) + len(outs) : len(taken) + len(outs) + 2]
        extra = rest[len(taken) + len(outs) + 2 :]
        operands, sources, first = [], [], 0
        for spec, ref in zip(specs, in_refs):
            if not isinstance(spec, Taken):
                operands.append(ref)
                continue
            pieces = spec.pieces() if callable(spec.pieces) else spec.pieces
            source = Source(ref, in_bufs[len(sources)], in_sems, first, pieces)
            operands.append(source)
            sources.append(source)
            first += spec.count
        for i in range(max(spec.count for spec in taken)):
            for source in sources:
                if i < len(source.copies):
                    source.start(i)
        sinks, first = [], 0
        for (_, _, pieces), ref, buf in zip(outs, out_refs, out_bufs):
            sinks.append(Sink(ref, buf, out_sems, first, pieces))
            first += len(pieces)
        body(*operands, *sinks, *extra)
        for sink in sinks:
            for i in range(len(sink.copies)):
                sink.send(i)
        for source in sources:
            for i in range(len(source.copies)):
                source.wait(i)
        for sink in sinks:
            for copy in sink.copies:
                copy.wait()

    return pl.pallas_call(
        kernel,
        in_specs=[HBM] * len(specs),
        out_specs=[HBM] * len(outs),
        out_shape=[jax.ShapeDtypeStruct(shape, dtype) for shape, dtype, _ in outs],
        scratch_shapes=[spec.space(spec.shape, spec.dtype) for spec in taken]
        + [pltpu.VMEM(shape, dtype) for shape, dtype, _ in outs]
        + [pltpu.SemaphoreType.DMA((n_in,)), pltpu.SemaphoreType.DMA((n_out,))]
        + list(scratch),
        compiler_params=pltpu.CompilerParams(vmem_limit_bytes=VMEM_LIMIT),
        cost_estimate=pl.CostEstimate(flops=flops, bytes_accessed=4 << 20, transcendentals=0),
        name=name,
    )(*args)


def my_columns(width):
    return pl.ds(pl.multiple_of(lax.axis_index("head") * width, 128), width)


def two_terms(row):
    high = row.astype(BF16).astype(F32)
    where_row = iota((16, row.shape[1]), 0)
    return jnp.where(where_row == 0, high, jnp.where(where_row == 1, row - high, 0.0)).astype(BF16)


def slot_of(trow, tcol, axis):
    n = trow.shape[1]
    earlier = (tcol == trow) & (iota((n, n), axis) < iota((n, n), 1 - axis))
    rank = jnp.sum(earlier.astype(jnp.int32), axis=axis, keepdims=True)
    return (trow if axis == 0 else tcol) * 8 + rank


SHIFTS, SCALES, GATING, NEAR, FAR, SOUND = range(6)


def front(clips, drops, mod, tokens, weights, audio, targets, audio_weights,
          kv, hidden, small, u, scale_out, sound_kv, sent):
    rows = tokens.buf.shape[0]
    sound_rows = audio.buf.shape[0]
    position = lax.axis_index("st")
    count = clips.buf.shape[0]
    clip_ref, dropped_ref = clips.wait(), drops.wait()
    clip = clip_ref[position]
    odd = position & 1

    def side_bias(tile):
        inside = (tile >= 0) & (tile < count)
        other = clip_ref[jnp.clip(tile, 0, count - 1)]
        return jnp.where(inside & (other == clip), -LOG4, DEAD)

    near = side_bias(position + 1 - 2 * odd)
    far = side_bias(position - 1 + 2 * odd)
    sound = jnp.where(dropped_ref[clip] == 0, -LOG4, DEAD)
    shifts, scales, gating = [mod[i, pl.ds(clip, 1), :] for i in range(3)]
    at = iota((8, shifts.shape[1]), 0)
    table = jnp.where(at == SHIFTS, shifts, jnp.where(at == SCALES, scales, gating))
    table = jnp.where(at == NEAR, near, jnp.where(at == FAR, far, table))
    small[...] = jnp.where(at == SOUND, sound, table)
    small.send()
    inputs = tokens[...].astype(F32)
    scale = row_scale(inputs)
    both = jnp.concatenate(
        ((inputs * scale * (1.0 + scales) + shifts).astype(BF16), two_terms(shifts)), axis=0
    )
    for i in range(2):
        block = pl.ds(i * rows, rows)
        made = mm(both, weights.wait(i)[i])
        kv[block, :] = made[:rows].astype(BF16)
        u[block, :] = (made[:rows] - (made[rows : rows + 1] + made[rows + 1 : rows + 2])).astype(BF16)
    kv.send()
    u.send()
    hidden[...] = both
    hidden.send()
    sounds = audio[...].astype(F32)
    sound_scale = row_scale(sounds)
    scale_out[pl.ds(0, rows), :] = jnp.broadcast_to(scale, (rows, 128))
    scale_out[pl.ds(rows, sound_rows), :] = jnp.broadcast_to(sound_scale, (sound_rows, 128))
    scale_out.send()
    sound_in = (sounds * sound_scale).astype(BF16)
    trow = targets[...]
    slot = slot_of(trow, to_col(trow), 0)
    slots = sent.shape[0]
    place = iota((slots, sound_rows), 0)
    dispatch = jnp.concatenate((place == slot, place == slot + 4), axis=1).astype(BF16)
    filled = jnp.sum(dispatch.astype(F32), axis=1, keepdims=True)
    pairs = [mm(sound_in, audio_weights.wait(i)[i]).astype(BF16) for i in range(2)]
    pairs = jnp.concatenate(pairs, axis=0)
    sound_kv[...] = pairs
    sound_kv.send()
    made = mm(dispatch, pairs)
    mark = ((iota(made.shape, 0) & 7) < 4) & (iota(made.shape, 1) == 0) & (filled < 0.5)
    sent[...] = jnp.where(mark, EMPTY, made).astype(BF16)


def query_front(hidden, wq, cotangent, small, wo, q, uq, g, gt):
    rows = q.shape[0]
    made = mm(hidden[...], wq[0])
    queries = made[:rows].astype(BF16)
    q[...] = (queries.astype(F32) * (float(HD) ** -0.5)).astype(BF16)
    q.send()
    uq[...] = (made[:rows] - (made[rows : rows + 1] + made[rows + 1 : rows + 2])).astype(BF16)
    uq.send()
    out_grad = (cotangent[...].astype(F32) * small[GATING : GATING + 1, :]).astype(BF16)
    grads = mm(out_grad, wo[...], NT)
    g[...] = grads.astype(BF16)
    g.send()
    gt[...] = grads.T.astype(BF16)


def attention(small, slots_in, q_in, g_in, gt_in, near, own, far,
              at, dq, d_own, d_near, d_far, d_audio, k_all, v_all, bias_ref):
    rows, width = q_in.buf.shape
    slots = slots_in.buf.shape[0]
    half = slots // 2
    table = small[:, 0:128]
    for i, bias in enumerate((table[NEAR : NEAR + 1], None, table[FAR : FAR + 1])):
        bias = jnp.full((1, 128), -LOG4, F32) if bias is None else bias
        bias_ref[pl.ds(i * rows, rows), :] = jnp.broadcast_to(bias, (rows, 128))
    pick_at = (iota((half, slots), 0) >> 2) * 8 + (iota((half, slots), 0) & 3)
    picks = [(iota((half, slots), 1) == pick_at + 4 * i).astype(BF16) for i in range(2)]
    lane = iota((rows, 128), 1)
    sinks = (d_near, d_own, d_far)
    tail = pl.ds(3 * rows, half)
    for pair in range(width // 128):
        cols = slice(pair * 128, (pair + 1) * 128)
        arrived = slots_in.wait(pair)[:, cols]
        k_all[tail, cols] = mm(picks[0], arrived).astype(BF16)
        v_all[tail, cols] = mm(picks[1], arrived).astype(BF16)
        if pair == 0:
            live = k_all[tail, cols].astype(F32)[:, 0:1] < EMPTY * 0.5
            sound = jnp.broadcast_to(table[SOUND : SOUND + 1], (half, 128))
            bias_ref[tail, :] = jnp.where(live, sound, DEAD)
        q_pair = q_in.wait(pair)[:, cols]
        g_pair = g_in.wait(pair)[:, cols]
        gt_pair = gt_in.wait(pair)[cols, :]
        for i, source in enumerate((near, own, far)):
            block = pl.ds(i * rows, rows)
            got = source.wait(pair)
            k_all[block, cols] = got[pl.ds(0, rows), cols]
            v_all[block, cols] = got[pl.ds(rows, rows), cols]
        keys = k_all[:, cols]
        values = v_all[:, cols]
        keys_t = keys.T
        values_t = values.T
        qs, gs, ps, ss = [], [], [], []
        for side in range(2):
            mine = (lane // HD) == side
            half_rows = slice(side * HD, (side + 1) * HD)
            head_rows = slice(pair * 128 + side * HD, pair * 128 + (side + 1) * HD)
            q = jnp.where(mine, q_pair, jnp.zeros_like(q_pair))
            g = jnp.where(mine, g_pair, jnp.zeros_like(g_pair))
            bias = jnp.concatenate([bias_ref[...]] * 2, axis=1)
            weights = jnp.exp(mm(keys, q, NT) + bias)
            inverse = 1.0 / jnp.sum(weights, axis=0, keepdims=True)
            probs = weights * inverse
            rounded = probs.astype(BF16)
            att = mm(values_t[half_rows], rounded).astype(BF16)
            at[head_rows, :] = att
            dots = jnp.sum(att.astype(F32) * gt_pair[half_rows].astype(F32), axis=0, keepdims=True)
            score_grad = (probs * (mm(values, g, NT) - dots)).astype(BF16)
            dq[head_rows, :] = (mm(keys_t[half_rows], score_grad) * (float(HD) ** -0.5)).astype(BF16)
            qs.append(q)
            gs.append(g)
            ps.append(rounded)
            ss.append(score_grad)
        d_keys = mm(jnp.concatenate(ss, axis=1), jnp.concatenate(qs, axis=0))
        d_values = mm(jnp.concatenate(ps, axis=1), jnp.concatenate(gs, axis=0))
        for b, sink in enumerate(sinks):
            block = slice(b * rows, (b + 1) * rows)
            sink[pl.ds(0, rows), cols] = d_keys[block].astype(sink.dtype)
            sink[pl.ds(rows, rows), cols] = d_values[block].astype(sink.dtype)
        d_audio[pl.ds(0, half), cols] = d_keys[3 * rows :].astype(BF16)
        d_audio[pl.ds(half, half), cols] = d_values[3 * rows :].astype(BF16)
        for sink in (at, dq, d_own, d_near, d_far, d_audio):
            sink.send(pair)


def group_block(weights, k, width):
    return weights[:, pl.ds(pl.multiple_of((lax.axis_index("head") ^ k) * width, 128), width)]


def out_first(d_audio, at, wo, d_slots, to_core, keep):
    slots, width = d_slots.shape
    half = slots // 2
    rows = at.buf.shape[1]
    back_row = iota((slots, half), 0)
    back_at = (back_row >> 3) * 4 + (back_row & 3)
    total = jnp.zeros((slots, width), F32)
    for i in range(2):
        put = ((iota((slots, half), 1) == back_at) & ((back_row & 4) == 4 * i)).astype(BF16)
        total = total + mm(put, d_audio[pl.ds(i * half, half), :])
    d_slots[...] = total.astype(BF16)
    d_slots.send()
    attended = at[...].astype(F32).T.astype(BF16)
    for sink, blocks in ((to_core, (1, 3)), (keep, (0, 2))):
        for i, k in enumerate(blocks):
            part = mm(attended, group_block(wo.wait(), k, width))
            sink[pl.ds(i * rows, rows), :] = part.astype(BF16)
        sink.send()


def head_blocks(part_ref, extra, to_core, keep):
    rows = part_ref.shape[0]
    width = to_core.shape[1]
    me = lax.axis_index("head")
    for sink, blocks in ((to_core, (1, 3)), (keep, (0, 2))):
        for i, k in enumerate(blocks):
            cols = pl.ds(pl.multiple_of((me ^ k) * width, 128), width)
            sink[pl.ds(i * (rows + 16), rows), :] = part_ref[:, cols]
            sink[pl.ds(i * (rows + 16) + rows, 16), :] = extra
        sink.send()


def extra_rows(dots, width):
    row = to_row(jnp.sum(dots, axis=1, keepdims=True))
    row = jnp.concatenate((row, jnp.zeros((1, width - row.shape[1]), F32)), axis=1)
    return two_terms(row)


def video_project(dq, d_own, near, far, uq, u, weights, after, to_core, keep, part_ref):
    rows, width = uq.buf.shape
    queries = dq[...].astype(F32).T.astype(BF16)
    pair = (d_own[...].astype(F32) + near[...].astype(F32) + far[...].astype(F32)).astype(BF16)
    grads = (queries, pair[:rows], pair[rows:])
    others = (uq[...], u[pl.ds(0, rows), :], u[pl.ds(rows, rows), :])
    dots = sum(grad.astype(F32) * other.astype(F32) for grad, other in zip(grads, others))
    extra = extra_rows(dots, width)
    part = sum(mm(grad, weights.wait(i)[i], NT) for i, grad in enumerate(grads))
    part_ref[...] = part.astype(BF16)
    head_blocks(part_ref, extra, to_core, keep)


def sound_project(targets, back, sound_kv, audio_weights, to_core, keep, part_ref):
    rows = targets.buf.shape[1]
    width = to_core.shape[1]
    trow = targets[...]
    slot = slot_of(trow, to_col(trow), 1)
    arrived = back[...]
    slots = arrived.shape[0]
    grads = []
    for i in range(2):
        pick = (iota((rows, slots), 1) == slot + 4 * i).astype(BF16)
        grads.append(mm(pick, arrived).astype(BF16))
    others = (sound_kv[pl.ds(0, rows), :], sound_kv[pl.ds(rows, rows), :])
    dots = sum(grad.astype(F32) * other.astype(F32) for grad, other in zip(grads, others))
    extra = extra_rows(dots, width)
    part = sum(mm(grad, audio_weights.wait(i)[i], NT) for i, grad in enumerate(grads))
    part_ref[...] = part.astype(BF16)
    head_blocks(part_ref, extra, to_core, keep)


def pair_sum(*refs):
    cross, mine = refs[-2:]
    first = 0
    for keep, arrived in zip(refs[:-2:2], refs[1:-2:2]):
        tall = keep.buf.shape[0] // 2
        own, other = pl.ds(0, tall), pl.ds(tall, tall)
        block = pl.ds(first, tall)
        total = keep[other, :].astype(F32) + arrived[other, :].astype(F32)
        cross[block, :] = total.astype(BF16)
        if first + tall == mine.shape[0]:
            extra = total[tall - 16 : tall - 15] + total[tall - 15 : tall - 14]
            cross[pl.ds(first + tall - 16, 16), :] = two_terms(extra)
            cross.send()
        mine[block, :] = keep[own, :].astype(F32) + arrived[own, :].astype(F32)
        first += tall


def finish(tokens, audio, cotangent, scale_in, small, mine, cross, sound_mine, sound_cross,
           video_out, video_grad, audio_grad):
    rows, width = video_grad.shape
    sound_rows = audio_grad.shape[0]
    scale = scale_in[...][:, 0:1]

    def mean_of(total, count):
        row = (total[count : count + 1] + total[count + 1 : count + 2])[:, :count]
        return to_col(row * (1.0 / (4 * width)))

    inputs = tokens[...].astype(F32)
    normed = inputs * scale[:rows]
    video = mine[...] + cross[...].astype(F32)
    video_out[...] = (inputs + small[GATING : GATING + 1, :] * video[:rows]).astype(BF16)
    video_out.send()
    video = video[rows:]
    hat = video[:rows] * (1.0 + small[SCALES : SCALES + 1, :]) - normed * mean_of(video, rows)
    video_grad[...] = (cotangent[...].astype(F32) + scale[:rows] * hat).astype(BF16)
    video_grad.send()
    normed = audio[...].astype(F32) * scale[rows:]
    sound = sound_mine[...] + sound_cross[...].astype(F32)
    hat = sound[:sound_rows] - normed * mean_of(sound, sound_rows)
    audio_grad[...] = (scale[rows:] * hat).astype(BF16)


def per_device(
    video_tokens,
    cotangent,
    audio_frames,
    input_weights,
    audio_weights,
    output_weight,
    modulation,
    tile_clip,
    dropped,
    audio_tile,
):
    rows, model = video_tokens.shape
    width = input_weights.shape[2]
    sound_rows = audio_frames.shape[0]
    count = lax.axis_size("st")
    slots = 8 * count
    half = slots // 2
    pairs = width // 128
    targets = audio_tile.T
    modulation = jnp.transpose(modulation, (1, 0, 2))
    columns = [(slice(None), pl.ds(p * 128, 128)) for p in range(pairs)]
    head_rows = [(pl.ds(p * 128, 128), slice(None)) for p in range(pairs)]

    def layers(first, last):
        pieces = [(pl.ds(i, 1), pl.ds(i - first, 1)) for i in range(first, last)]
        return Taken((last - first, model, width), BF16, pieces)

    def own_block(n, dtype=BF16):
        return Taken((n, width), dtype, lambda: [((slice(None), my_columns(width)), slice(None))])

    def scalars(arg):
        return Taken(arg.shape, arg.dtype, space=pltpu.SMEM)

    def split(arg, pieces):
        return Taken(arg.shape, arg.dtype, [(piece, piece) for piece in pieces])

    kv, hidden, small, u, scale, sound_kv, sent = call(
        front,
        (scalars(tile_clip), scalars(dropped), None, None, layers(1, 3), None, None, layers(0, 2)),
        (tile_clip, dropped, modulation, video_tokens, input_weights, audio_frames, targets, audio_weights),
        [
            ((2 * rows, width), BF16),
            ((rows + 16, model), BF16),
            ((8, model), F32),
            ((2 * rows, width), BF16),
            ((rows + sound_rows, 128), F32),
            ((2 * sound_rows, width), BF16),
            ((slots, width), BF16),
        ],
        2 * (rows + sound_rows) * model * 2 * width,
        "front",
    )
    near_swap = [(i, i ^ 1) for i in range(count)]
    far_swap = [p for i in range(1, count - 2, 2) for p in ((i, i + 1), (i + 1, i))]
    near = lax.ppermute(kv, "st", near_swap)
    far = lax.ppermute(kv, "st", far_swap)
    arrived = lax.all_to_all(sent, "st", split_axis=0, concat_axis=0, tiled=True)
    block = ((rows, width), BF16)
    queries, uq, grads, grads_t = call(
        query_front,
        (None, layers(0, 1), None, None, None),
        (hidden, input_weights, cotangent, small, output_weight),
        [block, block, block, ((width, rows), BF16)],
        HEAVY,
        "query_front",
    )
    attended_t, dq_t, d_own, d_near, d_far, d_audio = call(
        attention,
        (None, split(arrived, columns), split(queries, columns), split(grads, columns))
        + (split(grads_t, head_rows),)
        + (split(kv, columns),) * 3,
        (small, arrived, queries, grads, grads_t, near, kv, far),
        [
            ((width, rows), BF16, head_rows),
            ((width, rows), BF16, head_rows),
            ((2 * rows, width), BF16, columns),
            ((2 * rows, width), BF16, columns),
            ((2 * rows, width), BF16, columns),
            ((slots, width), BF16, columns),
        ],
        2 * 6 * rows * (3 * rows + half) * width,
        "attention",
        (
            pltpu.VMEM((3 * rows + half, width), BF16),
            pltpu.VMEM((3 * rows + half, width), BF16),
            pltpu.VMEM((3 * rows + half, 128), F32),
        ),
    )
    back_near = lax.ppermute(d_near, "st", near_swap)
    back_far = lax.ppermute(d_far, "st", far_swap)
    groups = lax.axis_size("head")
    core_swap = [(i, i ^ 1) for i in range(groups)]
    cross_swap = [(i, i ^ 2) for i in range(groups)]
    two = ((2 * rows, width), BF16)
    d_slots, out_to_core, out_keep = call(
        out_first,
        (None, None, None),
        (d_audio, attended_t, output_weight),
        [((slots, width), BF16), two, two],
        HEAVY,
        "out_first",
    )
    back = lax.all_to_all(d_slots, "st", split_axis=0, concat_axis=0, tiled=True)
    out_from_core = lax.ppermute(out_to_core, "head", core_swap)

    def head_sum(body, ins, args, n, cost, name, before=(), above=0):
        both = ((2 * (n + 16), width), BF16)
        scratch = (pltpu.VMEM((n, model), BF16),)
        to_core, keep = call(body, ins, args, [both, both], cost, name, scratch)
        cross, mine = call(
            pair_sum,
            (None,) * (2 + len(before)),
            (*before, keep, lax.ppermute(to_core, "head", core_swap)),
            [((above + n + 16, width), BF16), ((above + n + 16, width), F32)],
            rows * width,
            name + "_sum",
        )
        return mine, lax.ppermute(cross, "head", cross_swap)

    video = head_sum(
        video_project,
        (None,) * 6 + (layers(0, 3), RAW),
        (dq_t, d_own, back_near, back_far, uq, u, input_weights, out_from_core),
        rows,
        HEAVY,
        "video",
        (out_keep, out_from_core),
        rows,
    )
    sound = head_sum(
        sound_project,
        (None,) * 3 + (layers(0, 2),),
        (targets, back, sound_kv, audio_weights),
        sound_rows,
        10**9,
        "sound",
    )
    return call(
        finish,
        (own_block(rows), own_block(sound_rows), own_block(rows), None, own_block(8, F32)) + (None,) * 4,
        (video_tokens, audio_frames, cotangent, scale, small, *video, *sound),
        [((rows, width), BF16), ((rows, width), BF16), ((sound_rows, width), BF16)],
        4 * rows * width,
        "finish",
    )


def solution(mesh):
    return jax.shard_map(
        per_device,
        mesh=mesh,
        in_specs=(
            P("st", None),
            P("st", None),
            P("st", None),
            P(None, None, "head"),
            P(None, None, "head"),
            P("head", None),
            P(),
            P(),
            P(),
            P("st", None),
        ),
        out_specs=(P("st", "head"), P("st", "head"), P("st", "head")),
        check_vma=False,
    )
```

time: 111 us -> 105 us (0.946)
  Pallas kernels: 44.8 us -> 39.5 us
  starting transfers between devices: 39.3 us -> 36.4 us
  waiting for transfers between devices: 23.1 us -> 24.6 us
    pallas_call x10 -> x9, Pallas kernels: 44.8 us -> 39.5 us  [call(): pl.pallas_call(kernel, in_specs=[HBM] * len(specs), out_specs=[HBM] * len...]
    ppermute x1, waiting for transfers between devices: 8.06 us -> 3.72 us  [per_device(): back_near = lax.ppermute(d_near, 'st', near_swap)]
    ppermute x4 -> x5, waiting for transfers between devices: 5.12 us -> 8.21 us  [the longest x2 5.3 us: head_sum(): return (mine, lax.ppermute(cross, 'head', cross_swap))]
    ppermute x1, waiting for transfers between devices: 0.01 us -> 3.04 us  [per_device(): near = lax.ppermute(kv, 'st', near_swap)]
    ppermute x4 -> x5, starting transfers between devices: 10.3 us -> 7.72 us  [the longest x2 3.69 us: head_sum(): lax.ppermute(to_core, 'head', core_swap)]
    all_to_all x1, waiting for transfers between devices: 1.85 us -> 0.01 us  [per_device(): lax.all_to_all(d_slots, 'st', split_axis=0, concat_axis=0, tiled=True)]
    all_to_all x1, waiting for transfers between devices: 8.12 us -> 9.64 us  [per_device(): lax.all_to_all(sent, 'st', split_axis=0, concat_axis=0, tiled=True)]
    unnamed x8 -> x10, local copies, waits for them, and re-layouts: 2.28 us -> 3.03 us
  transfers between devices with their start and end apart: 10 -> 11, of which waited for: 5 -> 6; matrix products, arithmetic and copies ran while one was open for 0% -> 0% of each run, Pallas kernels for 14% -> 19%
where the time goes in v3:
time: 105 us; the launch traced here: 104 us
  Pallas kernels  39.5 us (38%)
  starting transfers between devices  36.4 us (35%)
  waiting for transfers between devices  24.6 us (23%)
  local copies, waits for them, and re-layouts  3.03 us (3%)
    pallas_call x9, Pallas kernels, call(): pl.pallas_call(kernel, in_specs=[HBM] * len(specs), out_specs=[HBM] * len...  39.5 us
    all_to_all x1, starting transfers between devices, per_device(): lax.all_to_all(sent, 'st', split_axis=0, concat_axis=0, tiled=True)  11.8 us
    all_to_all x1, starting transfers between devices, per_device(): lax.all_to_all(d_slots, 'st', split_axis=0, concat_axis=0, tiled=True)  9.67 us
    all_to_all x1, waiting for transfers between devices, per_device(): lax.all_to_all(sent, 'st', split_axis=0, concat_axis=0, tiled=True)  9.64 us
    ppermute x2, waiting for transfers between devices, head_sum(): return (mine, lax.ppermute(cross, 'head', cross_swap))  5.3 us
    ppermute x1, starting transfers between devices, per_device(): near = lax.ppermute(kv, 'st', near_swap)  4.25 us
    ppermute x1, waiting for transfers between devices, per_device(): back_near = lax.ppermute(d_near, 'st', near_swap)  3.72 us
    ppermute x2, starting transfers between devices, head_sum(): lax.ppermute(to_core, 'head', core_swap)  3.69 us
  transfers between devices with their start and end apart: 11, of which 6 were waited for; matrix products, arithmetic and copies ran while one was open for 0% of the time, Pallas kernels for 19%

profile of v3, /device:TPU:1, one launch (start us, length us, event | category | flops | bytes accessed | tf_op | source)
XLA Modules:
  0.0 104.4 jit_solution(4558636053990727611)
XLA Ops:
  0.6 5.5 %front.1 = (bf16[512,384]{1,0:T(8,128)(2,1)}, bf16[272,1536]{1,0:T(8,128)(2,1)}, f32[8,1536]{1,0:T(8,128)}, bf16[512,384]{1,0:T(8,128)(2,1)}, f32[384,128]{1,0:T...) custom-call(s32[64]{0:T(128)} %refs_0_.2, s32[4]{0:T(128)} %refs_1_.3, f32[3,4,1536]{2,1,0:T(4,128)} %bitcast.8, ...), custom_call_target="tpu_custom_call" | custom-call | flops 905969664 | bytes 4194304 | tf_op jit(solution)/shard_map/front/pallas_call | solution.py:145
  6.1 1.4 %collective-permute-start.1 = (bf16[512,384]{1,0:T(8,128)(2,1)}, bf16[512,384]{1,0:T(8,128)(2,1)}, u32[]{:S(2)}, u32[]{:S(2)}) collective-permute-start(bf16[512,384]{1,0:T(8,128)(2,1)} %get-tuple-element.38.refs_6_), channel_id=1, source_target_pairs={{4,8},{8,4},{12,16},{16,12},{20,24},{24,20},{28,32},{32,28},{36,40... | collective-permute-start | bytes 1179656 | tf_op jit(solution)/shard_map/ppermute | solution.py:494
  7.5 4.2 %collective-permute-start = (bf16[512,384]{1,0:T(8,128)(2,1)}, bf16[512,384]{1,0:T(8,128)(2,1)}, u32[]{:S(2)}, u32[]{:S(2)}) collective-permute-start(bf16[512,384]{1,0:T(8,128)(2,1)} %get-tuple-element.38.refs_6_), channel_id=1, source_target_pairs={{0,4},{4,0},{8,12},{12,8},{16,20},{20,16},{24,28},{28,24},{32,36},... | collective-permute-start | bytes 1179656 | tf_op jit(solution)/shard_map/ppermute | solution.py:493
  11.8 11.8 %all-to-all-start = ((bf16[64,8,384]{2,1,0:T(8,128)(2,1)}), bf16[64,8,384]{2,1,0:T(8,128)(2,1)}, u32[]{:S(2)}, u32[]{:S(2)}) async-start(bf16[64,8,384]{2,1,0:T(8,128)(2,1)} %bitcast.7), calls=%async_computation | async-start | bytes 786432 | tf_op jit(solution)/shard_map/all_to_all | solution.py:495
  23.6 3.9 %query_front.1 = (bf16[256,384]{1,0:T(8,128)(2,1)}, bf16[256,384]{1,0:T(8,128)(2,1)}, bf16[256,384]{1,0:T(8,128)(2,1)}, bf16[384,256]{1,0:T(8,128)(2,1)}) custom-call(bf16[272,1536]{1,0:T(8,128)(2,1)} %get-tuple-element.34.refs_0_, bf16[3,1536,384]{2,1,0:T(8,128)(2,1)} %refs_6_.1, bf16[256,1536]{1,0:T(8,128)(2,1)} %refs_2_.5, ...), custom_call_target="tpu_custom_call" | custom-call | flops 9999999827968 | bytes 4194304 | tf_op jit(solution)/shard_map/query_front/pallas_call | solution.py:145
  27.5 3.0 %collective-permute-done.refs_5_ = bf16[512,384]{1,0:T(8,128)(2,1)} collective-permute-done((bf16[512,384]{1,0:T(8,128)(2,1)}, bf16[512,384]{1,0:T(8,128)(2,1)}, u32[]{:S(2)}, u32[]{:S(2)}) %collective-permute-start) | collective-permute-done | bytes 393248 | tf_op jit(solution)/shard_map/ppermute | solution.py:493
  30.6 9.6 %all-to-all-done = bf16[64,8,384]{2,1,0:T(8,128)(2,1)} async-done(((bf16[64,8,384]{2,1,0:T(8,128)(2,1)}), bf16[64,8,384]{2,1,0:T(8,128)(2,1)}, u32[]{:S(2)}, u32[]{:S(2)}) %all-to-all-start) | async-done | bytes 393248 | tf_op jit(solution)/shard_map/all_to_all | solution.py:495
  40.2 11.5 %attention.1 = (bf16[384,256]{1,0:T(8,128)(2,1)}, bf16[384,256]{1,0:T(8,128)(2,1)}, bf16[512,384]{1,0:T(8,128)(2,1)}, bf16[512,384]{1,0:T(8,128)(2,1)}, bf16[512...) custom-call(f32[8,1536]{1,0:T(8,128)} %get-tuple-element.32.refs_3_.refs_0_.refs_4_, bf16[512,384]{1,0:T(8,128)(2,1)} %bitcast.3.refs_1_, ...), custom_call_target="tpu_custom_call" | custom-call | flops 1207959552 | bytes 4194304 | tf_op jit(solution)/shard_map/attention/pallas_call | solution.py:145
  51.7 0.1 collective-permute-start.3
  51.8 1.4 %collective-permute-start.4 = (bf16[512,384]{1,0:T(8,128)(2,1)}, bf16[512,384]{1,0:T(8,128)(2,1)}, u32[]{:S(2)}, u32[]{:S(2)}) collective-permute-start(bf16[512,384]{1,0:T(8,128)(2,1)} %get-tuple-element.46), channel_id=1, source_target_pairs={{4,8},{8,4},{12,16},{16,12},{20,24},{24,20},{28,32},{32,28},{36,40... | collective-permute-start | bytes 1179656 | tf_op jit(solution)/shard_map/ppermute | solution.py:528
  53.2 3.0 %out_first.1 = (bf16[512,384]{1,0:T(8,128)(2,1)}, bf16[512,384]{1,0:T(8,128)(2,1)}, bf16[512,384]{1,0:T(8,128)(2,1)}) custom-call(bf16[512,384]{1,0:T(8,128)(2,1)} %get-tuple-element.39.refs_0_, bf16[384,256]{1,0:T(8,128)(2,1)} %get-tuple-element.40.refs_1_, bf16[384,1536]{1,0:T(8,128)(2,1)} %refs_2_.4), custom_call_target="tpu_custom_call" | custom-call | flops 9999999827968 | bytes 4194304 | tf_op jit(solution)/shard_map/out_first/pallas_call | solution.py:145
  56.2 0.9 collective-permute-start.2
  57.1 9.7 %all-to-all-start.1 = ((bf16[64,8,384]{2,1,0:T(8,128)(2,1)}), bf16[64,8,384]{2,1,0:T(8,128)(2,1)}, u32[]{:S(2)}, u32[]{:S(2)}) async-start(bf16[64,8,384]{2,1,0:T(8,128)(2,1)} %bitcast.6), calls=%async_computation.1 | async-start | bytes 786432 | tf_op jit(solution)/shard_map/all_to_all | solution.py:541
  66.8 3.7 %collective-permute-done.3.refs_2_ = bf16[512,384]{1,0:T(8,128)(2,1)} collective-permute-done((bf16[512,384]{1,0:T(8,128)(2,1)}, bf16[512,384]{1,0:T(8,128)(2,1)}, u32[]{:S(2)}, u32[]{:S(2)}) %collective-permute-start.3) | collective-permute-done | bytes 393248 | tf_op jit(solution)/shard_map/ppermute | solution.py:527
  70.5 0.0 collective-permute-done.2.refs_7_.refs_1_
  70.5 0.8 copy-done.2
  71.3 4.8 %video.1 = (bf16[544,384]{1,0:T(8,128)(2,1)}, bf16[544,384]{1,0:T(8,128)(2,1)}) custom-call(bf16[384,256]{1,0:T(8,128)(2,1)} %get-tuple-element.43.refs_0_, bf16[512,384]{1,0:T(8,128)(2,1)} %get-tuple-element.44.refs_1_, bf16[512,384]{1,0:T(8,128)(2,1)} %collective-permute-done.3.refs_2_, bf16[512,384]{1,0:T(8,128)(2,1)} %collective-permute-done.4.refs_3_, ...), custom_call_target="tpu_custom_call" | custom-call | flops 9999999827968 | bytes 4194304 | tf_op jit(solution)/shard_map/video/pallas_call | solution.py:145
  76.1 3.0 %collective-permute-start.5 = (bf16[544,384]{1,0:T(8,128)(2,1)}, bf16[544,384]{1,0:T(8,128)(2,1)S(1)}, u32[]{:S(2)}, u32[]{:S(2)}) collective-permute-start(bf16[544,384]{1,0:T(8,128)(2,1)} %get-tuple-element.50), channel_id=1, source_target_pairs={{0,1},{1,0},{2,3},{3,2},{4,5},{5,4},{6,7},{7,6},{8,9},{9,8},{10,11... | collective-permute-start | bytes 1253384 | tf_op jit(solution)/shard_map/ppermute | solution.py:551
  79.1 1.6 %collective-permute-done.5.refs_3_ = bf16[544,384]{1,0:T(8,128)(2,1)S(1)} collective-permute-done((bf16[544,384]{1,0:T(8,128)(2,1)}, bf16[544,384]{1,0:T(8,128)(2,1)S(1)}, u32[]{:S(2)}, u32[]{:S(2)}) %collective-permute-start.5) | collective-permute-done | bytes 417824 | tf_op jit(solution)/shard_map/ppermute | solution.py:551
  80.7 0.8 copy-done
  81.4 2.5 %video_sum.1 = (bf16[528,384]{1,0:T(8,128)(2,1)}, f32[528,384]{1,0:T(8,128)}) custom-call(bf16[512,384]{1,0:T(8,128)(2,1)} %get-tuple-element.41.refs_0_, bf16[512,384]{1,0:T(8,128)(2,1)} %copy-done.2, bf16[544,384]{1,0:T(8,128)(2,1)} %get-tuple-element.49.refs_2_, bf16[544,384]{1,0:T(8,128)(2,1)} %copy-done), custom_call_target="tpu_custom_call" | custom-call | flops 98304 | bytes 4194304 | tf_op jit(solution)/shard_map/video_sum/pallas_call | solution.py:145
  83.9 2.4 %collective-permute-start.6 = (bf16[528,384]{1,0:T(8,128)(2,1)}, bf16[528,384]{1,0:T(8,128)(2,1)S(1)}, u32[]{:S(2)}, u32[]{:S(2)}) collective-permute-start(bf16[528,384]{1,0:T(8,128)(2,1)} %get-tuple-element.52), channel_id=1, source_target_pairs={{0,2},{1,3},{2,0},{3,1},{4,6},{5,7},{6,4},{7,5},{8,10},{9,11},{10,... | collective-permute-start | bytes 1216520 | tf_op jit(solution)/shard_map/ppermute | solution.py:556
  86.3 3.6 %sound.1 = (bf16[288,384]{1,0:T(8,128)(2,1)}, bf16[288,384]{1,0:T(8,128)(2,1)}) custom-call(s32[1,128]{1,0:T(1,128)} %bitcast.10, bf16[512,384]{1,0:T(8,128)(2,1)} %bitcast.5.refs_1_, bf16[256,384]{1,0:T(8,128)(2,1)} %get-tuple-element.54.refs_2_, bf16[2,1536,384]{2,1,0:T(8,128)(2,1)} %refs_3_.3), custom_call_target="tpu_custom_call" | custom-call | flops 1000000000 | bytes 4194304 | tf_op jit(solution)/shard_map/sound/pallas_call | solution.py:145
  89.9 0.7 collective-permute-start.7
  90.6 1.3 %collective-permute-done.7.refs_1_ = bf16[288,384]{1,0:T(8,128)(2,1)S(1)} collective-permute-done((bf16[288,384]{1,0:T(8,128)(2,1)}, bf16[288,384]{1,0:T(8,128)(2,1)S(1)}, u32[]{:S(2)}, u32[]{:S(2)}) %collective-permute-start.7) | collective-permute-done | bytes 221216 | tf_op jit(solution)/shard_map/ppermute | solution.py:551
  91.9 0.7 copy-done.3
  92.6 1.8 %sound_sum.1 = (bf16[144,384]{1,0:T(8,128)(2,1)}, f32[144,384]{1,0:T(8,128)}) custom-call(bf16[288,384]{1,0:T(8,128)(2,1)} %get-tuple-element.55.refs_0_, bf16[288,384]{1,0:T(8,128)(2,1)} %copy-done.3), custom_call_target="tpu_custom_call" | custom-call | flops 98304 | bytes 4194304 | tf_op jit(solution)/shard_map/sound_sum/pallas_call | solution.py:145
  94.5 0.8 collective-permute-start.8
  95.3 5.3 %collective-permute-done.8.refs_8_ = bf16[144,384]{1,0:T(8,128)(2,1)S(1)} collective-permute-done((bf16[144,384]{1,0:T(8,128)(2,1)}, bf16[144,384]{1,0:T(8,128)(2,1)S(1)}, u32[]{:S(2)}, u32[]{:S(2)}) %collective-permute-start.8) | collective-permute-done | bytes 110624 | tf_op jit(solution)/shard_map/ppermute | solution.py:556
  100.6 0.6 copy-done.4
  101.2 0.2 copy-done.1
  101.4 2.9 %finish.1 = (bf16[256,384]{1,0:T(8,128)(2,1)}, bf16[256,384]{1,0:T(8,128)(2,1)}, bf16[128,384]{1,0:T(8,128)(2,1)}) custom-call(bf16[256,1536]{1,0:T(8,128)(2,1)} %refs_0_.3, bf16[128,1536]{1,0:T(8,128)(2,1)} %refs_1_.5, bf16[256,1536]{1,0:T(8,128)(2,1)} %refs_2_.5, f32[384,128]{1,0:T(8,128)} %get-tuple-element.31.refs_3_, ...), custom_call_target="tpu_custom_call" | custom-call | flops 393216 | bytes 4194304 | tf_op jit(solution)/shard_map/finish/pallas_call | solution.py:145
  (9 shorter events, 0.0 us)
Async XLA Ops:
  6.1 21.4 %collective-permute-start.1 = (bf16[512,384]{1,0:T(8,128)(2,1)}, bf16[512,384]{1,0:T(8,128)(2,1)}, u32[]{:S(2)}, u32[]{:S(2)}) collective-permute-start(bf16[512,384]{1,0:T(8,128)(2,1)} %get-tuple-element.38.refs_6_), channel_id=1, source_target_pairs={{4,8},{8,4},{12,16},{16,12},{20,24},{24,20},{28,32},{32,28},{36,40... | collective-permute-start | bytes 1179656 | tf_op jit(solution)/shard_map/ppermute | solution.py:494
  7.5 23.1 %collective-permute-start = (bf16[512,384]{1,0:T(8,128)(2,1)}, bf16[512,384]{1,0:T(8,128)(2,1)}, u32[]{:S(2)}, u32[]{:S(2)}) collective-permute-start(bf16[512,384]{1,0:T(8,128)(2,1)} %get-tuple-element.38.refs_6_), channel_id=1, source_target_pairs={{0,4},{4,0},{8,12},{12,8},{16,20},{20,16},{24,28},{28,24},{32,36},... | collective-permute-start | bytes 1179656 | tf_op jit(solution)/shard_map/ppermute | solution.py:493
  11.8 28.4 %all-to-all-start = ((bf16[64,8,384]{2,1,0:T(8,128)(2,1)}), bf16[64,8,384]{2,1,0:T(8,128)(2,1)}, u32[]{:S(2)}, u32[]{:S(2)}) async-start(bf16[64,8,384]{2,1,0:T(8,128)(2,1)} %bitcast.7), calls=%async_computation | async-start | bytes 786432 | tf_op jit(solution)/shard_map/all_to_all | solution.py:495
  51.7 18.8 %collective-permute-start.3 = (bf16[512,384]{1,0:T(8,128)(2,1)}, bf16[512,384]{1,0:T(8,128)(2,1)}, u32[]{:S(2)}, u32[]{:S(2)}) collective-permute-start(bf16[512,384]{1,0:T(8,128)(2,1)} %get-tuple-element.45), channel_id=1, source_target_pairs={{0,4},{4,0},{8,12},{12,8},{16,20},{20,16},{24,28},{28,24},{32,36},... | collective-permute-start | bytes 1179656 | tf_op jit(solution)/shard_map/ppermute | solution.py:527
  51.8 18.7 %collective-permute-start.4 = (bf16[512,384]{1,0:T(8,128)(2,1)}, bf16[512,384]{1,0:T(8,128)(2,1)}, u32[]{:S(2)}, u32[]{:S(2)}) collective-permute-start(bf16[512,384]{1,0:T(8,128)(2,1)} %get-tuple-element.46), channel_id=1, source_target_pairs={{4,8},{8,4},{12,16},{16,12},{20,24},{24,20},{28,32},{32,28},{36,40... | collective-permute-start | bytes 1179656 | tf_op jit(solution)/shard_map/ppermute | solution.py:528
  56.2 14.3 %collective-permute-start.2 = (bf16[512,384]{1,0:T(8,128)(2,1)}, bf16[512,384]{1,0:T(8,128)(2,1)S(1)}, u32[]{:S(2)}, u32[]{:S(2)}) collective-permute-start(bf16[512,384]{1,0:T(8,128)(2,1)} %get-tuple-element.42), channel_id=1, source_target_pairs={{0,1},{1,0},{2,3},{3,2},{4,5},{5,4},{6,7},{7,6},{8,9},{9,8},{10,11... | collective-permute-start | bytes 1179656 | tf_op jit(solution)/shard_map/ppermute | solution.py:542
  57.1 29.2 %all-to-all-start.1 = ((bf16[64,8,384]{2,1,0:T(8,128)(2,1)}), bf16[64,8,384]{2,1,0:T(8,128)(2,1)}, u32[]{:S(2)}, u32[]{:S(2)}) async-start(bf16[64,8,384]{2,1,0:T(8,128)(2,1)} %bitcast.6), calls=%async_computation.1 | async-start | bytes 786432 | tf_op jit(solution)/shard_map/all_to_all | solution.py:541
  70.5 0.8 copy-start.2
  76.1 4.5 %collective-permute-start.5 = (bf16[544,384]{1,0:T(8,128)(2,1)}, bf16[544,384]{1,0:T(8,128)(2,1)S(1)}, u32[]{:S(2)}, u32[]{:S(2)}) collective-permute-start(bf16[544,384]{1,0:T(8,128)(2,1)} %get-tuple-element.50), channel_id=1, source_target_pairs={{0,1},{1,0},{2,3},{3,2},{4,5},{5,4},{6,7},{7,6},{8,9},{9,8},{10,11... | collective-permute-start | bytes 1253384 | tf_op jit(solution)/shard_map/ppermute | solution.py:551
  80.7 0.8 copy-start
  83.9 16.6 %collective-permute-start.6 = (bf16[528,384]{1,0:T(8,128)(2,1)}, bf16[528,384]{1,0:T(8,128)(2,1)S(1)}, u32[]{:S(2)}, u32[]{:S(2)}) collective-permute-start(bf16[528,384]{1,0:T(8,128)(2,1)} %get-tuple-element.52), channel_id=1, source_target_pairs={{0,2},{1,3},{2,0},{3,1},{4,6},{5,7},{6,4},{7,5},{8,10},{9,11},{10,... | collective-permute-start | bytes 1216520 | tf_op jit(solution)/shard_map/ppermute | solution.py:556
  89.9 2.1 %collective-permute-start.7 = (bf16[288,384]{1,0:T(8,128)(2,1)}, bf16[288,384]{1,0:T(8,128)(2,1)S(1)}, u32[]{:S(2)}, u32[]{:S(2)}) collective-permute-start(bf16[288,384]{1,0:T(8,128)(2,1)} %get-tuple-element.56), channel_id=1, source_target_pairs={{0,1},{1,0},{2,3},{3,2},{4,5},{5,4},{6,7},{7,6},{8,9},{9,8},{10,11... | collective-permute-start | bytes 663560 | tf_op jit(solution)/shard_map/ppermute | solution.py:551
  91.9 0.7 copy-start.3
  94.5 6.1 %collective-permute-start.8 = (bf16[144,384]{1,0:T(8,128)(2,1)}, bf16[144,384]{1,0:T(8,128)(2,1)S(1)}, u32[]{:S(2)}, u32[]{:S(2)}) collective-permute-start(bf16[144,384]{1,0:T(8,128)(2,1)} %get-tuple-element.58), channel_id=1, source_target_pairs={{0,2},{1,3},{2,0},{3,1},{4,6},{5,7},{6,4},{7,5},{8,10},{9,11},{10,... | collective-permute-start | bytes 331784 | tf_op jit(solution)/shard_map/ppermute | solution.py:556
  100.5 0.6 copy-start.4
  100.6 0.8 copy-start.1

commit v4 on v3

--- a/solution.py
+++ b/solution.py
@@ -265,6 +265,7 @@
     lane = iota((rows, 128), 1)
     sinks = (d_near, d_own, d_far)
     tail = pl.ds(3 * rows, half)
+    saved = []
     for pair in range(width // 128):
         cols = slice(pair * 128, (pair + 1) * 128)
         arrived = slots_in.wait(pair)[:, cols]
@@ -287,26 +288,34 @@
         keys_t = keys.T
         values_t = values.T
         qs, gs, ps, ss = [], [], [], []
+        bias = jnp.concatenate([bias_ref[...]] * 2, axis=1)
         for side in range(2):
             mine = (lane // HD) == side
+            qs.append(jnp.where(mine, q_pair, jnp.zeros_like(q_pair)))
+            gs.append(jnp.where(mine, g_pair, jnp.zeros_like(g_pair)))
+        scores = mm(keys, jnp.concatenate(qs, axis=0), NT)
+        scores = [scores[:, :rows], scores[:, rows:]]
+        grads = mm(values, jnp.concatenate(gs, axis=0), NT)
+        grads = [grads[:, :rows], grads[:, rows:]]
+        probs = []
+        for side in range(2):
+            weights = jnp.exp(scores[side] + bias)
+            probs.append(weights * (1.0 / jnp.sum(weights, axis=0, keepdims=True)))
+            ps.append(probs[side].astype(BF16))
+        atts = [mm(values_t[i * HD : (i + 1) * HD], ps[i]).astype(BF16) for i in range(2)]
+        saved.append((cols, keys, values, keys_t, qs, gs, ps, ss, probs, grads, atts, gt_pair))
+    for pair, (cols, keys, values, keys_t, qs, gs, ps, ss, probs, grads, atts, gt_pair) in enumerate(saved):
+        for side in range(2):
             half_rows = slice(side * HD, (side + 1) * HD)
             head_rows = slice(pair * 128 + side * HD, pair * 128 + (side + 1) * HD)
-            q = jnp.where(mine, q_pair, jnp.zeros_like(q_pair))
-            g = jnp.where(mine, g_pair, jnp.zeros_like(g_pair))
-            bias = jnp.concatenate([bias_ref[...]] * 2, axis=1)
-            weights = jnp.exp(mm(keys, q, NT) + bias)
-            inverse = 1.0 / jnp.sum(weights, axis=0, keepdims=True)
-            probs = weights * inverse
-            rounded = probs.astype(BF16)
-            att = mm(values_t[half_rows], rounded).astype(BF16)
-            at[head_rows, :] = att
-            dots = jnp.sum(att.astype(F32) * gt_pair[half_rows].astype(F32), axis=0, keepdims=True)
-            score_grad = (probs * (mm(values, g, NT) - dots)).astype(BF16)
-            dq[head_rows, :] = (mm(keys_t[half_rows], score_grad) * (float(HD) ** -0.5)).astype(BF16)
-            qs.append(q)
-            gs.append(g)
-            ps.append(rounded)
-            ss.append(score_grad)
+            at[head_rows, :] = atts[side]
+            dots = jnp.sum(atts[side].astype(F32) * gt_pair[half_rows].astype(F32), axis=0, keepdims=True)
+            ss.append((probs[side] * (grads[side] - dots)).astype(BF16))
+        for side in range(2):
+            half_rows = slice(side * HD, (side + 1) * HD)
+            head_rows = slice(pair * 128 + side * HD, pair * 128 + (side + 1) * HD)
+            dqs = mm(keys_t[half_rows], ss[side]) * (float(HD) ** -0.5)
+            dq[head_rows, :] = dqs.astype(BF16)
         d_keys = mm(jnp.concatenate(ss, axis=1), jnp.concatenate(qs, axis=0))
         d_values = mm(jnp.concatenate(ps, axis=1), jnp.concatenate(gs, axis=0))
         for b, sink in enumerate(sinks):

time: 105 us -> 102 us (0.971)
  Pallas kernels: 39.5 us -> 36.9 us
    pallas_call x9, Pallas kernels: 39.5 us -> 36.9 us  [call(): pl.pallas_call(kernel, in_specs=[HBM] * len(specs), out_specs=[HBM] * len...]
where the time goes in v4:
time: 102 us
  Pallas kernels  36.9 us (36%)
  starting transfers between devices  36.2 us (35%)
  waiting for transfers between devices  24.8 us (24%)
  local copies, waits for them, and re-layouts  3.03 us (3%)
    pallas_call x9, Pallas kernels, call(): pl.pallas_call(kernel, in_specs=[HBM] * len(specs), out_specs=[HBM] * len...  36.9 us
    all_to_all x1, starting transfers between devices, per_device(): lax.all_to_all(sent, 'st', split_axis=0, concat_axis=0, tiled=True)  11.6 us
    all_to_all x1, starting transfers between devices, per_device(): lax.all_to_all(d_slots, 'st', split_axis=0, concat_axis=0, tiled=True)  9.85 us
    all_to_all x1, waiting for transfers between devices, per_device(): lax.all_to_all(sent, 'st', split_axis=0, concat_axis=0, tiled=True)  9.64 us
    ppermute x2, waiting for transfers between devices, head_sum(): return (mine, lax.ppermute(cross, 'head', cross_swap))  5.48 us
    ppermute x1, starting transfers between devices, per_device(): near = lax.ppermute(kv, 'st', near_swap)  4.25 us
    ppermute x2, starting transfers between devices, head_sum(): lax.ppermute(to_core, 'head', core_swap)  3.55 us
    ppermute x1, waiting for transfers between devices, per_device(): back_near = lax.ppermute(d_near, 'st', near_swap)  3.48 us
  transfers between devices with their start and end apart: 11, of which 6 were waited for; matrix products, arithmetic and copies ran while one was open for 0% of the time, Pallas kernels for 19%

profile of v4, /device:TPU:1, one launch (start us, length us, event | category | flops | bytes accessed | tf_op | source)
XLA Modules:
  0.0 101.7 jit_solution(10982789314617511899)
XLA Ops:
  0.6 5.5 %front.1 = (bf16[512,384]{1,0:T(8,128)(2,1)}, bf16[272,1536]{1,0:T(8,128)(2,1)}, f32[8,1536]{1,0:T(8,128)}, bf16[512,384]{1,0:T(8,128)(2,1)}, f32[384,128]{1,0:T...) custom-call(s32[64]{0:T(128)} %refs_0_.2, s32[4]{0:T(128)} %refs_1_.3, f32[3,4,1536]{2,1,0:T(4,128)} %bitcast.8, ...), custom_call_target="tpu_custom_call" | custom-call | flops 905969664 | bytes 4194304 | tf_op jit(solution)/shard_map/front/pallas_call | solution.py:145
  6.1 1.4 %collective-permute-start.1 = (bf16[512,384]{1,0:T(8,128)(2,1)}, bf16[512,384]{1,0:T(8,128)(2,1)}, u32[]{:S(2)}, u32[]{:S(2)}) collective-permute-start(bf16[512,384]{1,0:T(8,128)(2,1)} %get-tuple-element.38.refs_6_), channel_id=1, source_target_pairs={{4,8},{8,4},{12,16},{16,12},{20,24},{24,20},{28,32},{32,28},{36,40... | collective-permute-start | bytes 1179656 | tf_op jit(solution)/shard_map/ppermute | solution.py:503
  7.5 4.2 %collective-permute-start = (bf16[512,384]{1,0:T(8,128)(2,1)}, bf16[512,384]{1,0:T(8,128)(2,1)}, u32[]{:S(2)}, u32[]{:S(2)}) collective-permute-start(bf16[512,384]{1,0:T(8,128)(2,1)} %get-tuple-element.38.refs_6_), channel_id=1, source_target_pairs={{0,4},{4,0},{8,12},{12,8},{16,20},{20,16},{24,28},{28,24},{32,36},... | collective-permute-start | bytes 1179656 | tf_op jit(solution)/shard_map/ppermute | solution.py:502
  11.8 11.6 %all-to-all-start = ((bf16[64,8,384]{2,1,0:T(8,128)(2,1)}), bf16[64,8,384]{2,1,0:T(8,128)(2,1)}, u32[]{:S(2)}, u32[]{:S(2)}) async-start(bf16[64,8,384]{2,1,0:T(8,128)(2,1)} %bitcast.7), calls=%async_computation | async-start | bytes 786432 | tf_op jit(solution)/shard_map/all_to_all | solution.py:504
  23.4 3.9 %query_front.1 = (bf16[256,384]{1,0:T(8,128)(2,1)}, bf16[256,384]{1,0:T(8,128)(2,1)}, bf16[256,384]{1,0:T(8,128)(2,1)}, bf16[384,256]{1,0:T(8,128)(2,1)}) custom-call(bf16[272,1536]{1,0:T(8,128)(2,1)} %get-tuple-element.34.refs_0_, bf16[3,1536,384]{2,1,0:T(8,128)(2,1)} %refs_6_.1, bf16[256,1536]{1,0:T(8,128)(2,1)} %refs_2_.5, ...), custom_call_target="tpu_custom_call" | custom-call | flops 9999999827968 | bytes 4194304 | tf_op jit(solution)/shard_map/query_front/pallas_call | solution.py:145
  27.4 3.2 %collective-permute-done.refs_5_ = bf16[512,384]{1,0:T(8,128)(2,1)} collective-permute-done((bf16[512,384]{1,0:T(8,128)(2,1)}, bf16[512,384]{1,0:T(8,128)(2,1)}, u32[]{:S(2)}, u32[]{:S(2)}) %collective-permute-start) | collective-permute-done | bytes 393248 | tf_op jit(solution)/shard_map/ppermute | solution.py:502
  30.6 9.6 %all-to-all-done = bf16[64,8,384]{2,1,0:T(8,128)(2,1)} async-done(((bf16[64,8,384]{2,1,0:T(8,128)(2,1)}), bf16[64,8,384]{2,1,0:T(8,128)(2,1)}, u32[]{:S(2)}, u32[]{:S(2)}) %all-to-all-start) | async-done | bytes 393248 | tf_op jit(solution)/shard_map/all_to_all | solution.py:504
  40.2 8.9 %attention.1 = (bf16[384,256]{1,0:T(8,128)(2,1)}, bf16[384,256]{1,0:T(8,128)(2,1)}, bf16[512,384]{1,0:T(8,128)(2,1)}, bf16[512,384]{1,0:T(8,128)(2,1)}, bf16[512...) custom-call(f32[8,1536]{1,0:T(8,128)} %get-tuple-element.32.refs_3_.refs_0_.refs_4_, bf16[512,384]{1,0:T(8,128)(2,1)} %bitcast.3.refs_1_, ...), custom_call_target="tpu_custom_call" | custom-call | flops 1207959552 | bytes 4194304 | tf_op jit(solution)/shard_map/attention/pallas_call | solution.py:145
  49.1 0.1 collective-permute-start.3
  49.2 1.4 %collective-permute-start.4 = (bf16[512,384]{1,0:T(8,128)(2,1)}, bf16[512,384]{1,0:T(8,128)(2,1)}, u32[]{:S(2)}, u32[]{:S(2)}) collective-permute-start(bf16[512,384]{1,0:T(8,128)(2,1)} %get-tuple-element.46), channel_id=1, source_target_pairs={{4,8},{8,4},{12,16},{16,12},{20,24},{24,20},{28,32},{32,28},{36,40... | collective-permute-start | bytes 1179656 | tf_op jit(solution)/shard_map/ppermute | solution.py:537
  50.6 3.0 %out_first.1 = (bf16[512,384]{1,0:T(8,128)(2,1)}, bf16[512,384]{1,0:T(8,128)(2,1)}, bf16[512,384]{1,0:T(8,128)(2,1)}) custom-call(bf16[512,384]{1,0:T(8,128)(2,1)} %get-tuple-element.39.refs_0_, bf16[384,256]{1,0:T(8,128)(2,1)} %get-tuple-element.40.refs_1_, bf16[384,1536]{1,0:T(8,128)(2,1)} %refs_2_.4), custom_call_target="tpu_custom_call" | custom-call | flops 9999999827968 | bytes 4194304 | tf_op jit(solution)/shard_map/out_first/pallas_call | solution.py:145
  53.6 0.9 collective-permute-start.2
  54.5 9.8 %all-to-all-start.1 = ((bf16[64,8,384]{2,1,0:T(8,128)(2,1)}), bf16[64,8,384]{2,1,0:T(8,128)(2,1)}, u32[]{:S(2)}, u32[]{:S(2)}) async-start(bf16[64,8,384]{2,1,0:T(8,128)(2,1)} %bitcast.6), calls=%async_computation.1 | async-start | bytes 786432 | tf_op jit(solution)/shard_map/all_to_all | solution.py:550
  64.3 3.5 %collective-permute-done.3.refs_2_ = bf16[512,384]{1,0:T(8,128)(2,1)} collective-permute-done((bf16[512,384]{1,0:T(8,128)(2,1)}, bf16[512,384]{1,0:T(8,128)(2,1)}, u32[]{:S(2)}, u32[]{:S(2)}) %collective-permute-start.3) | collective-permute-done | bytes 393248 | tf_op jit(solution)/shard_map/ppermute | solution.py:536
  67.8 0.0 collective-permute-done.4.refs_3_
  67.8 0.8 copy-done.2
  68.6 4.8 %video.1 = (bf16[544,384]{1,0:T(8,128)(2,1)}, bf16[544,384]{1,0:T(8,128)(2,1)}) custom-call(bf16[384,256]{1,0:T(8,128)(2,1)} %get-tuple-element.43.refs_0_, bf16[512,384]{1,0:T(8,128)(2,1)} %get-tuple-element.44.refs_1_, bf16[512,384]{1,0:T(8,128)(2,1)} %collective-permute-done.3.refs_2_, bf16[512,384]{1,0:T(8,128)(2,1)} %collective-permute-done.4.refs_3_, ...), custom_call_target="tpu_custom_call" | custom-call | flops 9999999827968 | bytes 4194304 | tf_op jit(solution)/shard_map/video/pallas_call | solution.py:145
  73.4 2.8 %collective-permute-start.5 = (bf16[544,384]{1,0:T(8,128)(2,1)}, bf16[544,384]{1,0:T(8,128)(2,1)S(1)}, u32[]{:S(2)}, u32[]{:S(2)}) collective-permute-start(bf16[544,384]{1,0:T(8,128)(2,1)} %get-tuple-element.50), channel_id=1, source_target_pairs={{0,1},{1,0},{2,3},{3,2},{4,5},{5,4},{6,7},{7,6},{8,9},{9,8},{10,11... | collective-permute-start | bytes 1253384 | tf_op jit(solution)/shard_map/ppermute | solution.py:560
  76.2 1.6 %collective-permute-done.5.refs_3_ = bf16[544,384]{1,0:T(8,128)(2,1)S(1)} collective-permute-done((bf16[544,384]{1,0:T(8,128)(2,1)}, bf16[544,384]{1,0:T(8,128)(2,1)S(1)}, u32[]{:S(2)}, u32[]{:S(2)}) %collective-permute-start.5) | collective-permute-done | bytes 417824 | tf_op jit(solution)/shard_map/ppermute | solution.py:560
  77.8 0.8 copy-done
  78.6 2.5 %video_sum.1 = (bf16[528,384]{1,0:T(8,128)(2,1)}, f32[528,384]{1,0:T(8,128)}) custom-call(bf16[512,384]{1,0:T(8,128)(2,1)} %get-tuple-element.41.refs_0_, bf16[512,384]{1,0:T(8,128)(2,1)} %copy-done.2, bf16[544,384]{1,0:T(8,128)(2,1)} %get-tuple-element.49.refs_2_, bf16[544,384]{1,0:T(8,128)(2,1)} %copy-done), custom_call_target="tpu_custom_call" | custom-call | flops 98304 | bytes 4194304 | tf_op jit(solution)/shard_map/video_sum/pallas_call | solution.py:145
  81.1 2.6 %collective-permute-start.6 = (bf16[528,384]{1,0:T(8,128)(2,1)}, bf16[528,384]{1,0:T(8,128)(2,1)S(1)}, u32[]{:S(2)}, u32[]{:S(2)}) collective-permute-start(bf16[528,384]{1,0:T(8,128)(2,1)} %get-tuple-element.52), channel_id=1, source_target_pairs={{0,2},{1,3},{2,0},{3,1},{4,6},{5,7},{6,4},{7,5},{8,10},{9,11},{10,... | collective-permute-start | bytes 1216520 | tf_op jit(solution)/shard_map/ppermute | solution.py:565
  83.7 3.6 %sound.1 = (bf16[288,384]{1,0:T(8,128)(2,1)}, bf16[288,384]{1,0:T(8,128)(2,1)}) custom-call(s32[1,128]{1,0:T(1,128)} %bitcast.10, bf16[512,384]{1,0:T(8,128)(2,1)} %bitcast.5.refs_1_, bf16[256,384]{1,0:T(8,128)(2,1)} %get-tuple-element.54.refs_2_, bf16[2,1536,384]{2,1,0:T(8,128)(2,1)} %refs_3_.3), custom_call_target="tpu_custom_call" | custom-call | flops 1000000000 | bytes 4194304 | tf_op jit(solution)/shard_map/sound/pallas_call | solution.py:145
  87.2 0.7 collective-permute-start.7
  88.0 1.3 %collective-permute-done.7.refs_1_ = bf16[288,384]{1,0:T(8,128)(2,1)S(1)} collective-permute-done((bf16[288,384]{1,0:T(8,128)(2,1)}, bf16[288,384]{1,0:T(8,128)(2,1)S(1)}, u32[]{:S(2)}, u32[]{:S(2)}) %collective-permute-start.7) | collective-permute-done | bytes 221216 | tf_op jit(solution)/shard_map/ppermute | solution.py:560
  89.3 0.7 copy-done.3
  90.0 1.8 %sound_sum.1 = (bf16[144,384]{1,0:T(8,128)(2,1)}, f32[144,384]{1,0:T(8,128)}) custom-call(bf16[288,384]{1,0:T(8,128)(2,1)} %get-tuple-element.55.refs_0_, bf16[288,384]{1,0:T(8,128)(2,1)} %copy-done.3), custom_call_target="tpu_custom_call" | custom-call | flops 98304 | bytes 4194304 | tf_op jit(solution)/shard_map/sound_sum/pallas_call | solution.py:145
  91.8 0.6 collective-permute-start.8
  92.4 5.5 %collective-permute-done.8.refs_8_ = bf16[144,384]{1,0:T(8,128)(2,1)S(1)} collective-permute-done((bf16[144,384]{1,0:T(8,128)(2,1)}, bf16[144,384]{1,0:T(8,128)(2,1)S(1)}, u32[]{:S(2)}, u32[]{:S(2)}) %collective-permute-start.8) | collective-permute-done | bytes 110624 | tf_op jit(solution)/shard_map/ppermute | solution.py:565
  97.9 0.6 copy-done.4
  98.5 0.2 copy-done.1
  98.7 2.9 %finish.1 = (bf16[256,384]{1,0:T(8,128)(2,1)}, bf16[256,384]{1,0:T(8,128)(2,1)}, bf16[128,384]{1,0:T(8,128)(2,1)}) custom-call(bf16[256,1536]{1,0:T(8,128)(2,1)} %refs_0_.3, bf16[128,1536]{1,0:T(8,128)(2,1)} %refs_1_.5, bf16[256,1536]{1,0:T(8,128)(2,1)} %refs_2_.5, f32[384,128]{1,0:T(8,128)} %get-tuple-element.31.refs_3_, ...), custom_call_target="tpu_custom_call" | custom-call | flops 393216 | bytes 4194304 | tf_op jit(solution)/shard_map/finish/pallas_call | solution.py:145
  (9 shorter events, 0.0 us)
Async XLA Ops:
  6.1 21.2 %collective-permute-start.1 = (bf16[512,384]{1,0:T(8,128)(2,1)}, bf16[512,384]{1,0:T(8,128)(2,1)}, u32[]{:S(2)}, u32[]{:S(2)}) collective-permute-start(bf16[512,384]{1,0:T(8,128)(2,1)} %get-tuple-element.38.refs_6_), channel_id=1, source_target_pairs={{4,8},{8,4},{12,16},{16,12},{20,24},{24,20},{28,32},{32,28},{36,40... | collective-permute-start | bytes 1179656 | tf_op jit(solution)/shard_map/ppermute | solution.py:503
  7.5 23.1 %collective-permute-start = (bf16[512,384]{1,0:T(8,128)(2,1)}, bf16[512,384]{1,0:T(8,128)(2,1)}, u32[]{:S(2)}, u32[]{:S(2)}) collective-permute-start(bf16[512,384]{1,0:T(8,128)(2,1)} %get-tuple-element.38.refs_6_), channel_id=1, source_target_pairs={{0,4},{4,0},{8,12},{12,8},{16,20},{20,16},{24,28},{28,24},{32,36},... | collective-permute-start | bytes 1179656 | tf_op jit(solution)/shard_map/ppermute | solution.py:502
  11.8 28.4 %all-to-all-start = ((bf16[64,8,384]{2,1,0:T(8,128)(2,1)}), bf16[64,8,384]{2,1,0:T(8,128)(2,1)}, u32[]{:S(2)}, u32[]{:S(2)}) async-start(bf16[64,8,384]{2,1,0:T(8,128)(2,1)} %bitcast.7), calls=%async_computation | async-start | bytes 786432 | tf_op jit(solution)/shard_map/all_to_all | solution.py:504
  49.1 18.7 %collective-permute-start.3 = (bf16[512,384]{1,0:T(8,128)(2,1)}, bf16[512,384]{1,0:T(8,128)(2,1)}, u32[]{:S(2)}, u32[]{:S(2)}) collective-permute-start(bf16[512,384]{1,0:T(8,128)(2,1)} %get-tuple-element.45), channel_id=1, source_target_pairs={{0,4},{4,0},{8,12},{12,8},{16,20},{20,16},{24,28},{28,24},{32,36},... | collective-permute-start | bytes 1179656 | tf_op jit(solution)/shard_map/ppermute | solution.py:536
  49.2 18.6 %collective-permute-start.4 = (bf16[512,384]{1,0:T(8,128)(2,1)}, bf16[512,384]{1,0:T(8,128)(2,1)}, u32[]{:S(2)}, u32[]{:S(2)}) collective-permute-start(bf16[512,384]{1,0:T(8,128)(2,1)} %get-tuple-element.46), channel_id=1, source_target_pairs={{4,8},{8,4},{12,16},{16,12},{20,24},{24,20},{28,32},{32,28},{36,40... | collective-permute-start | bytes 1179656 | tf_op jit(solution)/shard_map/ppermute | solution.py:537
  53.6 14.2 %collective-permute-start.2 = (bf16[512,384]{1,0:T(8,128)(2,1)}, bf16[512,384]{1,0:T(8,128)(2,1)S(1)}, u32[]{:S(2)}, u32[]{:S(2)}) collective-permute-start(bf16[512,384]{1,0:T(8,128)(2,1)} %get-tuple-element.42), channel_id=1, source_target_pairs={{0,1},{1,0},{2,3},{3,2},{4,5},{5,4},{6,7},{7,6},{8,9},{9,8},{10,11... | collective-permute-start | bytes 1179656 | tf_op jit(solution)/shard_map/ppermute | solution.py:551
  54.5 29.2 %all-to-all-start.1 = ((bf16[64,8,384]{2,1,0:T(8,128)(2,1)}), bf16[64,8,384]{2,1,0:T(8,128)(2,1)}, u32[]{:S(2)}, u32[]{:S(2)}) async-start(bf16[64,8,384]{2,1,0:T(8,128)(2,1)} %bitcast.6), calls=%async_computation.1 | async-start | bytes 786432 | tf_op jit(solution)/shard_map/all_to_all | solution.py:550
  67.8 0.8 copy-start.2
  73.4 4.4 %collective-permute-start.5 = (bf16[544,384]{1,0:T(8,128)(2,1)}, bf16[544,384]{1,0:T(8,128)(2,1)S(1)}, u32[]{:S(2)}, u32[]{:S(2)}) collective-permute-start(bf16[544,384]{1,0:T(8,128)(2,1)} %get-tuple-element.50), channel_id=1, source_target_pairs={{0,1},{1,0},{2,3},{3,2},{4,5},{5,4},{6,7},{7,6},{8,9},{9,8},{10,11... | collective-permute-start | bytes 1253384 | tf_op jit(solution)/shard_map/ppermute | solution.py:560
  77.8 0.8 copy-start
  81.1 16.8 %collective-permute-start.6 = (bf16[528,384]{1,0:T(8,128)(2,1)}, bf16[528,384]{1,0:T(8,128)(2,1)S(1)}, u32[]{:S(2)}, u32[]{:S(2)}) collective-permute-start(bf16[528,384]{1,0:T(8,128)(2,1)} %get-tuple-element.52), channel_id=1, source_target_pairs={{0,2},{1,3},{2,0},{3,1},{4,6},{5,7},{6,4},{7,5},{8,10},{9,11},{10,... | collective-permute-start | bytes 1216520 | tf_op jit(solution)/shard_map/ppermute | solution.py:565
  87.2 2.1 %collective-permute-start.7 = (bf16[288,384]{1,0:T(8,128)(2,1)}, bf16[288,384]{1,0:T(8,128)(2,1)S(1)}, u32[]{:S(2)}, u32[]{:S(2)}) collective-permute-start(bf16[288,384]{1,0:T(8,128)(2,1)} %get-tuple-element.56), channel_id=1, source_target_pairs={{0,1},{1,0},{2,3},{3,2},{4,5},{5,4},{6,7},{7,6},{8,9},{9,8},{10,11... | collective-permute-start | bytes 663560 | tf_op jit(solution)/shard_map/ppermute | solution.py:560
  89.3 0.7 copy-start.3
  91.8 6.1 %collective-permute-start.8 = (bf16[144,384]{1,0:T(8,128)(2,1)}, bf16[144,384]{1,0:T(8,128)(2,1)S(1)}, u32[]{:S(2)}, u32[]{:S(2)}) collective-permute-start(bf16[144,384]{1,0:T(8,128)(2,1)} %get-tuple-element.58), channel_id=1, source_target_pairs={{0,2},{1,3},{2,0},{3,1},{4,6},{5,7},{6,4},{7,5},{8,10},{9,11},{10,... | collective-permute-start | bytes 331784 | tf_op jit(solution)/shard_map/ppermute | solution.py:565
  97.9 0.6 copy-start.4
  97.9 0.8 copy-start.1

commit v5 on v4

--- a/solution.py
+++ b/solution.py
@@ -177,10 +177,8 @@
 SHIFTS, SCALES, GATING, NEAR, FAR, SOUND = range(6)
 
 
-def front(clips, drops, mod, tokens, weights, audio, targets, audio_weights,
-          kv, hidden, small, u, scale_out, sound_kv, sent):
+def video_front(clips, drops, mod, tokens, weights, kv, hidden, small, u, scale_out):
     rows = tokens.buf.shape[0]
-    sound_rows = audio.buf.shape[0]
     position = lax.axis_index("st")
     count = clips.buf.shape[0]
     clip_ref, dropped_ref = clips.wait(), drops.wait()
@@ -215,10 +213,14 @@
     u.send()
     hidden[...] = both
     hidden.send()
+    scale_out[...] = jnp.broadcast_to(scale, (rows, 128))
+
+
+def sound_front(audio, targets, audio_weights, after, scale_out, sound_kv, sent):
+    sound_rows = audio.buf.shape[0]
     sounds = audio[...].astype(F32)
     sound_scale = row_scale(sounds)
-    scale_out[pl.ds(0, rows), :] = jnp.broadcast_to(scale, (rows, 128))
-    scale_out[pl.ds(rows, sound_rows), :] = jnp.broadcast_to(sound_scale, (sound_rows, 128))
+    scale_out[...] = jnp.broadcast_to(sound_scale, (sound_rows, 128))
     scale_out.send()
     sound_in = (sounds * sound_scale).astype(BF16)
     trow = targets[...]
@@ -419,29 +421,29 @@
         first += tall
 
 
-def finish(tokens, audio, cotangent, scale_in, small, mine, cross, sound_mine, sound_cross,
-           video_out, video_grad, audio_grad):
-    rows, width = video_grad.shape
-    sound_rows = audio_grad.shape[0]
+def mean_of(total, count):
+    row = (total[count : count + 1] + total[count + 1 : count + 2])[:, :count]
+    return to_col(row * (1.0 / (4 * total.shape[1])))
+
+
+def finish_video(tokens, cotangent, scale_in, small, mine, cross, video_out, video_grad):
+    rows = video_grad.shape[0]
     scale = scale_in[...][:, 0:1]
-
-    def mean_of(total, count):
-        row = (total[count : count + 1] + total[count + 1 : count + 2])[:, :count]
-        return to_col(row * (1.0 / (4 * width)))
-
     inputs = tokens[...].astype(F32)
-    normed = inputs * scale[:rows]
     video = mine[...] + cross[...].astype(F32)
     video_out[...] = (inputs + small[GATING : GATING + 1, :] * video[:rows]).astype(BF16)
     video_out.send()
     video = video[rows:]
-    hat = video[:rows] * (1.0 + small[SCALES : SCALES + 1, :]) - normed * mean_of(video, rows)
-    video_grad[...] = (cotangent[...].astype(F32) + scale[:rows] * hat).astype(BF16)
-    video_grad.send()
-    normed = audio[...].astype(F32) * scale[rows:]
-    sound = sound_mine[...] + sound_cross[...].astype(F32)
-    hat = sound[:sound_rows] - normed * mean_of(sound, sound_rows)
-    audio_grad[...] = (scale[rows:] * hat).astype(BF16)
+    hat = video[:rows] * (1.0 + small[SCALES : SCALES + 1, :]) - inputs * scale * mean_of(video, rows)
+    video_grad[...] = (cotangent[...].astype(F32) + scale * hat).astype(BF16)
+
+
+def finish_sound(audio, scale_in, mine, cross, after, audio_grad):
+    rows = audio_grad.shape[0]
+    scale = scale_in[...][:, 0:1]
+    normed = audio[...].astype(F32) * scale
+    sound = mine[...] + cross[...].astype(F32)
+    audio_grad[...] = (scale * (sound[:rows] - normed * mean_of(sound, rows))).astype(BF16)
 
 
 def per_device(
@@ -481,21 +483,27 @@
     def split(arg, pieces):
         return Taken(arg.shape, arg.dtype, [(piece, piece) for piece in pieces])
 
-    kv, hidden, small, u, scale, sound_kv, sent = call(
-        front,
-        (scalars(tile_clip), scalars(dropped), None, None, layers(1, 3), None, None, layers(0, 2)),
-        (tile_clip, dropped, modulation, video_tokens, input_weights, audio_frames, targets, audio_weights),
+    kv, hidden, small, u, scale = call(
+        video_front,
+        (scalars(tile_clip), scalars(dropped), None, None, layers(1, 3)),
+        (tile_clip, dropped, modulation, video_tokens, input_weights),
         [
             ((2 * rows, width), BF16),
             ((rows + 16, model), BF16),
             ((8, model), F32),
             ((2 * rows, width), BF16),
-            ((rows + sound_rows, 128), F32),
-            ((2 * sound_rows, width), BF16),
-            ((slots, width), BF16),
+            ((rows, 128), F32),
         ],
-        2 * (rows + sound_rows) * model * 2 * width,
-        "front",
+        2 * rows * model * 2 * width,
+        "video_front",
+    )
+    sound_scale, sound_kv, sent = call(
+        sound_front,
+        (None, None, layers(0, 2), RAW),
+        (audio_frames, targets, audio_weights, kv),
+        [((sound_rows, 128), F32), ((2 * sound_rows, width), BF16), ((slots, width), BF16)],
+        2 * sound_rows * model * 2 * width,
+        "sound_front",
     )
     near_swap = [(i, i ^ 1) for i in range(count)]
     far_swap = [p for i in range(1, count - 2, 2) for p in ((i, i + 1), (i + 1, i))]
@@ -582,14 +590,23 @@
         10**9,
         "sound",
     )
-    return call(
-        finish,
-        (own_block(rows), own_block(sound_rows), own_block(rows), None, own_block(8, F32)) + (None,) * 4,
-        (video_tokens, audio_frames, cotangent, scale, small, *video, *sound),
-        [((rows, width), BF16), ((rows, width), BF16), ((sound_rows, width), BF16)],
+    video_out, video_grad = call(
+        finish_video,
+        (own_block(rows), own_block(rows), None, own_block(8, F32), None, None),
+        (video_tokens, cotangent, scale, small, *video),
+        [((rows, width), BF16), ((rows, width), BF16)],
         4 * rows * width,
-        "finish",
-    )
+        "finish_video",
+    )
+    (audio_grad,) = call(
+        finish_sound,
+        (own_block(sound_rows), None, None, None, RAW),
+        (audio_frames, sound_scale, *sound, video_grad),
+        [((sound_rows, width), BF16)],
+        2 * sound_rows * width,
+        "finish_sound",
+    )
+    return video_out, video_grad, audio_grad
 
 
 def solution(mesh):

time: 102 us -> 98.1 us (0.962)
  waiting for transfers between devices: 24.8 us -> 12.4 us
  starting transfers between devices: 36.2 us -> 40.2 us
  Pallas kernels: 36.9 us -> 40.4 us
    ppermute x2, waiting for transfers between devices: 5.48 us -> 0.38 us  [head_sum(): return (mine, lax.ppermute(cross, 'head', cross_swap))]
    pallas_call x9 -> x11, Pallas kernels: 36.9 us -> 40.4 us  [call(): pl.pallas_call(kernel, in_specs=[HBM] * len(specs), out_specs=[HBM] * len...]
    ppermute x1, waiting for transfers between devices: 3.48 us -> 0.01 us  [per_device(): back_near = lax.ppermute(d_near, 'st', near_swap)]
    ppermute x1, waiting for transfers between devices: 3.24 us -> 0.01 us  [per_device(): near = lax.ppermute(kv, 'st', near_swap)]
    ppermute x1, starting transfers between devices: 0.88 us -> 3.29 us  [per_device(): out_from_core = lax.ppermute(out_to_core, 'head', core_swap)]
    ppermute x2, starting transfers between devices: 3.15 us -> 4.82 us  [head_sum(): return (mine, lax.ppermute(cross, 'head', cross_swap))]
  transfers between devices with their start and end apart: 11 -> 11, of which waited for: 6 -> 4; matrix products, arithmetic and copies ran while one was open for 0% -> 0% of each run, Pallas kernels for 19% -> 26%
where the time goes in v5:
time: 98.1 us; the launch traced here: 97.6 us
  Pallas kernels  40.4 us (41%)
  starting transfers between devices  40.2 us (41%)
  waiting for transfers between devices  12.4 us (13%)
  local copies, waits for them, and re-layouts  3.58 us (4%)
    pallas_call x11, Pallas kernels, call(): pl.pallas_call(kernel, in_specs=[HBM] * len(specs), out_specs=[HBM] * len...  40.4 us
    all_to_all x1, starting transfers between devices, per_device(): lax.all_to_all(sent, 'st', split_axis=0, concat_axis=0, tiled=True)  11.6 us
    all_to_all x1, starting transfers between devices, per_device(): lax.all_to_all(d_slots, 'st', split_axis=0, concat_axis=0, tiled=True)  10.2 us
    all_to_all x1, waiting for transfers between devices, per_device(): lax.all_to_all(sent, 'st', split_axis=0, concat_axis=0, tiled=True)  9.11 us
    ppermute x2, starting transfers between devices, head_sum(): return (mine, lax.ppermute(cross, 'head', cross_swap))  4.82 us
    ppermute x1, starting transfers between devices, per_device(): near = lax.ppermute(kv, 'st', near_swap)  4.24 us
    unnamed x10, local copies, waits for them, and re-layouts  3.58 us
    ppermute x1, starting transfers between devices, per_device(): out_from_core = lax.ppermute(out_to_core, 'head', core_swap)  3.29 us
  transfers between devices with their start and end apart: 11, of which 4 were waited for; matrix products, arithmetic and copies ran while one was open for 0% of the time, Pallas kernels for 26%

profile of v5, /device:TPU:1, one launch (start us, length us, event | category | flops | bytes accessed | tf_op | source)
XLA Modules:
  0.0 97.6 jit_solution(1062970780619420976)
XLA Ops:
  0.6 4.1 %video_front.1 = (bf16[512,384]{1,0:T(8,128)(2,1)}, bf16[272,1536]{1,0:T(8,128)(2,1)}, f32[8,1536]{1,0:T(8,128)}, bf16[512,384]{1,0:T(8,128)(2,1)}, f32[256,128]{1,0:T(8,128)}) custom-call(s32[64]{0:T(128)} %refs_0_.4, s32[4]{0:T(128)} %refs_1_.3, f32[3,4,1536]{2,1,0:T(4,128)} %bitcast.8, bf16[256,1536]{1,0:T(8,128)(2,1)} %refs_0_.6, ...), custom_call_target="tpu_custom_call" | custom-call | flops 603979776 | bytes 4194304 | tf_op jit(solution)/shard_map/video_front/pallas_call | solution.py:145
  4.8 1.4 %collective-permute-start.1 = (bf16[512,384]{1,0:T(8,128)(2,1)}, bf16[512,384]{1,0:T(8,128)(2,1)}, u32[]{:S(2)}, u32[]{:S(2)}) collective-permute-start(bf16[512,384]{1,0:T(8,128)(2,1)} %get-tuple-element.36.refs_3_.refs_6_), channel_id=1, source_target_pairs={{4,8},{8,4},{12,16},{16,12},{20,24},{24,20},{28,32},{32,28},{36,40... | collective-permute-start | bytes 1179656 | tf_op jit(solution)/shard_map/ppermute | solution.py:511
  6.2 4.2 %collective-permute-start = (bf16[512,384]{1,0:T(8,128)(2,1)}, bf16[512,384]{1,0:T(8,128)(2,1)}, u32[]{:S(2)}, u32[]{:S(2)}) collective-permute-start(bf16[512,384]{1,0:T(8,128)(2,1)} %get-tuple-element.36.refs_3_.refs_6_), channel_id=1, source_target_pairs={{0,4},{4,0},{8,12},{12,8},{16,20},{20,16},{24,28},{28,24},{32,36},... | collective-permute-start | bytes 1179656 | tf_op jit(solution)/shard_map/ppermute | solution.py:510
  10.4 3.3 %sound_front.1 = (f32[128,128]{1,0:T(8,128)}, bf16[256,384]{1,0:T(8,128)(2,1)}, bf16[512,384]{1,0:T(8,128)(2,1)}) custom-call(bf16[128,1536]{1,0:T(8,128)(2,1)} %refs_0_.7, s32[1,128]{1,0:T(1,128)} %bitcast.9, bf16[2,1536,384]{2,1,0:T(8,128)(2,1)} %refs_3_.3, bf16[512,384]{1,0:T(8,128)(2,1)} %get-tuple-element.36.refs_3_.refs_6_), custom_call_target="tpu_custom_call" | custom-call | flops 301989888 | bytes 4194304 | tf_op jit(solution)/shard_map/sound_front/pallas_call | solution.py:145
  13.7 11.6 %all-to-all-start = ((bf16[64,8,384]{2,1,0:T(8,128)(2,1)}), bf16[64,8,384]{2,1,0:T(8,128)(2,1)}, u32[]{:S(2)}, u32[]{:S(2)}) async-start(bf16[64,8,384]{2,1,0:T(8,128)(2,1)} %bitcast.7), calls=%async_computation | async-start | bytes 786432 | tf_op jit(solution)/shard_map/all_to_all | solution.py:512
  25.4 3.9 %query_front.1 = (bf16[256,384]{1,0:T(8,128)(2,1)}, bf16[256,384]{1,0:T(8,128)(2,1)}, bf16[256,384]{1,0:T(8,128)(2,1)}, bf16[384,256]{1,0:T(8,128)(2,1)}) custom-call(bf16[272,1536]{1,0:T(8,128)(2,1)} %get-tuple-element.38.refs_0_, bf16[3,1536,384]{2,1,0:T(8,128)(2,1)} %refs_6_.1, bf16[256,1536]{1,0:T(8,128)(2,1)} %refs_1_.5, ...), custom_call_target="tpu_custom_call" | custom-call | flops 9999999827968 | bytes 4194304 | tf_op jit(solution)/shard_map/query_front/pallas_call | solution.py:145
  29.3 0.0 collective-permute-done.refs_5_
  29.3 9.1 %all-to-all-done = bf16[64,8,384]{2,1,0:T(8,128)(2,1)} async-done(((bf16[64,8,384]{2,1,0:T(8,128)(2,1)}), bf16[64,8,384]{2,1,0:T(8,128)(2,1)}, u32[]{:S(2)}, u32[]{:S(2)}) %all-to-all-start) | async-done | bytes 393248 | tf_op jit(solution)/shard_map/all_to_all | solution.py:512
  38.4 8.8 %attention.1 = (bf16[384,256]{1,0:T(8,128)(2,1)}, bf16[384,256]{1,0:T(8,128)(2,1)}, bf16[512,384]{1,0:T(8,128)(2,1)}, bf16[512,384]{1,0:T(8,128)(2,1)}, bf16[512...) custom-call(f32[8,1536]{1,0:T(8,128)} %get-tuple-element.35.refs_3_.refs_0_, bf16[512,384]{1,0:T(8,128)(2,1)} %bitcast.3.refs_1_, ...), custom_call_target="tpu_custom_call" | custom-call | flops 1207959552 | bytes 4194304 | tf_op jit(solution)/shard_map/attention/pallas_call | solution.py:145
  47.2 0.1 collective-permute-start.3
  47.3 1.4 %collective-permute-start.4 = (bf16[512,384]{1,0:T(8,128)(2,1)}, bf16[512,384]{1,0:T(8,128)(2,1)}, u32[]{:S(2)}, u32[]{:S(2)}) collective-permute-start(bf16[512,384]{1,0:T(8,128)(2,1)} %get-tuple-element.49), channel_id=1, source_target_pairs={{4,8},{8,4},{12,16},{16,12},{20,24},{24,20},{28,32},{32,28},{36,40... | collective-permute-start | bytes 1179656 | tf_op jit(solution)/shard_map/ppermute | solution.py:545
  48.8 3.0 %out_first.1 = (bf16[512,384]{1,0:T(8,128)(2,1)}, bf16[512,384]{1,0:T(8,128)(2,1)}, bf16[512,384]{1,0:T(8,128)(2,1)}) custom-call(bf16[512,384]{1,0:T(8,128)(2,1)} %get-tuple-element.42.refs_0_, bf16[384,256]{1,0:T(8,128)(2,1)} %get-tuple-element.43.refs_1_, bf16[384,1536]{1,0:T(8,128)(2,1)} %refs_2_.5), custom_call_target="tpu_custom_call" | custom-call | flops 9999999827968 | bytes 4194304 | tf_op jit(solution)/shard_map/out_first/pallas_call | solution.py:145
  51.8 3.3 %collective-permute-start.2 = (bf16[512,384]{1,0:T(8,128)(2,1)}, bf16[512,384]{1,0:T(8,128)(2,1)S(1)}, u32[]{:S(2)}, u32[]{:S(2)}) collective-permute-start(bf16[512,384]{1,0:T(8,128)(2,1)} %get-tuple-element.45), channel_id=1, source_target_pairs={{0,1},{1,0},{2,3},{3,2},{4,5},{5,4},{6,7},{7,6},{8,9},{9,8},{10,11... | collective-permute-start | bytes 1179656 | tf_op jit(solution)/shard_map/ppermute | solution.py:559
  55.1 10.2 %all-to-all-start.1 = ((bf16[64,8,384]{2,1,0:T(8,128)(2,1)}), bf16[64,8,384]{2,1,0:T(8,128)(2,1)}, u32[]{:S(2)}, u32[]{:S(2)}) async-start(bf16[64,8,384]{2,1,0:T(8,128)(2,1)} %bitcast.6), calls=%async_computation.1 | async-start | bytes 786432 | tf_op jit(solution)/shard_map/all_to_all | solution.py:558
  65.3 0.7 copy-done.2
  66.1 4.8 %video.1 = (bf16[544,384]{1,0:T(8,128)(2,1)}, bf16[544,384]{1,0:T(8,128)(2,1)}) custom-call(bf16[384,256]{1,0:T(8,128)(2,1)} %get-tuple-element.46.refs_0_, bf16[512,384]{1,0:T(8,128)(2,1)} %get-tuple-element.47.refs_1_, bf16[512,384]{1,0:T(8,128)(2,1)} %collective-permute-done.3.refs_2_, bf16[512,384]{1,0:T(8,128)(2,1)} %collective-permute-done.4.refs_3_, ...), custom_call_target="tpu_custom_call" | custom-call | flops 9999999827968 | bytes 4194304 | tf_op jit(solution)/shard_map/video/pallas_call | solution.py:145
  70.9 2.4 %collective-permute-start.5 = (bf16[544,384]{1,0:T(8,128)(2,1)}, bf16[544,384]{1,0:T(8,128)(2,1)S(1)}, u32[]{:S(2)}, u32[]{:S(2)}) collective-permute-start(bf16[544,384]{1,0:T(8,128)(2,1)} %get-tuple-element.53), channel_id=1, source_target_pairs={{0,1},{1,0},{2,3},{3,2},{4,5},{5,4},{6,7},{7,6},{8,9},{9,8},{10,11... | collective-permute-start | bytes 1253384 | tf_op jit(solution)/shard_map/ppermute | solution.py:568
  73.3 1.6 %collective-permute-done.5.refs_3_ = bf16[544,384]{1,0:T(8,128)(2,1)S(1)} collective-permute-done((bf16[544,384]{1,0:T(8,128)(2,1)}, bf16[544,384]{1,0:T(8,128)(2,1)S(1)}, u32[]{:S(2)}, u32[]{:S(2)}) %collective-permute-start.5) | collective-permute-done | bytes 417824 | tf_op jit(solution)/shard_map/ppermute | solution.py:568
  74.9 0.8 copy-done
  75.6 2.5 %video_sum.1 = (bf16[528,384]{1,0:T(8,128)(2,1)}, f32[528,384]{1,0:T(8,128)}) custom-call(bf16[512,384]{1,0:T(8,128)(2,1)} %get-tuple-element.44.refs_0_, bf16[512,384]{1,0:T(8,128)(2,1)} %copy-done.2, bf16[544,384]{1,0:T(8,128)(2,1)} %get-tuple-element.52.refs_2_, bf16[544,384]{1,0:T(8,128)(2,1)} %copy-done), custom_call_target="tpu_custom_call" | custom-call | flops 98304 | bytes 4194304 | tf_op jit(solution)/shard_map/video_sum/pallas_call | solution.py:145
  78.1 2.6 %collective-permute-start.6 = (bf16[528,384]{1,0:T(8,128)(2,1)}, bf16[528,384]{1,0:T(8,128)(2,1)S(1)}, u32[]{:S(2)}, u32[]{:S(2)}) collective-permute-start(bf16[528,384]{1,0:T(8,128)(2,1)} %get-tuple-element.55), channel_id=1, source_target_pairs={{0,2},{1,3},{2,0},{3,1},{4,6},{5,7},{6,4},{7,5},{8,10},{9,11},{10,... | collective-permute-start | bytes 1216520 | tf_op jit(solution)/shard_map/ppermute | solution.py:573
  80.7 3.6 %sound.1 = (bf16[288,384]{1,0:T(8,128)(2,1)}, bf16[288,384]{1,0:T(8,128)(2,1)}) custom-call(s32[1,128]{1,0:T(1,128)} %bitcast.10, bf16[512,384]{1,0:T(8,128)(2,1)} %bitcast.5.refs_1_, bf16[256,384]{1,0:T(8,128)(2,1)} %get-tuple-element.60.refs_2_, bf16[2,1536,384]{2,1,0:T(8,128)(2,1)} %refs_3_.3), custom_call_target="tpu_custom_call" | custom-call | flops 1000000000 | bytes 4194304 | tf_op jit(solution)/shard_map/sound/pallas_call | solution.py:145
  84.3 0.7 collective-permute-start.7
  85.0 1.3 %collective-permute-done.7.refs_1_ = bf16[288,384]{1,0:T(8,128)(2,1)S(1)} collective-permute-done((bf16[288,384]{1,0:T(8,128)(2,1)}, bf16[288,384]{1,0:T(8,128)(2,1)S(1)}, u32[]{:S(2)}, u32[]{:S(2)}) %collective-permute-start.7) | collective-permute-done | bytes 221216 | tf_op jit(solution)/shard_map/ppermute | solution.py:568
  86.3 0.7 copy-done.3
  87.0 1.8 %sound_sum.1 = (bf16[144,384]{1,0:T(8,128)(2,1)}, f32[144,384]{1,0:T(8,128)}) custom-call(bf16[288,384]{1,0:T(8,128)(2,1)} %get-tuple-element.61.refs_0_, bf16[288,384]{1,0:T(8,128)(2,1)} %copy-done.3), custom_call_target="tpu_custom_call" | custom-call | flops 98304 | bytes 4194304 | tf_op jit(solution)/shard_map/sound_sum/pallas_call | solution.py:145
  88.9 2.3 %collective-permute-start.8 = (bf16[144,384]{1,0:T(8,128)(2,1)}, bf16[144,384]{1,0:T(8,128)(2,1)S(1)}, u32[]{:S(2)}, u32[]{:S(2)}) collective-permute-start(bf16[144,384]{1,0:T(8,128)(2,1)} %get-tuple-element.64), channel_id=1, source_target_pairs={{0,2},{1,3},{2,0},{3,1},{4,6},{5,7},{6,4},{7,5},{8,10},{9,11},{10,... | collective-permute-start | bytes 331784 | tf_op jit(solution)/shard_map/ppermute | solution.py:573
  91.1 0.8 copy-done.1
  91.9 2.7 %finish_video.1 = (bf16[256,384]{1,0:T(8,128)(2,1)}, bf16[256,384]{1,0:T(8,128)(2,1)}) custom-call(bf16[256,1536]{1,0:T(8,128)(2,1)} %refs_0_.6, bf16[256,1536]{1,0:T(8,128)(2,1)} %refs_1_.5, f32[256,128]{1,0:T(8,128)} %get-tuple-element.34.refs_2_, f32[8,1536]{1,0:T(8,128)} %get-tuple-element.35.refs_3_.refs_0_, f32[528,384]{1,0:T(8,128)} %get-tuple-element.54.refs_4_, ...), custom_call_target="tpu_custom_call" | custom-call | flops 393216 | bytes 4194304 | tf_op jit(solution)/shard_map/finish_video/pallas_call | solution.py:145
  94.6 0.4 collective-permute-done.8.refs_3_
  94.9 0.6 copy-done.4
  95.6 1.9 %finish_sound.1 = bf16[128,384]{1,0:T(8,128)(2,1)} custom-call(bf16[128,1536]{1,0:T(8,128)(2,1)} %refs_0_.7, f32[128,128]{1,0:T(8,128)} %get-tuple-element.58.refs_1_, f32[144,384]{1,0:T(8,128)} %get-tuple-element.63.refs_2_, bf16[144,384]{1,0:T(8,128)(2,1)} %copy-done.4, bf16[256,384]{1,0:T(8,128)(2,1)} %get-tuple-element.32.refs_4_), custom_call_target="tpu_custom_call" | custom-call | flops 98304 | bytes 4194304 | tf_op jit(solution)/shard_map/finish_sound/pallas_call | solution.py:145
  (11 shorter events, 0.0 us)
Async XLA Ops:
  4.8 24.5 %collective-permute-start.1 = (bf16[512,384]{1,0:T(8,128)(2,1)}, bf16[512,384]{1,0:T(8,128)(2,1)}, u32[]{:S(2)}, u32[]{:S(2)}) collective-permute-start(bf16[512,384]{1,0:T(8,128)(2,1)} %get-tuple-element.36.refs_3_.refs_6_), channel_id=1, source_target_pairs={{4,8},{8,4},{12,16},{16,12},{20,24},{24,20},{28,32},{32,28},{36,40... | collective-permute-start | bytes 1179656 | tf_op jit(solution)/shard_map/ppermute | solution.py:511
  6.2 23.1 %collective-permute-start = (bf16[512,384]{1,0:T(8,128)(2,1)}, bf16[512,384]{1,0:T(8,128)(2,1)}, u32[]{:S(2)}, u32[]{:S(2)}) collective-permute-start(bf16[512,384]{1,0:T(8,128)(2,1)} %get-tuple-element.36.refs_3_.refs_6_), channel_id=1, source_target_pairs={{0,4},{4,0},{8,12},{12,8},{16,20},{20,16},{24,28},{28,24},{32,36},... | collective-permute-start | bytes 1179656 | tf_op jit(solution)/shard_map/ppermute | solution.py:510
  13.7 24.7 %all-to-all-start = ((bf16[64,8,384]{2,1,0:T(8,128)(2,1)}), bf16[64,8,384]{2,1,0:T(8,128)(2,1)}, u32[]{:S(2)}, u32[]{:S(2)}) async-start(bf16[64,8,384]{2,1,0:T(8,128)(2,1)} %bitcast.7), calls=%async_computation | async-start | bytes 786432 | tf_op jit(solution)/shard_map/all_to_all | solution.py:512
  47.2 18.1 %collective-permute-start.3 = (bf16[512,384]{1,0:T(8,128)(2,1)}, bf16[512,384]{1,0:T(8,128)(2,1)}, u32[]{:S(2)}, u32[]{:S(2)}) collective-permute-start(bf16[512,384]{1,0:T(8,128)(2,1)} %get-tuple-element.48), channel_id=1, source_target_pairs={{0,4},{4,0},{8,12},{12,8},{16,20},{20,16},{24,28},{28,24},{32,36},... | collective-permute-start | bytes 1179656 | tf_op jit(solution)/shard_map/ppermute | solution.py:544
  47.3 18.0 %collective-permute-start.4 = (bf16[512,384]{1,0:T(8,128)(2,1)}, bf16[512,384]{1,0:T(8,128)(2,1)}, u32[]{:S(2)}, u32[]{:S(2)}) collective-permute-start(bf16[512,384]{1,0:T(8,128)(2,1)} %get-tuple-element.49), channel_id=1, source_target_pairs={{4,8},{8,4},{12,16},{16,12},{20,24},{24,20},{28,32},{32,28},{36,40... | collective-permute-start | bytes 1179656 | tf_op jit(solution)/shard_map/ppermute | solution.py:545
  51.8 13.5 %collective-permute-start.2 = (bf16[512,384]{1,0:T(8,128)(2,1)}, bf16[512,384]{1,0:T(8,128)(2,1)S(1)}, u32[]{:S(2)}, u32[]{:S(2)}) collective-permute-start(bf16[512,384]{1,0:T(8,128)(2,1)} %get-tuple-element.45), channel_id=1, source_target_pairs={{0,1},{1,0},{2,3},{3,2},{4,5},{5,4},{6,7},{7,6},{8,9},{9,8},{10,11... | collective-permute-start | bytes 1179656 | tf_op jit(solution)/shard_map/ppermute | solution.py:559
  55.1 25.6 %all-to-all-start.1 = ((bf16[64,8,384]{2,1,0:T(8,128)(2,1)}), bf16[64,8,384]{2,1,0:T(8,128)(2,1)}, u32[]{:S(2)}, u32[]{:S(2)}) async-start(bf16[64,8,384]{2,1,0:T(8,128)(2,1)} %bitcast.6), calls=%async_computation.1 | async-start | bytes 786432 | tf_op jit(solution)/shard_map/all_to_all | solution.py:558
  65.3 0.8 copy-start.2
  70.9 4.0 %collective-permute-start.5 = (bf16[544,384]{1,0:T(8,128)(2,1)}, bf16[544,384]{1,0:T(8,128)(2,1)S(1)}, u32[]{:S(2)}, u32[]{:S(2)}) collective-permute-start(bf16[544,384]{1,0:T(8,128)(2,1)} %get-tuple-element.53), channel_id=1, source_target_pairs={{0,1},{1,0},{2,3},{3,2},{4,5},{5,4},{6,7},{7,6},{8,9},{9,8},{10,11... | collective-permute-start | bytes 1253384 | tf_op jit(solution)/shard_map/ppermute | solution.py:568
  74.9 0.8 copy-start
  78.1 13.0 %collective-permute-start.6 = (bf16[528,384]{1,0:T(8,128)(2,1)}, bf16[528,384]{1,0:T(8,128)(2,1)S(1)}, u32[]{:S(2)}, u32[]{:S(2)}) collective-permute-start(bf16[528,384]{1,0:T(8,128)(2,1)} %get-tuple-element.55), channel_id=1, source_target_pairs={{0,2},{1,3},{2,0},{3,1},{4,6},{5,7},{6,4},{7,5},{8,10},{9,11},{10,... | collective-permute-start | bytes 1216520 | tf_op jit(solution)/shard_map/ppermute | solution.py:573
  84.3 2.0 %collective-permute-start.7 = (bf16[288,384]{1,0:T(8,128)(2,1)}, bf16[288,384]{1,0:T(8,128)(2,1)S(1)}, u32[]{:S(2)}, u32[]{:S(2)}) collective-permute-start(bf16[288,384]{1,0:T(8,128)(2,1)} %get-tuple-element.62), channel_id=1, source_target_pairs={{0,1},{1,0},{2,3},{3,2},{4,5},{5,4},{6,7},{7,6},{8,9},{9,8},{10,11... | collective-permute-start | bytes 663560 | tf_op jit(solution)/shard_map/ppermute | solution.py:568
  86.3 0.7 copy-start.3
  88.9 6.1 %collective-permute-start.8 = (bf16[144,384]{1,0:T(8,128)(2,1)}, bf16[144,384]{1,0:T(8,128)(2,1)S(1)}, u32[]{:S(2)}, u32[]{:S(2)}) collective-permute-start(bf16[144,384]{1,0:T(8,128)(2,1)} %get-tuple-element.64), channel_id=1, source_target_pairs={{0,2},{1,3},{2,0},{3,1},{4,6},{5,7},{6,4},{7,5},{8,10},{9,11},{10,... | collective-permute-start | bytes 331784 | tf_op jit(solution)/shard_map/ppermute | solution.py:573
  91.1 0.8 copy-start.1
  94.9 0.6 copy-start.4
